TPU v7x, 32 devices: a whole 2x2x4 slice. The times are simulated.
32 devices in a mesh: grp: 2 (over x), wave: 16 (over z, y, core).
Axes of the slice: x: 2, y: 2, z: 4, core: 2. Of those that a mesh axis runs over, the one named last changes fastest.
Arguments:
- wave_pairs: int32 [640], P('wave'), may hold values from 0 to 639, each once
- band_owner: int32 [32], P('wave'), may hold values from 0 to 31, each once
- spectra_even: bfloat16 [640, 641, 256], P('wave', None, 'grp'), parts along dimension 2, may hold values from -0.15625 to 0.15625
- spectra_odd: bfloat16 [640, 640, 256], P('wave', None, 'grp'), parts along dimension 2, may hold values from -0.15625 to 0.15625
- legendre_even: bfloat16 [640, 32, 641], P('wave'), may hold values from -0.25 to 0.25
- legendre_odd: bfloat16 [640, 32, 640], P('wave'), may hold values from -0.25 to 0.25
Outputs:
- grid_values: bfloat16 [32, 2, 128, 2688], P('wave', None, 'grp'), parts along dimension 2
There are 2 independent parts, one for each index of `grp`. A program takes and returns all parts, laid end to end along the dimension named above; an argument that names none is the same for every part. Nothing has to cross between parts.
Inputs may be any that keep to these rules, and one draw needn't show every extreme that they name: `wave_pairs`: each lower wavenumber 0 to 639 stands in exactly one slot. `band_owner`: each latitude pair stands in exactly one slot.
All inputs are finite; a program needn't handle non-finite values.
Results may differ from a plain program's by a relative error of at most 0.0055.
Values may be sent and summed in bfloat16 or wider, within the bound.
No kernel may reach another device: no remote copies, remote signals or barrier semaphores. Data moves between devices by JAX's collectives and lax.ppermute only.
A program may use at most 64 MiB of HBM per device.

v0:
```python
import math

import jax
import jax.numpy as jnp
from jax import lax
from jax.sharding import PartitionSpec as P

M = 1280
NLON = 2688


def parity_half(panel, spectra, limit_count):
    column_ids = jnp.arange(spectra.shape[0], dtype=jnp.int32)[:, None]
    in_lower = column_ids < limit_count
    zeroed = jnp.zeros_like(spectra)
    masked = jnp.concatenate(
        [jnp.where(in_lower, spectra, zeroed), jnp.where(in_lower, zeroed, spectra)], axis=1
    )
    return jnp.dot(panel, masked, preferred_element_type=jnp.float32)


def legendre_pair(operands):
    low_wave, panel_even, panel_odd, spectra_even, spectra_odd = operands
    symmetric = parity_half(panel_even, spectra_even, (M - low_wave + 1) // 2)
    antisym = parity_half(panel_odd, spectra_odd, (M - low_wave) // 2)
    north_rows = (symmetric + antisym).astype(jnp.bfloat16)
    south_rows = (symmetric - antisym).astype(jnp.bfloat16)
    return jnp.stack([north_rows, south_rows], axis=1)


def wave_tables(low_wave):
    wavenumbers = jnp.stack([low_wave, M - 1 - low_wave], axis=-1)
    longitude = jnp.arange(NLON, dtype=jnp.int32)
    residue = wavenumbers[..., None] * longitude % NLON
    angles = residue.astype(jnp.float32) * (2.0 * math.pi / NLON)
    factor = jnp.where(wavenumbers == 0, 1.0, 2.0).astype(jnp.float32)[..., None]
    cosine = (factor * jnp.cos(angles)).astype(jnp.bfloat16)
    sine = (-factor * jnp.sin(angles)).astype(jnp.bfloat16)
    return jnp.stack([cosine, sine], axis=-2)


def fourier_sum(arrived, wave_table):
    fields = arrived.shape[-1] // 4
    shaped = arrived.reshape(arrived.shape[:4] + (2, 2, fields))
    return jnp.einsum("psahwrf,pswrn->ahfn", shaped, wave_table, preferred_element_type=jnp.float32)


def on_device(wave_pairs, band_owner, spectra_even, spectra_odd, legendre_even, legendre_odd):
    devices = lax.axis_size("wave")
    pairs_dev = wave_pairs.shape[0]
    lat_dev = band_owner.shape[0]
    fields = spectra_even.shape[2] // 2
    all_bands, all_pairs = (
        lax.all_gather(band_owner, "wave", axis=0, tiled=True),
        lax.all_gather(wave_pairs, "wave", axis=0, tiled=True),
    )
    pair_grid = all_pairs.reshape(devices, pairs_dev)

    def pair_step(pair_slot, running):
        operands = (
            lax.dynamic_index_in_dim(wave_pairs, pair_slot, 0, keepdims=False),
            lax.dynamic_index_in_dim(legendre_even, pair_slot, 0, keepdims=False),
            lax.dynamic_index_in_dim(legendre_odd, pair_slot, 0, keepdims=False),
            lax.dynamic_index_in_dim(spectra_even, pair_slot, 0, keepdims=False),
            lax.dynamic_index_in_dim(spectra_odd, pair_slot, 0, keepdims=False),
        )
        fourier_rows = jnp.take(legendre_pair(operands), all_bands, axis=0)
        fourier_rows = fourier_rows.reshape(devices, lat_dev, 2, 4 * fields)
        received = lax.all_to_all(fourier_rows, "wave", split_axis=0, concat_axis=0, tiled=True)
        source_waves = lax.dynamic_index_in_dim(pair_grid, pair_slot, 1, keepdims=False)
        wave_table = wave_tables(source_waves)
        return running + fourier_sum(received[None], wave_table[None])

    initial = jnp.zeros((lat_dev, 2, fields, NLON), jnp.float32)
    summed = lax.fori_loop(0, pairs_dev, pair_step, initial)
    return summed.astype(jnp.bfloat16)


def solution(mesh):
    return jax.shard_map(
        on_device,
        mesh=mesh,
        in_specs=(
            P("wave"),
            P("wave"),
            P("wave", None, "grp"),
            P("wave", None, "grp"),
            P("wave", None, None),
            P("wave", None, None),
        ),
        out_specs=P("wave", None, "grp", None),
        check_vma=False,
    )
```

profile of v0, /device:TPU:13, one launch (start us, length us, event | category | flops | bytes accessed | tf_op | source)
XLA Modules:
  0.0 792.7 jit_solution(12239611226685797487)
XLA Ops:
  4.2 8.0 %all-reduce.2 = (s32[32]{0:T(128)S(1)}, s32[640]{0:T(1024)S(1)}) all-reduce(s32[32]{0:T(128)S(1)} %dynamic-update-slice, s32[640]{0:T(1024)S(1)} %dynamic-update-slice.1), channel_id=1, replica_groups=mesh['grp'=2,'wave'=16] {'wave'}, use_global_device_ids=true, to_apply=%add | all-reduce | flops 672 | bytes 5376
  12.4 6.5 copy.40
  18.9 772.6 %while.17 = (s32[]{:T(128)}, f32[2,2,64,2688]{3,2,1,0:T(8,128)S(1)}, s32[32]{0:T(128)S(1)}, bf16[40,32,641]{2,1,0:T(8,128)(2,1)}, s32[40]{0:T(128)S(1)}, /*index...) while((s32[]{:T(128)}, ...), condition=%wide.region_1.2_spmd.clone, body=%wide.region_0.1_spmd.clone.sunk | while | flops 113442800 | bytes 8490709 | solution.py:75
  26.6 8.5 %all-to-all-start = ((bf16[16,2,2,256]{3,2,1,0:T(2,128)(2,1)}), bf16[16,2,2,256]{3,2,1,0:T(2,128)(2,1)S(1)}, u32[]{:S(2)}, u32[]{:S(2)}) async-start(bf16[16,2,2,256]{3,2,1,0:T(2,128)(2,1)} %broadcast_select_fusion.2), calls=%async_computation | async-start | bytes 65536 | tf_op jit(solution)/shard_map/while/body/eval_jaxpr/all_to_all | solution.py:69
  48.5 5.9 all-to-all-start
  67.7 5.9 all-to-all-start
  87.0 5.9 all-to-all-start
  106.2 5.9 all-to-all-start
  125.5 5.9 all-to-all-start
  144.7 5.9 all-to-all-start
  164.0 5.9 all-to-all-start
  183.2 5.9 all-to-all-start
  202.5 5.9 all-to-all-start
  221.7 5.9 all-to-all-start
  241.0 5.9 all-to-all-start
  260.2 5.9 all-to-all-start
  279.5 5.9 all-to-all-start
  298.7 5.9 all-to-all-start
  318.0 5.9 all-to-all-start
  337.2 5.9 all-to-all-start
  356.5 5.9 all-to-all-start
  375.7 5.9 all-to-all-start
  395.0 5.9 all-to-all-start
  414.2 5.9 all-to-all-start
  (990 shorter events, 592.0 us)
Async XLA Ops:
  26.6 12.7 %all-to-all-start = ((bf16[16,2,2,256]{3,2,1,0:T(2,128)(2,1)}), bf16[16,2,2,256]{3,2,1,0:T(2,128)(2,1)S(1)}, u32[]{:S(2)}, u32[]{:S(2)}) async-start(bf16[16,2,2,256]{3,2,1,0:T(2,128)(2,1)} %broadcast_select_fusion.2), calls=%async_computation | async-start | bytes 65536 | tf_op jit(solution)/shard_map/while/body/eval_jaxpr/all_to_all | solution.py:69
  48.5 10.1 %all-to-all-start = ((bf16[16,2,2,256]{3,2,1,0:T(2,128)(2,1)}), bf16[16,2,2,256]{3,2,1,0:T(2,128)(2,1)S(1)}, u32[]{:S(2)}, u32[]{:S(2)}) async-start(bf16[16,2,2,256]{3,2,1,0:T(2,128)(2,1)} %broadcast_select_fusion.2), calls=%async_computation | async-start | bytes 65536 | tf_op jit(solution)/shard_map/while/body/eval_jaxpr/all_to_all | solution.py:69
  67.7 10.1 %all-to-all-start = ((bf16[16,2,2,256]{3,2,1,0:T(2,128)(2,1)}), bf16[16,2,2,256]{3,2,1,0:T(2,128)(2,1)S(1)}, u32[]{:S(2)}, u32[]{:S(2)}) async-start(bf16[16,2,2,256]{3,2,1,0:T(2,128)(2,1)} %broadcast_select_fusion.2), calls=%async_computation | async-start | bytes 65536 | tf_op jit(solution)/shard_map/while/body/eval_jaxpr/all_to_all | solution.py:69
  87.0 10.1 %all-to-all-start = ((bf16[16,2,2,256]{3,2,1,0:T(2,128)(2,1)}), bf16[16,2,2,256]{3,2,1,0:T(2,128)(2,1)S(1)}, u32[]{:S(2)}, u32[]{:S(2)}) async-start(bf16[16,2,2,256]{3,2,1,0:T(2,128)(2,1)} %broadcast_select_fusion.2), calls=%async_computation | async-start | bytes 65536 | tf_op jit(solution)/shard_map/while/body/eval_jaxpr/all_to_all | solution.py:69
  106.2 10.1 %all-to-all-start = ((bf16[16,2,2,256]{3,2,1,0:T(2,128)(2,1)}), bf16[16,2,2,256]{3,2,1,0:T(2,128)(2,1)S(1)}, u32[]{:S(2)}, u32[]{:S(2)}) async-start(bf16[16,2,2,256]{3,2,1,0:T(2,128)(2,1)} %broadcast_select_fusion.2), calls=%async_computation | async-start | bytes 65536 | tf_op jit(solution)/shard_map/while/body/eval_jaxpr/all_to_all | solution.py:69
  125.5 10.1 %all-to-all-start = ((bf16[16,2,2,256]{3,2,1,0:T(2,128)(2,1)}), bf16[16,2,2,256]{3,2,1,0:T(2,128)(2,1)S(1)}, u32[]{:S(2)}, u32[]{:S(2)}) async-start(bf16[16,2,2,256]{3,2,1,0:T(2,128)(2,1)} %broadcast_select_fusion.2), calls=%async_computation | async-start | bytes 65536 | tf_op jit(solution)/shard_map/while/body/eval_jaxpr/all_to_all | solution.py:69
  144.7 10.1 %all-to-all-start = ((bf16[16,2,2,256]{3,2,1,0:T(2,128)(2,1)}), bf16[16,2,2,256]{3,2,1,0:T(2,128)(2,1)S(1)}, u32[]{:S(2)}, u32[]{:S(2)}) async-start(bf16[16,2,2,256]{3,2,1,0:T(2,128)(2,1)} %broadcast_select_fusion.2), calls=%async_computation | async-start | bytes 65536 | tf_op jit(solution)/shard_map/while/body/eval_jaxpr/all_to_all | solution.py:69
  164.0 10.1 %all-to-all-start = ((bf16[16,2,2,256]{3,2,1,0:T(2,128)(2,1)}), bf16[16,2,2,256]{3,2,1,0:T(2,128)(2,1)S(1)}, u32[]{:S(2)}, u32[]{:S(2)}) async-start(bf16[16,2,2,256]{3,2,1,0:T(2,128)(2,1)} %broadcast_select_fusion.2), calls=%async_computation | async-start | bytes 65536 | tf_op jit(solution)/shard_map/while/body/eval_jaxpr/all_to_all | solution.py:69
  183.2 10.1 %all-to-all-start = ((bf16[16,2,2,256]{3,2,1,0:T(2,128)(2,1)}), bf16[16,2,2,256]{3,2,1,0:T(2,128)(2,1)S(1)}, u32[]{:S(2)}, u32[]{:S(2)}) async-start(bf16[16,2,2,256]{3,2,1,0:T(2,128)(2,1)} %broadcast_select_fusion.2), calls=%async_computation | async-start | bytes 65536 | tf_op jit(solution)/shard_map/while/body/eval_jaxpr/all_to_all | solution.py:69
  202.5 10.1 %all-to-all-start = ((bf16[16,2,2,256]{3,2,1,0:T(2,128)(2,1)}), bf16[16,2,2,256]{3,2,1,0:T(2,128)(2,1)S(1)}, u32[]{:S(2)}, u32[]{:S(2)}) async-start(bf16[16,2,2,256]{3,2,1,0:T(2,128)(2,1)} %broadcast_select_fusion.2), calls=%async_computation | async-start | bytes 65536 | tf_op jit(solution)/shard_map/while/body/eval_jaxpr/all_to_all | solution.py:69
  221.7 10.1 %all-to-all-start = ((bf16[16,2,2,256]{3,2,1,0:T(2,128)(2,1)}), bf16[16,2,2,256]{3,2,1,0:T(2,128)(2,1)S(1)}, u32[]{:S(2)}, u32[]{:S(2)}) async-start(bf16[16,2,2,256]{3,2,1,0:T(2,128)(2,1)} %broadcast_select_fusion.2), calls=%async_computation | async-start | bytes 65536 | tf_op jit(solution)/shard_map/while/body/eval_jaxpr/all_to_all | solution.py:69
  241.0 10.1 %all-to-all-start = ((bf16[16,2,2,256]{3,2,1,0:T(2,128)(2,1)}), bf16[16,2,2,256]{3,2,1,0:T(2,128)(2,1)S(1)}, u32[]{:S(2)}, u32[]{:S(2)}) async-start(bf16[16,2,2,256]{3,2,1,0:T(2,128)(2,1)} %broadcast_select_fusion.2), calls=%async_computation | async-start | bytes 65536 | tf_op jit(solution)/shard_map/while/body/eval_jaxpr/all_to_all | solution.py:69
  260.2 10.1 %all-to-all-start = ((bf16[16,2,2,256]{3,2,1,0:T(2,128)(2,1)}), bf16[16,2,2,256]{3,2,1,0:T(2,128)(2,1)S(1)}, u32[]{:S(2)}, u32[]{:S(2)}) async-start(bf16[16,2,2,256]{3,2,1,0:T(2,128)(2,1)} %broadcast_select_fusion.2), calls=%async_computation | async-start | bytes 65536 | tf_op jit(solution)/shard_map/while/body/eval_jaxpr/all_to_all | solution.py:69
  298.7 10.1 %all-to-all-start = ((bf16[16,2,2,256]{3,2,1,0:T(2,128)(2,1)}), bf16[16,2,2,256]{3,2,1,0:T(2,128)(2,1)S(1)}, u32[]{:S(2)}, u32[]{:S(2)}) async-start(bf16[16,2,2,256]{3,2,1,0:T(2,128)(2,1)} %broadcast_select_fusion.2), calls=%async_computation | async-start | bytes 65536 | tf_op jit(solution)/shard_map/while/body/eval_jaxpr/all_to_all | solution.py:69
  356.5 10.1 %all-to-all-start = ((bf16[16,2,2,256]{3,2,1,0:T(2,128)(2,1)}), bf16[16,2,2,256]{3,2,1,0:T(2,128)(2,1)S(1)}, u32[]{:S(2)}, u32[]{:S(2)}) async-start(bf16[16,2,2,256]{3,2,1,0:T(2,128)(2,1)} %broadcast_select_fusion.2), calls=%async_computation | async-start | bytes 65536 | tf_op jit(solution)/shard_map/while/body/eval_jaxpr/all_to_all | solution.py:69
  414.2 10.1 %all-to-all-start = ((bf16[16,2,2,256]{3,2,1,0:T(2,128)(2,1)}), bf16[16,2,2,256]{3,2,1,0:T(2,128)(2,1)S(1)}, u32[]{:S(2)}, u32[]{:S(2)}) async-start(bf16[16,2,2,256]{3,2,1,0:T(2,128)(2,1)} %broadcast_select_fusion.2), calls=%async_computation | async-start | bytes 65536 | tf_op jit(solution)/shard_map/while/body/eval_jaxpr/all_to_all | solution.py:69
  472.0 10.1 %all-to-all-start = ((bf16[16,2,2,256]{3,2,1,0:T(2,128)(2,1)}), bf16[16,2,2,256]{3,2,1,0:T(2,128)(2,1)S(1)}, u32[]{:S(2)}, u32[]{:S(2)}) async-start(bf16[16,2,2,256]{3,2,1,0:T(2,128)(2,1)} %broadcast_select_fusion.2), calls=%async_computation | async-start | bytes 65536 | tf_op jit(solution)/shard_map/while/body/eval_jaxpr/all_to_all | solution.py:69
  491.2 10.1 %all-to-all-start = ((bf16[16,2,2,256]{3,2,1,0:T(2,128)(2,1)}), bf16[16,2,2,256]{3,2,1,0:T(2,128)(2,1)S(1)}, u32[]{:S(2)}, u32[]{:S(2)}) async-start(bf16[16,2,2,256]{3,2,1,0:T(2,128)(2,1)} %broadcast_select_fusion.2), calls=%async_computation | async-start | bytes 65536 | tf_op jit(solution)/shard_map/while/body/eval_jaxpr/all_to_all | solution.py:69
  529.7 10.1 %all-to-all-start = ((bf16[16,2,2,256]{3,2,1,0:T(2,128)(2,1)}), bf16[16,2,2,256]{3,2,1,0:T(2,128)(2,1)S(1)}, u32[]{:S(2)}, u32[]{:S(2)}) async-start(bf16[16,2,2,256]{3,2,1,0:T(2,128)(2,1)} %broadcast_select_fusion.2), calls=%async_computation | async-start | bytes 65536 | tf_op jit(solution)/shard_map/while/body/eval_jaxpr/all_to_all | solution.py:69
  549.0 10.1 %all-to-all-start = ((bf16[16,2,2,256]{3,2,1,0:T(2,128)(2,1)}), bf16[16,2,2,256]{3,2,1,0:T(2,128)(2,1)S(1)}, u32[]{:S(2)}, u32[]{:S(2)}) async-start(bf16[16,2,2,256]{3,2,1,0:T(2,128)(2,1)} %broadcast_select_fusion.2), calls=%async_computation | async-start | bytes 65536 | tf_op jit(solution)/shard_map/while/body/eval_jaxpr/all_to_all | solution.py:69
  606.7 10.1 %all-to-all-start = ((bf16[16,2,2,256]{3,2,1,0:T(2,128)(2,1)}), bf16[16,2,2,256]{3,2,1,0:T(2,128)(2,1)S(1)}, u32[]{:S(2)}, u32[]{:S(2)}) async-start(bf16[16,2,2,256]{3,2,1,0:T(2,128)(2,1)} %broadcast_select_fusion.2), calls=%async_computation | async-start | bytes 65536 | tf_op jit(solution)/shard_map/while/body/eval_jaxpr/all_to_all | solution.py:69
  664.5 10.1 %all-to-all-start = ((bf16[16,2,2,256]{3,2,1,0:T(2,128)(2,1)}), bf16[16,2,2,256]{3,2,1,0:T(2,128)(2,1)S(1)}, u32[]{:S(2)}, u32[]{:S(2)}) async-start(bf16[16,2,2,256]{3,2,1,0:T(2,128)(2,1)} %broadcast_select_fusion.2), calls=%async_computation | async-start | bytes 65536 | tf_op jit(solution)/shard_map/while/body/eval_jaxpr/all_to_all | solution.py:69
  722.2 10.1 %all-to-all-start = ((bf16[16,2,2,256]{3,2,1,0:T(2,128)(2,1)}), bf16[16,2,2,256]{3,2,1,0:T(2,128)(2,1)S(1)}, u32[]{:S(2)}, u32[]{:S(2)}) async-start(bf16[16,2,2,256]{3,2,1,0:T(2,128)(2,1)} %broadcast_select_fusion.2), calls=%async_computation | async-start | bytes 65536 | tf_op jit(solution)/shard_map/while/body/eval_jaxpr/all_to_all | solution.py:69
  780.0 10.1 %all-to-all-start = ((bf16[16,2,2,256]{3,2,1,0:T(2,128)(2,1)}), bf16[16,2,2,256]{3,2,1,0:T(2,128)(2,1)S(1)}, u32[]{:S(2)}, u32[]{:S(2)}) async-start(bf16[16,2,2,256]{3,2,1,0:T(2,128)(2,1)} %broadcast_select_fusion.2), calls=%async_computation | async-start | bytes 65536 | tf_op jit(solution)/shard_map/while/body/eval_jaxpr/all_to_all | solution.py:69
  (17 other events, 168.0 us)
where the time goes:
time: 806 us; the launch traced here: 793 us
  starting transfers between devices  239 us (30%)
  other arithmetic  185 us (23%)
  matrix products  127 us (16%)
  waiting for transfers between devices  99.1 us (12%)
  local copies, waits for them, and re-layouts  74.6 us (9%)
  loops' own time  58.4 us (7%)
    all_to_all x40, starting transfers between devices, pair_step(): lax.all_to_all(fourier_rows, 'wave', split_axis=0, concat_axis=0, tiled=T...  239 us
    all_to_all x40, waiting for transfers between devices, pair_step(): lax.all_to_all(fourier_rows, 'wave', split_axis=0, concat_axis=0, tiled=T...  99.1 us
    select_n x80, other arithmetic, parity_half(): jnp.where(in_lower, spectra, zeroed)  85.7 us
    dot_general x80, matrix products, parity_half(): return jnp.dot(panel, masked, preferred_element_type=jnp.float32)  76.8 us
    convert_element_type x40, other arithmetic, wave_tables(): cosine = (factor * jnp.cos(angles)).astype(jnp.bfloat16)  66.4 us
    another operation x1, loops' own time, on_device(): summed = lax.fori_loop(0, pairs_dev, pair_step, initial)  58.4 us
    dot_general x40, matrix products, fourier_sum(): jnp.einsum('psahwrf,pswrn->ahfn', shaped, wave_table, preferred_element_t...  50.4 us
    select_n x80, other arithmetic, pair_step(): fourier_rows = jnp.take(legendre_pair(operands), all_bands, axis=0)  29.1 us
  transfers between devices with their start and end apart: 40, of which 40 were waited for; matrix products, arithmetic and copies ran while one was open for 9% of the time, Pallas kernels for 0%

commit v1 on v0

v1 whole, which is shorter than its diff:
```python
import functools
import math

import jax
import jax.numpy as jnp
from jax import lax
from jax.experimental import pallas as pl
from jax.experimental.pallas import tpu as pltpu
from jax.sharding import PartitionSpec as P

M = 1280
NLON = 2688
HALF = NLON // 2
ROWS = 8
LANES = 128


def round_up(value, unit):
    return -(-value // unit) * unit


def legendre_kernel(waves_ref, se_ref, so_ref, le_ref, lo_ref, out_ref, columns_ref, rows_ref):
    lats = le_ref.shape[1]
    he, ho = le_ref.shape[2], lo_ref.shape[2]
    columns_ref[...] = se_ref[...].astype(jnp.float32).reshape(columns_ref.shape)
    base = pl.program_id(0) * ROWS
    ids_e = lax.broadcasted_iota(jnp.int32, (lats, he), 1)
    ids_o = lax.broadcasted_iota(jnp.int32, (lats, ho), 1)
    for p in range(ROWS):
        low = waves_ref[base + p]
        low_is_even = low % 2 == 0

        def split(panel, ids, count):
            in_low = ids < count
            zero = jnp.zeros_like(panel)
            lower = jnp.where(in_low, panel, zero)
            upper = jnp.where(in_low, zero, panel)
            return jnp.concatenate([lower, upper], axis=0)

        even = split(le_ref[p], ids_e, (M - low + 1) // 2)
        odd = split(lo_ref[p], ids_o, (M - low) // 2)
        xe = columns_ref[pl.ds(p, he, stride=ROWS), :].astype(jnp.bfloat16)
        sym = jnp.dot(even, xe, preferred_element_type=jnp.float32)
        anti = jnp.dot(odd, so_ref[p], preferred_element_type=jnp.float32)
        first = jnp.where(low_is_even, 0, lats) + p * 2 * lats
        second = jnp.where(low_is_even, lats, 0) + p * 2 * lats
        north, south = sym + anti, sym - anti
        rows_ref[0, pl.ds(pl.multiple_of(first, ROWS), lats), :] = north[:lats]
        rows_ref[0, pl.ds(pl.multiple_of(second, ROWS), lats), :] = north[lats:]
        rows_ref[1, pl.ds(pl.multiple_of(first, ROWS), lats), :] = south[:lats]
        rows_ref[1, pl.ds(pl.multiple_of(second, ROWS), lats), :] = south[lats:]

    def emit(lat, carry):
        for h in range(2):
            for w in range(2):
                picked = rows_ref[h, pl.ds(w * lats + lat, ROWS, stride=2 * lats), :]
                out_ref[lat, h, w] = picked.astype(jnp.bfloat16)
        return carry

    lax.fori_loop(0, lats, emit, 0, unroll=8)


def legendre_stage(waves, spectra_even, spectra_odd, legendre_even, legendre_odd):
    pairs, he, width = spectra_even.shape
    ho = spectra_odd.shape[1]
    lats = legendre_even.shape[1]
    by_column = jnp.transpose(spectra_even, (1, 0, 2))
    return pl.pallas_call(
        legendre_kernel,
        out_shape=jax.ShapeDtypeStruct((lats, 2, 2, pairs, width), jnp.bfloat16),
        grid_spec=pltpu.PrefetchScalarGridSpec(
            num_scalar_prefetch=1,
            grid=(pairs // ROWS,),
            in_specs=[
                pl.BlockSpec((he, ROWS, width), lambda i, w: (0, i, 0)),
                pl.BlockSpec((ROWS, ho, width), lambda i, w: (i, 0, 0)),
                pl.BlockSpec((ROWS, lats, he), lambda i, w: (i, 0, 0)),
                pl.BlockSpec((ROWS, lats, ho), lambda i, w: (i, 0, 0)),
            ],
            out_specs=pl.BlockSpec((lats, 2, 2, ROWS, width), lambda i, w: (0, 0, 0, i, 0)),
            scratch_shapes=[
                pltpu.VMEM((he * ROWS, width), jnp.float32),
                pltpu.VMEM((2, ROWS * 2 * lats, width), jnp.float32),
            ],
        ),
        compiler_params=pltpu.CompilerParams(vmem_limit_bytes=40 * 1024 * 1024),
        cost_estimate=pl.CostEstimate(
            flops=4 * pairs * lats * 2 * (he + ho) * width,
            bytes_accessed=2 * pairs * (he + ho) * (width + lats),
            transcendentals=0,
        ),
        name="legendre",
    )(waves, by_column, spectra_odd, legendre_even, legendre_odd)


def pick_kernel(bands_ref, rows_ref, out_ref, sems):
    lats = rows_ref.shape[0]

    def copy(slot):
        return pltpu.make_async_copy(rows_ref.at[bands_ref[slot]], out_ref.at[slot], sems.at[slot])

    @pl.loop(0, lats)
    def _(slot):
        copy(slot).start()

    @pl.loop(0, lats)
    def _(slot):
        copy(slot).wait()


def pick_latitudes(bands, rows):
    return pl.pallas_call(
        pick_kernel,
        out_shape=jax.ShapeDtypeStruct(rows.shape, rows.dtype),
        grid_spec=pltpu.PrefetchScalarGridSpec(
            num_scalar_prefetch=1,
            grid=(),
            in_specs=[pl.BlockSpec(memory_space=pl.ANY)],
            out_specs=pl.BlockSpec(memory_space=pl.ANY),
            scratch_shapes=[pltpu.SemaphoreType.DMA((rows.shape[0],))],
        ),
        name="pick",
    )(bands, rows)


def table_kernel(waves_ref, out_ref):
    low = waves_ref[...]
    rows = low.shape[0]
    even = jnp.where(low % 2 == 0, low, M - 1 - low)
    odd = M - 1 - even
    lane = lax.broadcasted_iota(jnp.int32, (rows, LANES), 1).astype(jnp.float32)
    unit = 2.0 * math.pi / NLON

    def angle(product):
        turns = jnp.floor(product * (1.0 / NLON))
        return (product - turns * NLON) * unit

    for w, wave in enumerate((even, odd)):
        number = wave.astype(jnp.float32)
        factor = jnp.where(wave == 0, 1.0, 2.0)
        start = angle(number * lane)
        step = angle(number * LANES)
        c, s = factor * jnp.cos(start), -factor * jnp.sin(start)
        dc, ds = jnp.cos(step), jnp.sin(step)
        for b in range(0, HALF, LANES):
            size = min(LANES, HALF - b)
            out_ref[w, 0, :, b : b + size] = c[:, :size].astype(jnp.bfloat16)
            out_ref[w, 1, :, b : b + size] = s[:, :size].astype(jnp.bfloat16)
            c, s = c * dc + s * ds, s * dc - c * ds


def wave_tables(waves):
    total = waves.shape[0]
    rows = 64
    return pl.pallas_call(
        table_kernel,
        out_shape=jax.ShapeDtypeStruct((2, 2, total, HALF), jnp.bfloat16),
        grid=(total // rows,),
        in_specs=[pl.BlockSpec((rows, LANES), lambda i: (i, 0))],
        out_specs=pl.BlockSpec((2, 2, rows, HALF), lambda i: (0, 0, i, 0)),
        compiler_params=pltpu.CompilerParams(vmem_limit_bytes=32 * 1024 * 1024),
        cost_estimate=pl.CostEstimate(
            flops=4 * 4 * total * HALF, bytes_accessed=8 * total * HALF, transcendentals=8 * total * LANES
        ),
        name="tables",
    )(jnp.broadcast_to(waves[:, None], (total, LANES)))


def fourier_kernel(arrived_ref, table_ref, out_ref, left_ref):
    devices, slots, _, _, pairs, width = arrived_ref.shape
    fields = width // 2
    total = devices * pairs
    for w in range(2):
        for s in range(slots):
            for h in range(2):
                x = jnp.concatenate([arrived_ref[d, s, h, w] for d in range(devices)], axis=0)
                xt = x.T
                r = (s * 2 + h) * fields
                left_ref[w, r : r + fields, :total] = xt[:fields]
                left_ref[w, r : r + fields, total:] = xt[fields:]
    chunk = 256
    ends = list(range(0, HALF, chunk)) + [HALF]
    for lo, hi in zip(ends[:-1], ends[1:]):
        sums = []
        for w in range(2):
            cos, sin = table_ref[w, 0, :, lo:hi], table_ref[w, 1, :, lo:hi]
            sums.append(
                jnp.dot(left_ref[w], jnp.concatenate([cos, sin], axis=0), preferred_element_type=jnp.float32)
            )
        plus = (sums[0] + sums[1]).astype(jnp.bfloat16)
        minus = (sums[0] - sums[1]).astype(jnp.bfloat16)
        out_ref[:, lo:hi] = plus
        out_ref[:, HALF + lo : HALF + hi] = minus


def fourier_stage(arrived, table):
    devices, slots, _, _, pairs, width = arrived.shape
    fields = width // 2
    total = devices * pairs
    out = pl.pallas_call(
        fourier_kernel,
        out_shape=jax.ShapeDtypeStruct((slots * 2 * fields, NLON), jnp.bfloat16),
        in_specs=[pl.BlockSpec(memory_space=pltpu.VMEM)] * 2,
        out_specs=pl.BlockSpec(memory_space=pltpu.VMEM),
        scratch_shapes=[pltpu.VMEM((2, slots * 2 * fields, 2 * total), jnp.bfloat16)],
        compiler_params=pltpu.CompilerParams(vmem_limit_bytes=40 * 1024 * 1024),
        name="fourier",
    )(arrived, table)
    return out.reshape(slots, 2, fields, NLON)


def on_device(wave_pairs, band_owner, spectra_even, spectra_odd, legendre_even, legendre_odd):
    devices = lax.axis_size("wave")
    pairs = round_up(wave_pairs.shape[0], ROWS)
    extra = pairs - wave_pairs.shape[0]
    slots = band_owner.shape[0]
    width = spectra_even.shape[2]
    if extra:
        wave_pairs = jnp.pad(wave_pairs, (0, extra))
        spectra_even, spectra_odd, legendre_even, legendre_odd = (
            jnp.pad(a, ((0, extra), (0, 0), (0, 0)))
            for a in (spectra_even, spectra_odd, legendre_even, legendre_odd)
        )

    own = jnp.pad(jnp.concatenate([wave_pairs, band_owner]), (0, round_up(pairs + slots, LANES) - pairs - slots))
    index = lax.all_to_all(jnp.broadcast_to(own, (devices,) + own.shape), "wave", 0, 0, tiled=True)
    all_pairs = index[:, :pairs].reshape(-1)
    all_bands = index[:, pairs : pairs + slots].reshape(-1)

    rows = legendre_stage(wave_pairs, spectra_even, spectra_odd, legendre_even, legendre_odd)
    picked = pick_latitudes(all_bands, rows).reshape(devices, slots, 2, 2, pairs, width)
    arrived = lax.all_to_all(picked, "wave", 0, 0, tiled=True)
    table = wave_tables(all_pairs)
    return fourier_stage(arrived, table)


def solution(mesh):
    return jax.shard_map(
        on_device,
        mesh=mesh,
        in_specs=(
            P("wave"),
            P("wave"),
            P("wave", None, "grp"),
            P("wave", None, "grp"),
            P("wave", None, None),
            P("wave", None, None),
        ),
        out_specs=P("wave", None, "grp", None),
        check_vma=False,
    )
```

time: 806 us -> 112 us (0.14); the launches traced: 793 us -> 111 us
  starting transfers between devices: 239 us -> 12.6 us
  other arithmetic: 185 us -> 0.75 us
  matrix products: 127 us -> 0 us
  waiting for transfers between devices: 99.1 us -> 19.7 us
  Pallas kernels: 0 us -> 63.1 us
  local copies, waits for them, and re-layouts: 74.6 us -> 15 us
  loops' own time: 58.4 us -> 0 us
    all_to_all x40 -> x2, starting transfers between devices: 239 us -> 12.6 us  [the longest x1 6.55 us: on_device(): lax.all_to_all(jnp.broadcast_to(own, (devices,) + own.shape), 'wave', 0,...]
    dot_general x120 -> x0, matrix products: 127 us -> none  [the longest x80 76.8 us: parity_half(): return jnp.dot(panel, masked, preferred_element_type=jnp.float32)]
    select_n x200 -> x0, other arithmetic: 115 us -> none  [the longest x80 85.7 us: parity_half(): jnp.where(in_lower, spectra, zeroed)]
    all_to_all x40 -> x2, waiting for transfers between devices: 99.1 us -> 19.7 us  [the longest x1 19.7 us: on_device(): arrived = lax.all_to_all(picked, 'wave', 0, 0, tiled=True)]
    convert_element_type x41 -> x0, other arithmetic: 67.6 us -> none  [the longest x40 66.4 us: wave_tables(): cosine = (factor * jnp.cos(angles)).astype(jnp.bfloat16)]
    pallas_call x0 -> x4, Pallas kernels: none -> 63.1 us  [the longest x1 41.8 us: pick_latitudes(): pl.pallas_call(pick_kernel, out_shape=jax.ShapeDtypeStruct(rows.shape, ro...]
    another operation x1 -> x0, loops' own time: 58.4 us -> none  [on_device(): summed = lax.fori_loop(0, pairs_dev, pair_step, initial)]
    gather x40 -> x0, local copies, waits for them, and re-layouts: 25.4 us -> none  [pair_step(): fourier_rows = jnp.take(legendre_pair(operands), all_bands, axis=0)]
  transfers between devices with their start and end apart: 40 -> 2, of which waited for: 40 -> 1; matrix products, arithmetic and copies ran while one was open for 9% -> 0% of each run, Pallas kernels for 0% -> 16%
where the time goes in v1:
time: 112 us; the launch traced here: 111 us
  Pallas kernels  63.1 us (56%)
  waiting for transfers between devices  19.7 us (18%)
  local copies, waits for them, and re-layouts  15 us (13%)
  starting transfers between devices  12.6 us (11%)
    pallas_call x1, Pallas kernels, pick_latitudes(): pl.pallas_call(pick_kernel, out_shape=jax.ShapeDtypeStruct(rows.shape, ro...  41.8 us
    all_to_all x1, waiting for transfers between devices, on_device(): arrived = lax.all_to_all(picked, 'wave', 0, 0, tiled=True)  19.7 us
    unnamed x14, local copies, waits for them, and re-layouts  13.5 us
    pallas_call x1, Pallas kernels, legendre_stage(): pl.pallas_call(legendre_kernel, out_shape=jax.ShapeDtypeStruct((lats, 2,...  10 us
    pallas_call x1, Pallas kernels, wave_tables(): pl.pallas_call(table_kernel, out_shape=jax.ShapeDtypeStruct((2, 2, total,...  7.74 us
    all_to_all x1, starting transfers between devices, on_device(): lax.all_to_all(jnp.broadcast_to(own, (devices,) + own.shape), 'wave', 0,...  6.55 us
    all_to_all x1, starting transfers between devices, on_device(): arrived = lax.all_to_all(picked, 'wave', 0, 0, tiled=True)  6.04 us
    pallas_call x1, Pallas kernels, fourier_stage(): pl.pallas_call(fourier_kernel, out_shape=jax.ShapeDtypeStruct((slots * 2...  3.51 us
  transfers between devices with their start and end apart: 2, of which 1 were waited for; matrix products, arithmetic and copies ran while one was open for 0% of the time, Pallas kernels for 16%

profile of v1, /device:TPU:13, one launch (start us, length us, event | category | flops | bytes accessed | tf_op | source)
XLA Modules:
  0.0 111.1 jit_solution(1565753952592588258)
XLA Ops:
  0.0 0.7 pad_add_fusion
  0.8 0.6 broadcast_in_dim.10
  1.4 6.6 %all-to-all-start = ((s32[16,1,128]{2,1,0:T(1,128)}), s32[16,1,128]{2,1,0:T(1,128)S(1)}, u32[]{:S(2)}, u32[]{:S(2)}) async-start(s32[16,1,128]{2,1,0:T(1,128)} %broadcast_in_dim.10), calls=%async_computation | async-start | bytes 16384 | tf_op jit(solution)/shard_map/all_to_all | solution.py:226
  7.9 0.0 copy-start.2
  7.9 2.9 %copy-done.2 = bf16[40,640,128]{2,1,0:T(8,128)(2,1)S(1)} copy-done((bf16[40,640,128]{2,1,0:T(8,128)(2,1)S(1)}, bf16[40,640,128]{2,1,0:T(8,128)(2,1)}, u32[]{:S(2)}) %copy-start.2) | copy-done | bytes 6553624
  10.8 1.5 %copy-done.4 = bf16[40,32,641]{2,1,0:T(8,128)(2,1)S(1)} copy-done((bf16[40,32,641]{2,1,0:T(8,128)(2,1)S(1)}, bf16[40,32,641]{2,1,0:T(8,128)(2,1)}, u32[]{:S(2)}) %copy-start.4) | copy-done | bytes 1640984
  12.3 1.4 %copy-done.5 = bf16[40,32,640]{2,1,0:T(8,128)(2,1)S(1)} copy-done((bf16[40,32,640]{2,1,0:T(8,128)(2,1)S(1)}, bf16[40,32,640]{2,1,0:T(8,128)(2,1)}, u32[]{:S(2)}) %copy-start.5) | copy-done | bytes 1638424
  13.7 0.7 copy-done.6
  14.4 10.0 %legendre.1.rows_ref = bf16[32,2,2,40,128]{4,3,2,1,0:T(8,128)(2,1)S(1)} custom-call(s32[40]{0:T(128)S(1)} %copy-done.6, bf16[641,40,128]{2,1,0:T(8,128)(2,1)} %bitcast.5, bf16[40,640,128]{2,1,0:T(8,128)(2,1)S(1)} %copy-done.2, bf16[40,32,641]{2,1,0:T(8,128)(2,1)S(1)} %copy-done.4, bf16[40,32,640]{2,1,0:T(8,128)(2,1)S(1)} %copy-done.5), custom_call_target="tpu_custom_call" | custom-call | flops 1679032320 | bytes 16396800 | tf_op jit(solution)/shard_map/legendre/pallas_call | solution.py:68
  24.4 0.0 copy-start.3
  24.5 1.0 copy-done.3
  25.5 0.0 all-to-all-done
  25.5 0.1 slice.8
  25.6 0.6 reshape.14.bands_ref
  26.2 41.8 %pick.1 = bf16[32,2,2,40,128]{4,3,2,1,0:T(8,128)(2,1)} custom-call(s32[32]{0:T(128)} %reshape.14.bands_ref, bf16[32,2,2,40,128]{4,3,2,1,0:T(8,128)(2,1)} %copy-done.3), custom_call_target="tpu_custom_call" | custom-call | tf_op jit(solution)/shard_map/pick/pallas_call | solution.py:112
  68.0 6.0 %all-to-all-start.1 = ((bf16[16,2,2,2,40,128]{5,4,3,2,1,0:T(8,128)(2,1)}), bf16[16,2,2,2,40,128]{5,4,3,2,1,0:T(8,128)(2,1)S(1)}, u32[]{:S(2)}, u32[]{:S(2)}) async-start(bf16[16,2,2,2,40,128]{5,4,3,2,1,0:T(8,128)(2,1)} %bitcast.6), calls=%async_computation.1 | async-start | bytes 2621440 | tf_op jit(solution)/shard_map/all_to_all | solution.py:232
  74.0 0.1 broadcast_in_dim.11
  74.1 0.1 broadcast_in_dim.12.waves_ref
  74.2 7.7 %tables.1.table_ref = bf16[2,2,640,1344]{3,2,1,0:T(8,128)(2,1)S(1)} custom-call(s32[640,128]{1,0:T(8,128)S(1)} %broadcast_in_dim.12.waves_ref), custom_call_target="tpu_custom_call" | custom-call | flops 13762560 | bytes 6881280 | tf_op jit(solution)/shard_map/tables/pallas_call | solution.py:155
  82.0 0.0 copy-start
  82.0 2.9 %copy-done = bf16[2,2,640,1344]{3,2,1,0:T(8,128)(2,1)} copy-done((bf16[2,2,640,1344]{3,2,1,0:T(8,128)(2,1)}, bf16[2,2,640,1344]{3,2,1,0:T(8,128)(2,1)S(1)}, u32[]{:S(2)}) %copy-start) | copy-done | bytes 6881304
  84.9 19.7 %all-to-all-done.1.arrived_ref = bf16[16,2,2,2,40,128]{5,4,3,2,1,0:T(8,128)(2,1)S(1)} async-done(((bf16[16,2,2,2,40,128]{5,4,3,2,1,0:T(8,128)(2,1)}), bf16[16,2,2,2,40,128]{5,4,3,2,1,0:T(8,128)(2,1)S(1)}, u32[]{:S(2)}, u32[]{:S(2)}) %all-to-all-start.1) | async-done | bytes 1310752 | tf_op jit(solution)/shard_map/all_to_all | solution.py:232
  104.6 3.0 %copy-done.1 = bf16[2,2,640,1344]{3,2,1,0:T(8,128)(2,1)S(1)} copy-done((bf16[2,2,640,1344]{3,2,1,0:T(8,128)(2,1)S(1)}, bf16[2,2,640,1344]{3,2,1,0:T(8,128)(2,1)}, u32[]{:S(2)}) %copy-start.1) | copy-done | bytes 6881304
  107.6 3.5 %fourier.1 = bf16[256,2688]{1,0:T(8,128)(2,1)} custom-call(bf16[16,2,2,2,40,128]{5,4,3,2,1,0:T(8,128)(2,1)S(1)} %all-to-all-done.1.arrived_ref, bf16[2,2,640,1344]{3,2,1,0:T(8,128)(2,1)S(1)} %copy-done.1), custom_call_target="tpu_custom_call" | custom-call | tf_op jit(solution)/shard_map/fourier/pallas_call | solution.py:200
  (5 shorter events, 0.0 us)
Async XLA Ops:
  1.4 24.1 %all-to-all-start = ((s32[16,1,128]{2,1,0:T(1,128)}), s32[16,1,128]{2,1,0:T(1,128)S(1)}, u32[]{:S(2)}, u32[]{:S(2)}) async-start(s32[16,1,128]{2,1,0:T(1,128)} %broadcast_in_dim.10), calls=%async_computation | async-start | bytes 16384 | tf_op jit(solution)/shard_map/all_to_all | solution.py:226
  7.9 2.9 %copy-start.2 = (bf16[40,640,128]{2,1,0:T(8,128)(2,1)S(1)}, bf16[40,640,128]{2,1,0:T(8,128)(2,1)}, u32[]{:S(2)}) copy-start(bf16[40,640,128]{2,1,0:T(8,128)(2,1)} %so_ref.1) | copy-start | bytes 19660804
  10.8 1.5 %copy-start.4 = (bf16[40,32,641]{2,1,0:T(8,128)(2,1)S(1)}, bf16[40,32,641]{2,1,0:T(8,128)(2,1)}, u32[]{:S(2)}) copy-start(bf16[40,32,641]{2,1,0:T(8,128)(2,1)} %le_ref.1) | copy-start | bytes 4922884
  12.3 1.4 %copy-start.5 = (bf16[40,32,640]{2,1,0:T(8,128)(2,1)S(1)}, bf16[40,32,640]{2,1,0:T(8,128)(2,1)}, u32[]{:S(2)}) copy-start(bf16[40,32,640]{2,1,0:T(8,128)(2,1)} %lo_ref.1) | copy-start | bytes 4915204
  13.7 0.7 copy-start.6
  24.4 1.1 copy-start.3
  68.0 36.6 %all-to-all-start.1 = ((bf16[16,2,2,2,40,128]{5,4,3,2,1,0:T(8,128)(2,1)}), bf16[16,2,2,2,40,128]{5,4,3,2,1,0:T(8,128)(2,1)S(1)}, u32[]{:S(2)}, u32[]{:S(2)}) async-start(bf16[16,2,2,2,40,128]{5,4,3,2,1,0:T(8,128)(2,1)} %bitcast.6), calls=%async_computation.1 | async-start | bytes 2621440 | tf_op jit(solution)/shard_map/all_to_all | solution.py:232
  82.0 2.9 %copy-start = (bf16[2,2,640,1344]{3,2,1,0:T(8,128)(2,1)}, bf16[2,2,640,1344]{3,2,1,0:T(8,128)(2,1)S(1)}, u32[]{:S(2)}) copy-start(bf16[2,2,640,1344]{3,2,1,0:T(8,128)(2,1)S(1)} %tables.1.table_ref) | copy-start | bytes 20643844
  104.6 3.0 %copy-start.1 = (bf16[2,2,640,1344]{3,2,1,0:T(8,128)(2,1)S(1)}, bf16[2,2,640,1344]{3,2,1,0:T(8,128)(2,1)}, u32[]{:S(2)}) copy-start(bf16[2,2,640,1344]{3,2,1,0:T(8,128)(2,1)} %copy-done) | copy-start | bytes 20643844

commit v2 on v1

v2 whole, which is shorter than its diff:
```python
import functools
import math

import jax
import jax.numpy as jnp
from jax import lax
from jax.experimental import pallas as pl
from jax.experimental.pallas import tpu as pltpu
from jax.sharding import PartitionSpec as P

M = 1280
NLON = 2688
HALF = NLON // 2
ROWS = 8
LANES = 128


def round_up(value, unit):
    return -(-value // unit) * unit


def legendre_kernel(
    waves_ref, se_hbm, so_hbm, le_hbm, lo_hbm, out_ref, se_ref, so_ref, le_ref, lo_ref, columns_ref, sems
):
    pairs, lats, he = le_ref.shape
    ho = lo_ref.shape[2]
    groups = pairs // ROWS

    def copies(g):
        at = pl.ds(pl.multiple_of(g * ROWS, ROWS), ROWS)
        return (
            pltpu.make_async_copy(lo_hbm.at[at], lo_ref.at[at], sems.at[0, g]),
            pltpu.make_async_copy(so_hbm.at[at], so_ref.at[at], sems.at[1, g]),
            pltpu.make_async_copy(le_hbm.at[at], le_ref.at[at], sems.at[2, g]),
            pltpu.make_async_copy(se_hbm.at[:, at], se_ref.at[:, at], sems.at[3, g]),
        )

    for g in range(groups):
        for copy in copies(g):
            copy.start()

    ids_e = lax.broadcasted_iota(jnp.int32, (lats, he), 1)
    ids_o = lax.broadcasted_iota(jnp.int32, (lats, ho), 1)

    def split(panel, ids, count):
        in_low = ids < count
        zero = jnp.zeros_like(panel)
        lower = jnp.where(in_low, panel, zero)
        upper = jnp.where(in_low, zero, panel)
        return jnp.concatenate([lower, upper], axis=0)

    @pl.loop(0, groups)
    def _(g):
        for copy in copies(g):
            copy.wait()
        base = pl.multiple_of(g * ROWS, ROWS)
        columns_ref[...] = se_ref[:, pl.ds(base, ROWS), :].astype(jnp.float32).reshape(columns_ref.shape)
        for p in range(ROWS):
            low = waves_ref[base + p]
            parity = low % 2
            even = split(le_ref[base + p], ids_e, (M - low + 1) // 2)
            odd = split(lo_ref[base + p], ids_o, (M - low) // 2)
            xe = columns_ref[pl.ds(p, he, stride=ROWS), :].astype(jnp.bfloat16)
            sym = jnp.dot(even, xe, preferred_element_type=jnp.float32)
            anti = jnp.dot(odd, so_ref[base + p], preferred_element_type=jnp.float32)
            for h, rows in enumerate((sym + anti, sym - anti)):
                for w in range(2):
                    start = (parity ^ w) * (lats * pairs) + base + p
                    out_ref[h, pl.ds(start, lats, stride=pairs), :] = rows[w * lats : (w + 1) * lats]


def in_hbm(x):
    return pltpu.with_memory_space_constraint(x, pltpu.HBM)


def in_vmem(x):
    return pltpu.with_memory_space_constraint(x, pltpu.VMEM)


def legendre_stage(waves, spectra_even, spectra_odd, legendre_even, legendre_odd):
    pairs, he, width = spectra_even.shape
    ho = spectra_odd.shape[1]
    lats = legendre_even.shape[1]
    by_column = jnp.transpose(spectra_even, (1, 0, 2))
    return pl.pallas_call(
        legendre_kernel,
        out_shape=pltpu.VMEM((2, 2 * lats * pairs, width), jnp.float32),
        grid_spec=pltpu.PrefetchScalarGridSpec(
            num_scalar_prefetch=1,
            grid=(),
            in_specs=[pl.BlockSpec(memory_space=pl.ANY)] * 4,
            out_specs=pl.BlockSpec(memory_space=pltpu.VMEM),
            scratch_shapes=[
                pltpu.VMEM((he, pairs, width), jnp.bfloat16),
                pltpu.VMEM((pairs, ho, width), jnp.bfloat16),
                pltpu.VMEM((pairs, lats, he), jnp.bfloat16),
                pltpu.VMEM((pairs, lats, ho), jnp.bfloat16),
                pltpu.VMEM((he * ROWS, width), jnp.float32),
                pltpu.SemaphoreType.DMA((4, pairs // ROWS)),
            ],
        ),
        compiler_params=pltpu.CompilerParams(vmem_limit_bytes=40 * 1024 * 1024),
        cost_estimate=pl.CostEstimate(
            flops=4 * pairs * lats * 2 * (he + ho) * width,
            bytes_accessed=2 * pairs * (he + ho) * (width + lats),
            transcendentals=0,
        ),
        name="legendre",
    )(waves, in_hbm(by_column), in_hbm(spectra_odd), in_hbm(legendre_even), in_hbm(legendre_odd))


def pick_kernel(bands_ref, rows_ref, out_ref):
    lats, _, _, pairs, _ = out_ref.shape

    def emit(slot, carry):
        band = bands_ref[slot]
        for h in range(2):
            for w in range(2):
                start = pl.multiple_of((w * lats + band) * pairs, ROWS)
                out_ref[slot, h, w] = rows_ref[h, pl.ds(start, pairs), :].astype(jnp.bfloat16)
        return carry

    lax.fori_loop(0, lats, emit, 0, unroll=8)


def pick_latitudes(bands, rows, pairs):
    lats = bands.shape[0]
    width = rows.shape[2]
    return pl.pallas_call(
        pick_kernel,
        out_shape=jax.ShapeDtypeStruct((lats, 2, 2, pairs, width), jnp.bfloat16),
        grid_spec=pltpu.PrefetchScalarGridSpec(
            num_scalar_prefetch=1,
            grid=(),
            in_specs=[pl.BlockSpec(memory_space=pltpu.VMEM)],
            out_specs=pl.BlockSpec(memory_space=pltpu.VMEM),
        ),
        compiler_params=pltpu.CompilerParams(vmem_limit_bytes=16 * 1024 * 1024),
        name="pick",
    )(bands, in_vmem(rows))


def table_kernel(waves_ref, out_ref):
    unit = 2.0 * math.pi / NLON
    block = 64

    def angle(product):
        turns = jnp.floor(product * (1.0 / NLON))
        return (product - turns * NLON) * unit

    @pl.loop(0, waves_ref.shape[0] // block)
    def _(i):
        at = pl.ds(pl.multiple_of(i * block, block), block)
        low = waves_ref[at, :]
        even = jnp.where(low % 2 == 0, low, M - 1 - low)
        odd = M - 1 - even
        lane = lax.broadcasted_iota(jnp.int32, low.shape, 1).astype(jnp.float32)
        for w, wave in enumerate((even, odd)):
            number = wave.astype(jnp.float32)
            factor = jnp.where(wave == 0, 1.0, 2.0)
            start = angle(number * lane)
            step = angle(number * LANES)
            c, s = factor * jnp.cos(start), -factor * jnp.sin(start)
            dc, ds = jnp.cos(step), jnp.sin(step)
            for b in range(0, HALF, LANES):
                size = min(LANES, HALF - b)
                out_ref[w, 0, at, b : b + size] = c[:, :size].astype(jnp.bfloat16)
                out_ref[w, 1, at, b : b + size] = s[:, :size].astype(jnp.bfloat16)
                c, s = c * dc + s * ds, s * dc - c * ds


def wave_tables(waves):
    total = waves.shape[0]
    return pl.pallas_call(
        table_kernel,
        out_shape=pltpu.VMEM((2, 2, total, HALF), jnp.bfloat16),
        in_specs=[pl.BlockSpec(memory_space=pltpu.VMEM)],
        out_specs=pl.BlockSpec(memory_space=pltpu.VMEM),
        compiler_params=pltpu.CompilerParams(vmem_limit_bytes=16 * 1024 * 1024),
        cost_estimate=pl.CostEstimate(
            flops=4 * 4 * total * HALF, bytes_accessed=8 * total * HALF, transcendentals=8 * total * LANES
        ),
        name="tables",
    )(jnp.broadcast_to(waves[:, None], (total, LANES)))


def fourier_kernel(arrived_ref, table_ref, out_ref, left_ref):
    devices, slots, _, _, pairs, width = arrived_ref.shape
    fields = width // 2
    total = devices * pairs
    for w in range(2):
        for s in range(slots):
            for h in range(2):
                x = jnp.concatenate([arrived_ref[d, s, h, w] for d in range(devices)], axis=0)
                xt = x.T
                r = (s * 2 + h) * fields
                left_ref[w, r : r + fields, :total] = xt[:fields]
                left_ref[w, r : r + fields, total:] = xt[fields:]
    chunk = 256
    ends = list(range(0, HALF, chunk)) + [HALF]
    for lo, hi in zip(ends[:-1], ends[1:]):
        sums = []
        for w in range(2):
            cos, sin = table_ref[w, 0, :, lo:hi], table_ref[w, 1, :, lo:hi]
            sums.append(
                jnp.dot(left_ref[w], jnp.concatenate([cos, sin], axis=0), preferred_element_type=jnp.float32)
            )
        plus = (sums[0] + sums[1]).astype(jnp.bfloat16)
        minus = (sums[0] - sums[1]).astype(jnp.bfloat16)
        out_ref[:, lo:hi] = plus
        out_ref[:, HALF + lo : HALF + hi] = minus


def fourier_stage(arrived, table):
    devices, slots, _, _, pairs, width = arrived.shape
    fields = width // 2
    total = devices * pairs
    out = pl.pallas_call(
        fourier_kernel,
        out_shape=jax.ShapeDtypeStruct((slots * 2 * fields, NLON), jnp.bfloat16),
        in_specs=[pl.BlockSpec(memory_space=pltpu.VMEM)] * 2,
        out_specs=pl.BlockSpec(memory_space=pltpu.VMEM),
        scratch_shapes=[pltpu.VMEM((2, slots * 2 * fields, 2 * total), jnp.bfloat16)],
        compiler_params=pltpu.CompilerParams(vmem_limit_bytes=24 * 1024 * 1024),
        name="fourier",
    )(arrived, in_vmem(table))
    return out.reshape(slots, 2, fields, NLON)


def on_device(wave_pairs, band_owner, spectra_even, spectra_odd, legendre_even, legendre_odd):
    devices = lax.axis_size("wave")
    pairs = round_up(wave_pairs.shape[0], ROWS)
    extra = pairs - wave_pairs.shape[0]
    slots = band_owner.shape[0]
    width = spectra_even.shape[2]
    if extra:
        wave_pairs = jnp.pad(wave_pairs, (0, extra))
        spectra_even, spectra_odd, legendre_even, legendre_odd = (
            jnp.pad(a, ((0, extra), (0, 0), (0, 0)))
            for a in (spectra_even, spectra_odd, legendre_even, legendre_odd)
        )

    own = jnp.pad(jnp.concatenate([wave_pairs, band_owner]), (0, round_up(pairs + slots, LANES) - pairs - slots))
    index = lax.all_gather(own, "wave", axis=0)
    all_pairs = index[:, :pairs].reshape(-1)
    all_bands = index[:, pairs : pairs + slots].reshape(-1)

    rows = legendre_stage(wave_pairs, spectra_even, spectra_odd, legendre_even, legendre_odd)
    picked = pick_latitudes(all_bands, rows, pairs).reshape(devices, slots, 2, 2, pairs, width)
    arrived = lax.all_to_all(picked, "wave", 0, 0, tiled=True)
    table = wave_tables(all_pairs)
    return fourier_stage(arrived, table)


def solution(mesh):
    return jax.shard_map(
        on_device,
        mesh=mesh,
        in_specs=(
            P("wave"),
            P("wave"),
            P("wave", None, "grp"),
            P("wave", None, "grp"),
            P("wave", None, None),
            P("wave", None, None),
        ),
        out_specs=P("wave", None, "grp", None),
        check_vma=False,
    )
```

time: 112 us -> 75.6 us (0.67)
  Pallas kernels: 63.1 us -> 21.5 us
  blocking collectives: 0 us -> 15.5 us
  local copies, waits for them, and re-layouts: 15 us -> 7.02 us
  starting transfers between devices: 12.6 us -> 10.3 us
    pallas_call x3, Pallas kernels: 59.5 us -> 18 us  [the longest x1 9.1 us: legendre_stage(): pl.pallas_call(legendre_kernel, out_shape=pltpu.VMEM((2, 2 * lats * pairs...]
    all_gather x0 -> x1, blocking collectives: none -> 15.5 us  [on_device(): index = lax.all_gather(own, 'wave', axis=0)]
    unnamed x14 -> x7, local copies, waits for them, and re-layouts: 13.5 us -> 6.64 us
    all_to_all x1 -> x0, starting transfers between devices: 6.55 us -> none  [on_device(): lax.all_to_all(jnp.broadcast_to(own, (devices,) + own.shape), 'wave', 0,...]
    all_to_all x1, starting transfers between devices: 6.04 us -> 10.3 us  [on_device(): arrived = lax.all_to_all(picked, 'wave', 0, 0, tiled=True)]
  transfers between devices with their start and end apart: 2 -> 1, of which waited for: 1 -> 1; matrix products, arithmetic and copies ran while one was open for 0% -> 0% of each run, Pallas kernels for 16% -> 9%
where the time goes in v2:
time: 75.6 us; the launch traced here: 75.3 us
  Pallas kernels  21.5 us (28%)
  waiting for transfers between devices  20.3 us (27%)
  blocking collectives  15.5 us (21%)
  starting transfers between devices  10.3 us (14%)
  local copies, waits for them, and re-layouts  7.02 us (9%)
    all_to_all x1, waiting for transfers between devices, on_device(): arrived = lax.all_to_all(picked, 'wave', 0, 0, tiled=True)  20.3 us
    all_gather x1, blocking collectives, on_device(): index = lax.all_gather(own, 'wave', axis=0)  15.5 us
    all_to_all x1, starting transfers between devices, on_device(): arrived = lax.all_to_all(picked, 'wave', 0, 0, tiled=True)  10.3 us
    pallas_call x1, Pallas kernels, legendre_stage(): pl.pallas_call(legendre_kernel, out_shape=pltpu.VMEM((2, 2 * lats * pairs...  9.1 us
    pallas_call x1, Pallas kernels, wave_tables(): pl.pallas_call(table_kernel, out_shape=pltpu.VMEM((2, 2, total, HALF), jn...  7.12 us
    unnamed x7, local copies, waits for them, and re-layouts  6.64 us
    pallas_call x1, Pallas kernels, fourier_stage(): pl.pallas_call(fourier_kernel, out_shape=jax.ShapeDtypeStruct((slots * 2...  3.51 us
    pallas_call x1, Pallas kernels, pick_latitudes(): pl.pallas_call(pick_kernel, out_shape=jax.ShapeDtypeStruct((lats, 2, 2, p...  1.76 us
  transfers between devices with their start and end apart: 1, of which 1 were waited for; matrix products, arithmetic and copies ran while one was open for 0% of the time, Pallas kernels for 9%

profile of v2, /device:TPU:13, one launch (start us, length us, event | category | flops | bytes accessed | tf_op | source)
XLA Modules:
  0.0 75.3 jit_solution(9471476566522818706)
XLA Ops:
  0.0 0.7 pad_add_fusion
  0.8 15.5 %all-gather.1 = s32[16,1,128]{2,1,0:T(1,128)S(1)} all-gather(s32[1,1,128]{2,1,0:T(1,128)S(1)} %pad_bitcast_fusion), channel_id=2, replica_groups=mesh['grp'=2,'wave'=16] {'wave'}, dimensions={0}, use_global_device_ids=true | all-gather | bytes 8704 | tf_op jit(solution)/shard_map/all_gather | solution.py:244
  16.2 0.1 slice.8
  16.3 0.1 reshape.10.bands_ref
  16.4 0.0 copy-start.2
  16.4 0.6 copy-done.2
  17.0 9.1 %legendre.1.rows_ref = f32[2,2560,128]{2,1,0:T(8,128)S(1)} custom-call(s32[40]{0:T(128)S(1)} %copy-done.2, bf16[641,40,128]{2,1,0:T(8,128)(2,1)} %bitcast.7, bf16[40,640,128]{2,1,0:T(8,128)(2,1)} %so_hbm.1, bf16[40,32,641]{2,1,0:T(8,128)(2,1)} %le_hbm.1, bf16[40,32,640]{2,1,0:T(8,128)(2,1)} %lo_hbm.1), custom_call_target="tpu_custom_call" | custom-call | flops 1679032320 | bytes 16396800 | tf_op jit(solution)/shard_map/legendre/pallas_call | solution.py:85
  26.2 1.8 %pick.1 = bf16[32,2,2,40,128]{4,3,2,1,0:T(8,128)(2,1)} custom-call(s32[32]{0:T(128)S(1)} %reshape.10.bands_ref, f32[2,2560,128]{2,1,0:T(8,128)S(1)} %legendre.1.rows_ref), custom_call_target="tpu_custom_call" | custom-call | tf_op jit(solution)/shard_map/pick/pallas_call | solution.py:129
  27.9 10.3 %all-to-all-start = ((bf16[16,2,2,2,40,128]{5,4,3,2,1,0:T(8,128)(2,1)}), bf16[16,2,2,2,40,128]{5,4,3,2,1,0:T(8,128)(2,1)S(1)}, u32[]{:S(2)}, u32[]{:S(2)}) async-start(bf16[16,2,2,2,40,128]{5,4,3,2,1,0:T(8,128)(2,1)} %bitcast.3), calls=%async_computation | async-start | bytes 2621440 | tf_op jit(solution)/shard_map/all_to_all | solution.py:250
  38.2 0.1 broadcast_in_dim.7
  38.3 0.1 broadcast_in_dim.8.waves_ref
  38.4 7.1 %tables.1.table_ref = bf16[2,2,640,1344]{3,2,1,0:T(8,128)(2,1)S(1)} custom-call(s32[640,128]{1,0:T(8,128)S(1)} %broadcast_in_dim.8.waves_ref), custom_call_target="tpu_custom_call" | custom-call | flops 13762560 | bytes 6881280 | tf_op jit(solution)/shard_map/tables/pallas_call | solution.py:174
  45.6 0.0 copy-start
  45.6 2.9 %copy-done = bf16[2,2,640,1344]{3,2,1,0:T(8,128)(2,1)} copy-done((bf16[2,2,640,1344]{3,2,1,0:T(8,128)(2,1)}, bf16[2,2,640,1344]{3,2,1,0:T(8,128)(2,1)S(1)}, u32[]{:S(2)}) %copy-start) | copy-done | bytes 6881304
  48.5 20.3 %all-to-all-done.arrived_ref = bf16[16,2,2,2,40,128]{5,4,3,2,1,0:T(8,128)(2,1)S(1)} async-done(((bf16[16,2,2,2,40,128]{5,4,3,2,1,0:T(8,128)(2,1)}), bf16[16,2,2,2,40,128]{5,4,3,2,1,0:T(8,128)(2,1)S(1)}, u32[]{:S(2)}, u32[]{:S(2)}) %all-to-all-start) | async-done | bytes 1310752 | tf_op jit(solution)/shard_map/all_to_all | solution.py:250
  68.8 0.0 copy-start.1
  68.8 3.0 %copy-done.1 = bf16[2,2,640,1344]{3,2,1,0:T(8,128)(2,1)S(1)} copy-done((bf16[2,2,640,1344]{3,2,1,0:T(8,128)(2,1)S(1)}, bf16[2,2,640,1344]{3,2,1,0:T(8,128)(2,1)}, u32[]{:S(2)}) %copy-start.1) | copy-done | bytes 6881304
  71.8 3.5 %fourier.1 = bf16[256,2688]{1,0:T(8,128)(2,1)} custom-call(bf16[16,2,2,2,40,128]{5,4,3,2,1,0:T(8,128)(2,1)S(1)} %all-to-all-done.arrived_ref, bf16[2,2,640,1344]{3,2,1,0:T(8,128)(2,1)S(1)} %copy-done.1), custom_call_target="tpu_custom_call" | custom-call | tf_op jit(solution)/shard_map/fourier/pallas_call | solution.py:218
  (1 shorter events, 0.0 us)
Async XLA Ops:
  16.4 0.7 copy-start.2
  27.9 40.9 %all-to-all-start = ((bf16[16,2,2,2,40,128]{5,4,3,2,1,0:T(8,128)(2,1)}), bf16[16,2,2,2,40,128]{5,4,3,2,1,0:T(8,128)(2,1)S(1)}, u32[]{:S(2)}, u32[]{:S(2)}) async-start(bf16[16,2,2,2,40,128]{5,4,3,2,1,0:T(8,128)(2,1)} %bitcast.3), calls=%async_computation | async-start | bytes 2621440 | tf_op jit(solution)/shard_map/all_to_all | solution.py:250
  45.6 2.9 %copy-start = (bf16[2,2,640,1344]{3,2,1,0:T(8,128)(2,1)}, bf16[2,2,640,1344]{3,2,1,0:T(8,128)(2,1)S(1)}, u32[]{:S(2)}) copy-start(bf16[2,2,640,1344]{3,2,1,0:T(8,128)(2,1)S(1)} %tables.1.table_ref) | copy-start | bytes 20643844
  68.8 3.0 %copy-start.1 = (bf16[2,2,640,1344]{3,2,1,0:T(8,128)(2,1)S(1)}, bf16[2,2,640,1344]{3,2,1,0:T(8,128)(2,1)}, u32[]{:S(2)}) copy-start(bf16[2,2,640,1344]{3,2,1,0:T(8,128)(2,1)} %copy-done) | copy-start | bytes 20643844

commit v3 on v2

v3 whole, which is shorter than its diff:
```python
import functools
import math

import jax
import jax.numpy as jnp
from jax import lax
from jax.experimental import pallas as pl
from jax.experimental.pallas import tpu as pltpu
from jax.sharding import PartitionSpec as P

M = 1280
NLON = 2688
HALF = NLON // 2
ROWS = 8
LANES = 128


def round_up(value, unit):
    return -(-value // unit) * unit


def legendre_kernel(
    first, waves_ref, se_hbm, so_hbm, le_hbm, lo_hbm, out_ref, se_ref, so_ref, le_ref, lo_ref, columns_ref, sems
):
    pairs, lats, he = le_ref.shape
    ho = lo_ref.shape[2]
    groups = pairs // ROWS

    def copies(g):
        at = pl.ds(pl.multiple_of(g * ROWS, ROWS), ROWS)
        source = pl.ds(pl.multiple_of(first + g * ROWS, ROWS), ROWS)
        return (
            pltpu.make_async_copy(lo_hbm.at[source], lo_ref.at[at], sems.at[0, g]),
            pltpu.make_async_copy(so_hbm.at[source], so_ref.at[at], sems.at[1, g]),
            pltpu.make_async_copy(le_hbm.at[source], le_ref.at[at], sems.at[2, g]),
            pltpu.make_async_copy(se_hbm.at[:, source], se_ref.at[g], sems.at[3, g]),
        )

    for g in range(groups):
        for copy in copies(g):
            copy.start()

    ids_e = lax.broadcasted_iota(jnp.int32, (lats, he), 1)
    ids_o = lax.broadcasted_iota(jnp.int32, (lats, ho), 1)

    def split(panel, ids, count):
        in_low = ids < count
        zero = jnp.zeros_like(panel)
        lower = jnp.where(in_low, panel, zero)
        upper = jnp.where(in_low, zero, panel)
        return jnp.concatenate([lower, upper], axis=0)

    @pl.loop(0, groups)
    def _(g):
        for copy in copies(g):
            copy.wait()
        base = pl.multiple_of(g * ROWS, ROWS)
        columns_ref[...] = se_ref[g].astype(jnp.float32).reshape(columns_ref.shape)
        for p in range(ROWS):
            low = waves_ref[first + base + p]
            parity = low % 2
            even = split(le_ref[base + p], ids_e, (M - low + 1) // 2)
            odd = split(lo_ref[base + p], ids_o, (M - low) // 2)
            xe = columns_ref[pl.ds(p, he, stride=ROWS), :].astype(jnp.bfloat16)
            sym = jnp.dot(even, xe, preferred_element_type=jnp.float32)
            anti = jnp.dot(odd, so_ref[base + p], preferred_element_type=jnp.float32)
            for h, rows in enumerate((sym + anti, sym - anti)):
                for w in range(2):
                    start = (parity ^ w) * (lats * pairs) + base + p
                    out_ref[h, pl.ds(start, lats, stride=pairs), :] = rows[w * lats : (w + 1) * lats]


def in_hbm(x):
    return pltpu.with_memory_space_constraint(x, pltpu.HBM)


def in_vmem(x):
    return pltpu.with_memory_space_constraint(x, pltpu.VMEM)


def legendre_stage(first, pairs, waves, spectra_even, spectra_odd, legendre_even, legendre_odd):
    _, he, width = spectra_even.shape
    ho = spectra_odd.shape[1]
    lats = legendre_even.shape[1]
    by_column = jnp.transpose(spectra_even, (1, 0, 2))
    return pl.pallas_call(
        functools.partial(legendre_kernel, first),
        out_shape=pltpu.VMEM((2, 2 * lats * pairs, width), jnp.float32),
        grid_spec=pltpu.PrefetchScalarGridSpec(
            num_scalar_prefetch=1,
            grid=(),
            in_specs=[pl.BlockSpec(memory_space=pl.ANY)] * 4,
            out_specs=pl.BlockSpec(memory_space=pltpu.VMEM),
            scratch_shapes=[
                pltpu.VMEM((pairs // ROWS, he, ROWS, width), jnp.bfloat16),
                pltpu.VMEM((pairs, ho, width), jnp.bfloat16),
                pltpu.VMEM((pairs, lats, he), jnp.bfloat16),
                pltpu.VMEM((pairs, lats, ho), jnp.bfloat16),
                pltpu.VMEM((he * ROWS, width), jnp.float32),
                pltpu.SemaphoreType.DMA((4, pairs // ROWS)),
            ],
        ),
        compiler_params=pltpu.CompilerParams(vmem_limit_bytes=40 * 1024 * 1024),
        cost_estimate=pl.CostEstimate(
            flops=4 * pairs * lats * 2 * (he + ho) * width,
            bytes_accessed=2 * pairs * (he + ho) * (width + lats),
            transcendentals=0,
        ),
        name=f"legendre_{first}",
    )(in_hbm(waves), in_hbm(by_column), in_hbm(spectra_odd), in_hbm(legendre_even), in_hbm(legendre_odd))


def pick_kernel(bands_ref, rows_ref, out_ref):
    lats, _, _, pairs, _ = out_ref.shape

    def emit(slot, carry):
        band = bands_ref[slot]
        for h in range(2):
            for w in range(2):
                start = pl.multiple_of((w * lats + band) * pairs, ROWS)
                out_ref[slot, h, w] = rows_ref[h, pl.ds(start, pairs), :].astype(jnp.bfloat16)
        return carry

    lax.fori_loop(0, lats, emit, 0, unroll=8)


def pick_latitudes(bands, rows, pairs):
    lats = bands.shape[0]
    width = rows.shape[2]
    return pl.pallas_call(
        pick_kernel,
        out_shape=jax.ShapeDtypeStruct((lats, 2, 2, pairs, width), jnp.bfloat16),
        grid_spec=pltpu.PrefetchScalarGridSpec(
            num_scalar_prefetch=1,
            grid=(),
            in_specs=[pl.BlockSpec(memory_space=pltpu.VMEM)],
            out_specs=pl.BlockSpec(memory_space=pltpu.VMEM),
        ),
        compiler_params=pltpu.CompilerParams(vmem_limit_bytes=16 * 1024 * 1024),
        name=f"pick_{pairs}",
    )(bands, in_vmem(rows))


def table_kernel(waves_ref, out_ref):
    low = waves_ref[...]
    even = jnp.where(low % 2 == 0, low, M - 1 - low)
    odd = M - 1 - even
    lane = lax.broadcasted_iota(jnp.int32, low.shape, 1).astype(jnp.float32)
    unit = 2.0 * math.pi / NLON

    def angle(product):
        turns = jnp.floor(product * (1.0 / NLON))
        return (product - turns * NLON) * unit

    for w, wave in enumerate((even, odd)):
        number = wave.astype(jnp.float32)
        factor = jnp.where(wave == 0, 1.0, 2.0)
        start = angle(number * lane)
        step = angle(number * LANES)
        c, s = factor * jnp.cos(start), -factor * jnp.sin(start)
        dc, ds = jnp.cos(step), jnp.sin(step)
        for b in range(0, HALF, LANES):
            size = min(LANES, HALF - b)
            out_ref[w, 0, :, b : b + size] = c[:, :size].astype(jnp.bfloat16)
            out_ref[w, 1, :, b : b + size] = s[:, :size].astype(jnp.bfloat16)
            c, s = c * dc + s * ds, s * dc - c * ds


def wave_tables(waves):
    total = waves.shape[0]
    rows = 64
    return pl.pallas_call(
        table_kernel,
        out_shape=pltpu.HBM((2, 2, total, HALF), jnp.bfloat16),
        grid=(total // rows,),
        in_specs=[pl.BlockSpec((rows, LANES), lambda i: (i, 0))],
        out_specs=pl.BlockSpec((2, 2, rows, HALF), lambda i: (0, 0, i, 0)),
        compiler_params=pltpu.CompilerParams(vmem_limit_bytes=32 * 1024 * 1024),
        cost_estimate=pl.CostEstimate(
            flops=4 * 4 * total * HALF, bytes_accessed=8 * total * HALF, transcendentals=8 * total * LANES
        ),
        name="tables",
    )(jnp.broadcast_to(waves[:, None], (total, LANES)))


def index_kernel(waves_ref, bands_ref, out_ref):
    waves, bands = waves_ref[...], bands_ref[...]
    lanes = out_ref.shape[2]
    rest = jnp.zeros((1, lanes - waves.shape[1] - bands.shape[1]), jnp.int32)
    row = jnp.concatenate([waves, bands, rest], axis=1)
    out_ref[...] = jnp.broadcast_to(row[None], out_ref.shape)


def index_rows(devices, waves, bands):
    lanes = round_up(waves.shape[0] + bands.shape[0], LANES)
    return pl.pallas_call(
        index_kernel,
        out_shape=pltpu.VMEM((devices, 1, lanes), jnp.int32),
        in_specs=[pl.BlockSpec(memory_space=pltpu.VMEM)] * 2,
        out_specs=pl.BlockSpec(memory_space=pltpu.VMEM),
        name="index",
    )(waves[None], bands[None])


def fourier_kernel(start, last, arrived_ref, table_hbm, before_hbm, out_hbm, left_ref, table_ref, sums_ref, row_ref, sems, out_sems):
    devices, slots, _, _, pairs, width = arrived_ref.shape
    fields = width // 2
    total = devices * pairs
    chunk = 256
    ends = list(range(0, HALF, chunk)) + [HALF]
    spans = list(zip(ends[:-1], ends[1:]))

    def loads(i):
        lo, hi = spans[i]
        at = table_hbm.at[:, :, start : start + total, lo:hi]
        copies = [pltpu.make_async_copy(at, table_ref.at[:, :, :, lo:hi], sems.at[0, i])]
        if before_hbm is not None:
            copies.append(
                pltpu.make_async_copy(before_hbm.at[:, :, lo:hi], sums_ref.at[:, :, lo:hi], sems.at[1, i])
            )
        return copies

    for i in range(len(spans)):
        for copy in loads(i):
            copy.start()

    for w in range(2):
        for s in range(slots):
            for h in range(2):
                x = jnp.concatenate([arrived_ref[d, s, h, w] for d in range(devices)], axis=0)
                xt = x.T
                r = (s * 2 + h) * fields
                left_ref[w, r : r + fields, :total] = xt[:fields]
                left_ref[w, r : r + fields, total:] = xt[fields:]

    stores = []
    sent = [0, round_up(HALF, LANES)]
    for i, (lo, hi) in enumerate(spans):
        for copy in loads(i):
            copy.wait()
        e, o = [
            jnp.dot(
                left_ref[w],
                jnp.concatenate([table_ref[w, 0, :, lo:hi], table_ref[w, 1, :, lo:hi]], axis=0),
                preferred_element_type=jnp.float32,
            )
            for w in range(2)
        ]
        plus, minus = e + o, e - o
        if before_hbm is not None:
            plus += sums_ref[0, :, lo:hi]
            minus += sums_ref[1, :, lo:hi]
        if not last:
            sums_ref[0, :, lo:hi] = plus
            sums_ref[1, :, lo:hi] = minus
            copy = pltpu.make_async_copy(sums_ref.at[:, :, lo:hi], out_hbm.at[:, :, lo:hi], out_sems.at[0, i])
            copy.start()
            stores.append(copy)
            continue
        row_ref[:, lo:hi] = plus.astype(jnp.bfloat16)
        row_ref[:, HALF + lo : HALF + hi] = minus.astype(jnp.bfloat16)
        done = hi == HALF
        reach = (round_up(HALF, LANES) if done else hi, NLON if done else (HALF + hi) // LANES * LANES)
        for part in range(2):
            at = slice(sent[part], reach[part])
            copy = pltpu.make_async_copy(row_ref.at[:, at], out_hbm.at[:, at], out_sems.at[part, i])
            copy.start()
            stores.append(copy)
            sent[part] = reach[part]
    for copy in stores:
        copy.wait()


def fourier_stage(arrived, table, start, before, last):
    devices, slots, _, _, pairs, width = arrived.shape
    fields = width // 2
    total = devices * pairs
    rows = slots * 2 * fields
    spans = pl.cdiv(HALF, 256)
    kernel = functools.partial(fourier_kernel, start, last)
    operands = [arrived, in_hbm(table)]
    if before is not None:
        operands.append(before)
    else:
        kernel = lambda a, t, *rest: fourier_kernel(start, last, a, t, None, *rest)
    shape = jax.ShapeDtypeStruct((rows, NLON), jnp.bfloat16) if last else jax.ShapeDtypeStruct((2, rows, HALF), jnp.float32)
    return pl.pallas_call(
        kernel,
        out_shape=shape,
        in_specs=[pl.BlockSpec(memory_space=pltpu.VMEM)] + [pl.BlockSpec(memory_space=pl.ANY)] * (len(operands) - 1),
        out_specs=pl.BlockSpec(memory_space=pl.ANY),
        scratch_shapes=[
            pltpu.VMEM((2, rows, 2 * total), jnp.bfloat16),
            pltpu.VMEM((2, 2, total, HALF), jnp.bfloat16),
            pltpu.VMEM((2, rows, HALF), jnp.float32),
            pltpu.VMEM((rows, NLON), jnp.bfloat16),
            pltpu.SemaphoreType.DMA((2, spans)),
            pltpu.SemaphoreType.DMA((2, spans)),
        ],
        compiler_params=pltpu.CompilerParams(vmem_limit_bytes=40 * 1024 * 1024),
        cost_estimate=pl.CostEstimate(
            flops=8 * rows * total * HALF, bytes_accessed=8 * total * HALF, transcendentals=0
        ),
        name=f"fourier_{start}",
    )(*operands)


def on_device(wave_pairs, band_owner, spectra_even, spectra_odd, legendre_even, legendre_odd):
    devices = lax.axis_size("wave")
    pairs = round_up(wave_pairs.shape[0], ROWS)
    extra = pairs - wave_pairs.shape[0]
    slots = band_owner.shape[0]
    width = spectra_even.shape[2]
    if extra:
        wave_pairs = jnp.pad(wave_pairs, (0, extra))
        spectra_even, spectra_odd, legendre_even, legendre_odd = (
            jnp.pad(a, ((0, extra), (0, 0), (0, 0)))
            for a in (spectra_even, spectra_odd, legendre_even, legendre_odd)
        )
    groups = pairs // ROWS
    cut = groups * 2 // 5 * ROWS
    ranges = [(lo, hi) for lo, hi in ((0, cut), (cut, pairs)) if hi > lo]

    index = lax.all_to_all(index_rows(devices, wave_pairs, band_owner), "wave", 0, 0, tiled=True)[:, 0]
    all_bands = index[:, pairs : pairs + slots].reshape(-1)
    all_pairs = jnp.concatenate([index[:, lo:hi].reshape(-1) for lo, hi in ranges])

    arrived = []
    for lo, hi in ranges:
        rows = legendre_stage(lo, hi - lo, wave_pairs, spectra_even, spectra_odd, legendre_even, legendre_odd)
        picked = pick_latitudes(all_bands, rows, hi - lo).reshape(devices, slots, 2, 2, hi - lo, width)
        arrived.append(lax.all_to_all(picked, "wave", 0, 0, tiled=True))
    table = wave_tables(all_pairs)
    result = None
    for i, (lo, hi) in enumerate(ranges):
        result = fourier_stage(arrived[i], table, devices * lo, result, i == len(ranges) - 1)
    return result.reshape(slots, 2, width // 2, NLON)


def solution(mesh):
    return jax.shard_map(
        on_device,
        mesh=mesh,
        in_specs=(
            P("wave"),
            P("wave"),
            P("wave", None, "grp"),
            P("wave", None, "grp"),
            P("wave", None, None),
            P("wave", None, None),
        ),
        out_specs=P("wave", None, "grp", None),
        check_vma=False,
    )
```

time: 75.6 us -> 65.5 us (0.87)
  blocking collectives: 15.5 us -> 0 us
  Pallas kernels: 21.5 us -> 34 us
  waiting for transfers between devices: 20.3 us -> 12.5 us
  starting transfers between devices: 10.3 us -> 17.6 us
  local copies, waits for them, and re-layouts: 7.02 us -> 0.54 us
    all_gather x1 -> x0, blocking collectives: 15.5 us -> none  [on_device(): index = lax.all_gather(own, 'wave', axis=0)]
    pallas_call x3 -> x6, Pallas kernels: 19.7 us -> 31 us  [the longest x2 11.9 us: legendre_stage(): pl.pallas_call(functools.partial(legendre_kernel, first), out_shape=pltpu...]
    all_to_all x1 -> x3, waiting for transfers between devices: 20.3 us -> 12.5 us  [the longest x2 12.5 us: on_device(): arrived.append(lax.all_to_all(picked, 'wave', 0, 0, tiled=True))]
    all_to_all x1 -> x3, starting transfers between devices: 10.3 us -> 17.6 us  [the longest x2 11 us: on_device(): arrived.append(lax.all_to_all(picked, 'wave', 0, 0, tiled=True))]
    unnamed x7 -> x0, local copies, waits for them, and re-layouts: 6.64 us -> none
    pallas_call x1 -> x2, Pallas kernels: 1.76 us -> 2.95 us  [pick_latitudes(): pl.pallas_call(pick_kernel, out_shape=jax.ShapeDtypeStruct((lats, 2, 2, p...]
  transfers between devices with their start and end apart: 1 -> 3, of which waited for: 1 -> 2; matrix products, arithmetic and copies ran while one was open for 0% -> 1% of each run, Pallas kernels for 9% -> 39%
where the time goes in v3:
time: 65.5 us; the launch traced here: 64.7 us
  Pallas kernels  34 us (52%)
  starting transfers between devices  17.6 us (27%)
  waiting for transfers between devices  12.5 us (19%)
    all_to_all x2, waiting for transfers between devices, on_device(): arrived.append(lax.all_to_all(picked, 'wave', 0, 0, tiled=True))  12.5 us
    pallas_call x2, Pallas kernels, legendre_stage(): pl.pallas_call(functools.partial(legendre_kernel, first), out_shape=pltpu...  11.9 us
    all_to_all x2, starting transfers between devices, on_device(): arrived.append(lax.all_to_all(picked, 'wave', 0, 0, tiled=True))  11 us
    pallas_call x2, Pallas kernels, fourier_stage(): pl.pallas_call(kernel, out_shape=shape, in_specs=[pl.BlockSpec(memory_spa...  9.11 us
    pallas_call x1, Pallas kernels, wave_tables(): pl.pallas_call(table_kernel, out_shape=pltpu.HBM((2, 2, total, HALF), jnp...  8.73 us
    all_to_all x1, starting transfers between devices, on_device(): lax.all_to_all(index_rows(devices, wave_pairs, band_owner), 'wave', 0, 0,...  6.55 us
    pallas_call x2, Pallas kernels, pick_latitudes(): pl.pallas_call(pick_kernel, out_shape=jax.ShapeDtypeStruct((lats, 2, 2, p...  2.95 us
    pallas_call x1, Pallas kernels, index_rows(): pl.pallas_call(index_kernel, out_shape=pltpu.VMEM((devices, 1, lanes), jn...  1.34 us
  transfers between devices with their start and end apart: 3, of which 2 were waited for; matrix products, arithmetic and copies ran while one was open for 1% of the time, Pallas kernels for 39%

profile of v3, /device:TPU:13, one launch (start us, length us, event | category | flops | bytes accessed | tf_op | source)
XLA Modules:
  0.0 64.7 jit_solution(737844807376136252)
XLA Ops:
  0.0 1.3 %index.1 = s32[16,1,128]{2,1,0:T(1,128)} custom-call(s32[1,40]{1,0:T(1,128)} %bitcast.13, s32[1,2]{1,0:T(1,128)} %bitcast.14), custom_call_target="tpu_custom_call" | custom-call | tf_op jit(solution)/shard_map/index/pallas_call | solution.py:196
  1.3 6.6 %all-to-all-start = ((s32[16,1,128]{2,1,0:T(1,128)}), s32[16,1,128]{2,1,0:T(1,128)S(1)}, u32[]{:S(2)}, u32[]{:S(2)}) async-start(s32[16,1,128]{2,1,0:T(1,128)} %index.1), calls=%async_computation | async-start | bytes 16384 | tf_op jit(solution)/shard_map/all_to_all | solution.py:324
  7.9 5.4 %legendre_0.1.rows_ref = f32[2,1024,128]{2,1,0:T(8,128)S(1)} custom-call(s32[40]{0:T(128)} %waves_ref.3, bf16[641,40,128]{2,1,0:T(8,128)(2,1)} %bitcast.8, bf16[40,640,128]{2,1,0:T(8,128)(2,1)} %so_hbm.3, bf16[40,32,641]{2,1,0:T(8,128)(2,1)} %le_hbm.3, bf16[40,32,640]{2,1,0:T(8,128)(2,1)} %lo_hbm.3), custom_call_target="tpu_custom_call" | custom-call | flops 671612928 | bytes 6558720 | tf_op jit(solution)/shard_map/legendre_0/pallas_call | solution.py:86
  13.3 0.0 all-to-all-done
  13.3 0.1 slice.12
  13.3 0.1 reshape.19.bands_ref
  13.4 1.4 %pick_16.1 = bf16[32,2,2,16,128]{4,3,2,1,0:T(8,128)(2,1)} custom-call(s32[32]{0:T(128)S(1)} %reshape.19.bands_ref, f32[2,1024,128]{2,1,0:T(8,128)S(1)} %legendre_0.1.rows_ref), custom_call_target="tpu_custom_call" | custom-call | tf_op jit(solution)/shard_map/pick_16/pallas_call | solution.py:130
  14.9 6.0 %all-to-all-start.2 = ((bf16[16,2,2,2,16,128]{5,4,3,2,1,0:T(8,128)(2,1)}), bf16[16,2,2,2,16,128]{5,4,3,2,1,0:T(8,128)(2,1)S(1)}, u32[]{:S(2)}, u32[]{:S(2)}) async-start(bf16[16,2,2,2,16,128]{5,4,3,2,1,0:T(8,128)(2,1)} %bitcast.5), calls=%async_computation.2 | async-start | bytes 1048576 | tf_op jit(solution)/shard_map/all_to_all | solution.py:332
  20.9 6.5 %legendre_16.1.rows_ref = f32[2,1536,128]{2,1,0:T(8,128)S(1)} custom-call(s32[40]{0:T(128)} %waves_ref.3, bf16[641,40,128]{2,1,0:T(8,128)(2,1)} %bitcast.9, bf16[40,640,128]{2,1,0:T(8,128)(2,1)} %so_hbm.3, bf16[40,32,641]{2,1,0:T(8,128)(2,1)} %le_hbm.3, bf16[40,32,640]{2,1,0:T(8,128)(2,1)} %lo_hbm.3), custom_call_target="tpu_custom_call" | custom-call | flops 1007419392 | bytes 9838080 | tf_op jit(solution)/shard_map/legendre_16/pallas_call | solution.py:86
  27.4 1.5 %pick_24.1 = bf16[32,2,2,24,128]{4,3,2,1,0:T(8,128)(2,1)} custom-call(s32[32]{0:T(128)S(1)} %reshape.19.bands_ref, f32[2,1536,128]{2,1,0:T(8,128)S(1)} %legendre_16.1.rows_ref), custom_call_target="tpu_custom_call" | custom-call | tf_op jit(solution)/shard_map/pick_24/pallas_call | solution.py:130
  28.9 5.5 %all-to-all-done.2.a = bf16[16,2,2,2,16,128]{5,4,3,2,1,0:T(8,128)(2,1)S(1)} async-done(((bf16[16,2,2,2,16,128]{5,4,3,2,1,0:T(8,128)(2,1)}), bf16[16,2,2,2,16,128]{5,4,3,2,1,0:T(8,128)(2,1)S(1)}, u32[]{:S(2)}, u32[]{:S(2)}) %all-to-all-start.2) | async-done | bytes 524320 | tf_op jit(solution)/shard_map/all_to_all | solution.py:332
  34.5 5.0 %all-to-all-start.1 = ((bf16[16,2,2,2,24,128]{5,4,3,2,1,0:T(8,128)(2,1)}), bf16[16,2,2,2,24,128]{5,4,3,2,1,0:T(8,128)(2,1)}, u32[]{:S(2)}, u32[]{:S(2)}) async-start(bf16[16,2,2,2,24,128]{5,4,3,2,1,0:T(8,128)(2,1)} %bitcast.4), calls=%async_computation.1 | async-start | bytes 1572864 | tf_op jit(solution)/shard_map/all_to_all | solution.py:332
  39.5 0.1 slice.14
  39.6 0.1 reshape.21
  39.7 0.1 reshape.22
  39.8 0.1 broadcast_in_dim.14.waves_ref
  39.9 8.7 %tables.1.t.table_hbm = bf16[2,2,640,1344]{3,2,1,0:T(8,128)(2,1)} custom-call(s32[640,128]{1,0:T(8,128)S(1)} %broadcast_in_dim.14.waves_ref), custom_call_target="tpu_custom_call" | custom-call | flops 13762560 | bytes 6881280 | tf_op jit(solution)/shard_map/tables/pallas_call | solution.py:172
  48.6 3.3 %fourier_0.1.before_hbm = f32[2,256,1344]{2,1,0:T(8,128)S(1)} custom-call(bf16[16,2,2,2,16,128]{5,4,3,2,1,0:T(8,128)(2,1)S(1)} %all-to-all-done.2.a, bf16[2,2,640,1344]{3,2,1,0:T(8,128)(2,1)} %tables.1.t.table_hbm), custom_call_target="tpu_custom_call" | custom-call | flops 704643072 | bytes 2752512 | tf_op jit(solution)/shard_map/fourier_0/pallas_call | solution.py:287
  51.9 6.9 %all-to-all-done.1.arrived_ref = bf16[16,2,2,2,24,128]{5,4,3,2,1,0:T(8,128)(2,1)} async-done(((bf16[16,2,2,2,24,128]{5,4,3,2,1,0:T(8,128)(2,1)}), bf16[16,2,2,2,24,128]{5,4,3,2,1,0:T(8,128)(2,1)}, u32[]{:S(2)}, u32[]{:S(2)}) %all-to-all-start.1) | async-done | bytes 786464 | tf_op jit(solution)/shard_map/all_to_all | solution.py:332
  58.9 5.8 %fourier_256.1 = bf16[256,2688]{1,0:T(8,128)(2,1)} custom-call(bf16[16,2,2,2,24,128]{5,4,3,2,1,0:T(8,128)(2,1)} %all-to-all-done.1.arrived_ref, bf16[2,2,640,1344]{3,2,1,0:T(8,128)(2,1)} %tables.1.t.table_hbm, f32[2,256,1344]{2,1,0:T(8,128)S(1)} %fourier_0.1.before_hbm), custom_call_target="tpu_custom_call" | custom-call | flops 1056964608 | bytes 4128768 | tf_op jit(solution)/shard_map/fourier_256/pallas_call | solution.py:287
  (1 shorter events, 0.0 us)
Async XLA Ops:
  1.3 11.9 %all-to-all-start = ((s32[16,1,128]{2,1,0:T(1,128)}), s32[16,1,128]{2,1,0:T(1,128)S(1)}, u32[]{:S(2)}, u32[]{:S(2)}) async-start(s32[16,1,128]{2,1,0:T(1,128)} %index.1), calls=%async_computation | async-start | bytes 16384 | tf_op jit(solution)/shard_map/all_to_all | solution.py:324
  14.9 19.6 %all-to-all-start.2 = ((bf16[16,2,2,2,16,128]{5,4,3,2,1,0:T(8,128)(2,1)}), bf16[16,2,2,2,16,128]{5,4,3,2,1,0:T(8,128)(2,1)S(1)}, u32[]{:S(2)}, u32[]{:S(2)}) async-start(bf16[16,2,2,2,16,128]{5,4,3,2,1,0:T(8,128)(2,1)} %bitcast.5), calls=%async_computation.2 | async-start | bytes 1048576 | tf_op jit(solution)/shard_map/all_to_all | solution.py:332
  34.5 24.4 %all-to-all-start.1 = ((bf16[16,2,2,2,24,128]{5,4,3,2,1,0:T(8,128)(2,1)}), bf16[16,2,2,2,24,128]{5,4,3,2,1,0:T(8,128)(2,1)}, u32[]{:S(2)}, u32[]{:S(2)}) async-start(bf16[16,2,2,2,24,128]{5,4,3,2,1,0:T(8,128)(2,1)} %bitcast.4), calls=%async_computation.1 | async-start | bytes 1572864 | tf_op jit(solution)/shard_map/all_to_all | solution.py:332

commit v4 on v3

--- a/solution.py
+++ b/solution.py
@@ -19,9 +19,12 @@
     return -(-value // unit) * unit
 
 
-def legendre_kernel(
-    first, waves_ref, se_hbm, so_hbm, le_hbm, lo_hbm, out_ref, se_ref, so_ref, le_ref, lo_ref, columns_ref, sems
-):
+def legendre_kernel(first, direct, waves_ref, *refs):
+    bands_ref = refs[0] if direct else None
+    se_hbm, so_hbm, le_hbm, lo_hbm = refs[direct : direct + 4]
+    rest = refs[direct + 4 :]
+    se_ref, so_ref, le_ref, lo_ref, columns_ref, sems = rest[-6:]
+    rows_ref = rest[-7] if direct else rest[0]
     pairs, lats, he = le_ref.shape
     ho = lo_ref.shape[2]
     groups = pairs // ROWS
@@ -36,9 +39,8 @@
             pltpu.make_async_copy(se_hbm.at[:, source], se_ref.at[g], sems.at[3, g]),
         )
 
-    for g in range(groups):
-        for copy in copies(g):
-            copy.start()
+    for copy in copies(0):
+        copy.start()
 
     ids_e = lax.broadcasted_iota(jnp.int32, (lats, he), 1)
     ids_o = lax.broadcasted_iota(jnp.int32, (lats, ho), 1)
@@ -54,6 +56,12 @@
     def _(g):
         for copy in copies(g):
             copy.wait()
+
+        @pl.when(g + 1 < groups)
+        def _():
+            for copy in copies(g + 1):
+                copy.start()
+
         base = pl.multiple_of(g * ROWS, ROWS)
         columns_ref[...] = se_ref[g].astype(jnp.float32).reshape(columns_ref.shape)
         for p in range(ROWS):
@@ -67,7 +75,17 @@
             for h, rows in enumerate((sym + anti, sym - anti)):
                 for w in range(2):
                     start = (parity ^ w) * (lats * pairs) + base + p
-                    out_ref[h, pl.ds(start, lats, stride=pairs), :] = rows[w * lats : (w + 1) * lats]
+                    rows_ref[h, pl.ds(start, lats, stride=pairs), :] = rows[w * lats : (w + 1) * lats]
+
+    if direct:
+        me = lax.axis_index("wave")
+        for k, out_ref in enumerate(rest[:-7]):
+            for slot in range(out_ref.shape[0]):
+                band = bands_ref[(me ^ k) * out_ref.shape[0] + slot]
+                for h in range(2):
+                    for w in range(2):
+                        start = pl.multiple_of((w * lats + band) * pairs, ROWS)
+                        out_ref[slot, h, w] = rows_ref[h, pl.ds(start, pairs), :].astype(jnp.bfloat16)
 
 
 def in_hbm(x):
@@ -78,20 +96,28 @@
     return pltpu.with_memory_space_constraint(x, pltpu.VMEM)
 
 
-def legendre_stage(first, pairs, waves, spectra_even, spectra_odd, legendre_even, legendre_odd):
+def legendre_stage(first, pairs, bands, devices, waves, spectra_even, spectra_odd, legendre_even, legendre_odd):
     _, he, width = spectra_even.shape
     ho = spectra_odd.shape[1]
     lats = legendre_even.shape[1]
     by_column = jnp.transpose(spectra_even, (1, 0, 2))
-    return pl.pallas_call(
-        functools.partial(legendre_kernel, first),
-        out_shape=pltpu.VMEM((2, 2 * lats * pairs, width), jnp.float32),
+    direct = bands is not None
+    rows = pltpu.VMEM((2, 2 * lats * pairs, width), jnp.float32)
+    scalars = [in_hbm(waves)]
+    out_shape = rows
+    if direct:
+        scalars.append(bands)
+        out_shape = [pltpu.VMEM((lats // devices, 2, 2, pairs, width), jnp.bfloat16)] * devices
+    return pl.pallas_call(
+        functools.partial(legendre_kernel, first, int(direct)),
+        out_shape=out_shape,
         grid_spec=pltpu.PrefetchScalarGridSpec(
-            num_scalar_prefetch=1,
+            num_scalar_prefetch=len(scalars),
             grid=(),
             in_specs=[pl.BlockSpec(memory_space=pl.ANY)] * 4,
-            out_specs=pl.BlockSpec(memory_space=pltpu.VMEM),
-            scratch_shapes=[
+            out_specs=[pl.BlockSpec(memory_space=pltpu.VMEM)] * devices if direct else pl.BlockSpec(memory_space=pltpu.VMEM),
+            scratch_shapes=[rows] * direct
+            + [
                 pltpu.VMEM((pairs // ROWS, he, ROWS, width), jnp.bfloat16),
                 pltpu.VMEM((pairs, ho, width), jnp.bfloat16),
                 pltpu.VMEM((pairs, lats, he), jnp.bfloat16),
@@ -107,7 +133,7 @@
             transcendentals=0,
         ),
         name=f"legendre_{first}",
-    )(in_hbm(waves), in_hbm(by_column), in_hbm(spectra_odd), in_hbm(legendre_even), in_hbm(legendre_odd))
+    )(*scalars, in_hbm(by_column), in_hbm(spectra_odd), in_hbm(legendre_even), in_hbm(legendre_odd))
 
 
 def pick_kernel(bands_ref, rows_ref, out_ref):
@@ -202,10 +228,16 @@
     )(waves[None], bands[None])
 
 
-def fourier_kernel(start, last, arrived_ref, table_hbm, before_hbm, out_hbm, left_ref, table_ref, sums_ref, row_ref, sems, out_sems):
-    devices, slots, _, _, pairs, width = arrived_ref.shape
+def fourier_kernel(start, last, parts, added, *refs):
+    arrived = refs[:parts]
+    table_hbm = refs[parts]
+    before_hbm = refs[parts + 1] if added else None
+    out_hbm, left_ref, table_ref, sums_ref, row_ref, sems, out_sems = refs[parts + 1 + added :]
+    if parts == 1:
+        arrived = [arrived[0].at[d] for d in range(arrived[0].shape[0])]
+    slots, _, _, pairs, width = arrived[0].shape
     fields = width // 2
-    total = devices * pairs
+    total = len(arrived) * pairs
     chunk = 256
     ends = list(range(0, HALF, chunk)) + [HALF]
     spans = list(zip(ends[:-1], ends[1:]))
@@ -214,7 +246,7 @@
         lo, hi = spans[i]
         at = table_hbm.at[:, :, start : start + total, lo:hi]
         copies = [pltpu.make_async_copy(at, table_ref.at[:, :, :, lo:hi], sems.at[0, i])]
-        if before_hbm is not None:
+        if added:
             copies.append(
                 pltpu.make_async_copy(before_hbm.at[:, :, lo:hi], sums_ref.at[:, :, lo:hi], sems.at[1, i])
             )
@@ -227,7 +259,7 @@
     for w in range(2):
         for s in range(slots):
             for h in range(2):
-                x = jnp.concatenate([arrived_ref[d, s, h, w] for d in range(devices)], axis=0)
+                x = jnp.concatenate([rows[s, h, w] for rows in arrived], axis=0)
                 xt = x.T
                 r = (s * 2 + h) * fields
                 left_ref[w, r : r + fields, :total] = xt[:fields]
@@ -247,7 +279,7 @@
             for w in range(2)
         ]
         plus, minus = e + o, e - o
-        if before_hbm is not None:
+        if added:
             plus += sums_ref[0, :, lo:hi]
             minus += sums_ref[1, :, lo:hi]
         if not last:
@@ -272,22 +304,21 @@
 
 
 def fourier_stage(arrived, table, start, before, last):
-    devices, slots, _, _, pairs, width = arrived.shape
+    slots, _, _, pairs, width = arrived[0].shape[-5:]
     fields = width // 2
+    devices = len(arrived) if len(arrived) > 1 else arrived[0].shape[0]
     total = devices * pairs
     rows = slots * 2 * fields
     spans = pl.cdiv(HALF, 256)
-    kernel = functools.partial(fourier_kernel, start, last)
-    operands = [arrived, in_hbm(table)]
+    operands = [*arrived, in_hbm(table)]
     if before is not None:
         operands.append(before)
-    else:
-        kernel = lambda a, t, *rest: fourier_kernel(start, last, a, t, None, *rest)
     shape = jax.ShapeDtypeStruct((rows, NLON), jnp.bfloat16) if last else jax.ShapeDtypeStruct((2, rows, HALF), jnp.float32)
     return pl.pallas_call(
-        kernel,
+        functools.partial(fourier_kernel, start, last, len(arrived), int(before is not None)),
         out_shape=shape,
-        in_specs=[pl.BlockSpec(memory_space=pltpu.VMEM)] + [pl.BlockSpec(memory_space=pl.ANY)] * (len(operands) - 1),
+        in_specs=[pl.BlockSpec(memory_space=pltpu.VMEM)] * len(arrived)
+        + [pl.BlockSpec(memory_space=pl.ANY)] * (len(operands) - len(arrived)),
         out_specs=pl.BlockSpec(memory_space=pl.ANY),
         scratch_shapes=[
             pltpu.VMEM((2, rows, 2 * total), jnp.bfloat16),
@@ -318,22 +349,29 @@
             for a in (spectra_even, spectra_odd, legendre_even, legendre_odd)
         )
     groups = pairs // ROWS
-    cut = groups * 2 // 5 * ROWS
-    ranges = [(lo, hi) for lo, hi in ((0, cut), (cut, pairs)) if hi > lo]
+    cut = groups * 2 // 5 * ROWS or pairs
 
     index = lax.all_to_all(index_rows(devices, wave_pairs, band_owner), "wave", 0, 0, tiled=True)[:, 0]
     all_bands = index[:, pairs : pairs + slots].reshape(-1)
-    all_pairs = jnp.concatenate([index[:, lo:hi].reshape(-1) for lo, hi in ranges])
-
-    arrived = []
-    for lo, hi in ranges:
-        rows = legendre_stage(lo, hi - lo, wave_pairs, spectra_even, spectra_odd, legendre_even, legendre_odd)
-        picked = pick_latitudes(all_bands, rows, hi - lo).reshape(devices, slots, 2, 2, hi - lo, width)
-        arrived.append(lax.all_to_all(picked, "wave", 0, 0, tiled=True))
-    table = wave_tables(all_pairs)
-    result = None
-    for i, (lo, hi) in enumerate(ranges):
-        result = fourier_stage(arrived[i], table, devices * lo, result, i == len(ranges) - 1)
+    fields = (wave_pairs, spectra_even, spectra_odd, legendre_even, legendre_odd)
+
+    rows = legendre_stage(0, cut, None, devices, *fields)
+    picked = pick_latitudes(all_bands, rows, cut).reshape(devices, slots, 2, 2, cut, width)
+    next_bands, picked = lax.optimization_barrier((all_bands, picked))
+    waves = [index[:, :cut].reshape(-1)]
+    arrived = [[lax.all_to_all(picked, "wave", 0, 0, tiled=True)]]
+    if cut < pairs:
+        outgoing = legendre_stage(cut, pairs - cut, next_bands, devices, *fields)
+        partner = [[(i, i ^ k) for i in range(devices)] for k in range(devices)]
+        arrived.append([outgoing[0]] + [lax.ppermute(outgoing[k], "wave", partner[k]) for k in range(1, devices)])
+        order = lax.axis_index("wave") ^ jnp.arange(devices)
+        chosen = (order[:, None] == jnp.arange(devices)[None])[:, :, None]
+        waves.append(jnp.sum(jnp.where(chosen, index[None, :, cut:pairs], 0), axis=1).reshape(-1))
+    table = wave_tables(jnp.concatenate(waves))
+    result, start = None, 0
+    for i, some in enumerate(arrived):
+        result = fourier_stage(some, table, start, result, i == len(arrived) - 1)
+        start += waves[i].shape[0]
     return result.reshape(slots, 2, width // 2, NLON)
 
 

time: 65.5 us -> 72.2 us (1.10)
  the two profiles are of different devices: /device:TPU:13 before, /device:TPU:0 now
where the time goes in v4:
time: 72.2 us; the launch traced here: 71.8 us
  starting transfers between devices  34.4 us (48%)
  Pallas kernels  33.4 us (46%)
  waiting for transfers between devices  3.1 us (4%)
    ppermute x15, starting transfers between devices, on_device(): lax.ppermute(outgoing[k], 'wave', partner[k])  21.3 us
    pallas_call x2, Pallas kernels, legendre_stage(): pl.pallas_call(functools.partial(legendre_kernel, first, int(direct)), ou...  13.9 us
    pallas_call x1, Pallas kernels, wave_tables(): pl.pallas_call(table_kernel, out_shape=pltpu.HBM((2, 2, total, HALF), jnp...  8.79 us
    pallas_call x2, Pallas kernels, fourier_stage(): pl.pallas_call(functools.partial(fourier_kernel, start, last, len(arrived...  7.98 us
    all_to_all x1, starting transfers between devices, on_device(): lax.all_to_all(index_rows(devices, wave_pairs, band_owner), 'wave', 0, 0,...  7.39 us
    all_to_all x1, starting transfers between devices, on_device(): arrived = [[lax.all_to_all(picked, 'wave', 0, 0, tiled=True)]]  5.66 us
    ppermute x15, waiting for transfers between devices, on_device(): lax.ppermute(outgoing[k], 'wave', partner[k])  2.74 us
  transfers between devices with their start and end apart: 17, of which 3 were waited for; matrix products, arithmetic and copies ran while one was open for 1% of the time, Pallas kernels for 36%

profile of v4, /device:TPU:0, one launch (start us, length us, event | category | flops | bytes accessed | tf_op | source)
XLA Modules:
  0.0 71.8 jit_solution(15531999662220023696)
XLA Ops:
  0.0 1.3 %index.1 = s32[16,1,128]{2,1,0:T(1,128)} custom-call(s32[1,40]{1,0:T(1,128)} %bitcast.12, s32[1,2]{1,0:T(1,128)} %bitcast.13), custom_call_target="tpu_custom_call" | custom-call | tf_op jit(solution)/shard_map/index/pallas_call | solution.py:222
  1.3 7.4 %all-to-all-start = ((s32[16,1,128]{2,1,0:T(1,128)}), s32[16,1,128]{2,1,0:T(1,128)S(1)}, u32[]{:S(2)}, u32[]{:S(2)}) async-start(s32[16,1,128]{2,1,0:T(1,128)} %index.1), calls=%async_computation | async-start | bytes 16384 | tf_op jit(solution)/shard_map/all_to_all | solution.py:354
  8.7 6.0 %legendre_0.1.rows_ref = f32[2,1024,128]{2,1,0:T(8,128)S(1)} custom-call(s32[40]{0:T(128)} %waves_ref.3, bf16[641,40,128]{2,1,0:T(8,128)(2,1)} %bitcast.7, bf16[40,640,128]{2,1,0:T(8,128)(2,1)} %refs_2_.3, bf16[40,32,641]{2,1,0:T(8,128)(2,1)} %refs_3_.3, bf16[40,32,640]{2,1,0:T(8,128)(2,1)} %refs_4_.1), custom_call_target="tpu_custom_call" | custom-call | flops 671612928 | bytes 6558720 | tf_op jit(solution)/shard_map/legendre_0/pallas_call | solution.py:111
  14.7 0.4 all-to-all-done
  15.2 1.4 %pick_16.1 = bf16[32,2,2,16,128]{4,3,2,1,0:T(8,128)(2,1)} custom-call(s32[32]{0:T(128)S(1)} %reshape.41.bands_ref.refs_0_, f32[2,1024,128]{2,1,0:T(8,128)S(1)} %legendre_0.1.rows_ref), custom_call_target="tpu_custom_call" | custom-call | tf_op jit(solution)/shard_map/pick_16/pallas_call | solution.py:156
  16.7 5.7 %all-to-all-start.1 = ((bf16[16,2,2,2,16,128]{5,4,3,2,1,0:T(8,128)(2,1)}), bf16[16,2,2,2,16,128]{5,4,3,2,1,0:T(8,128)(2,1)S(1)}, u32[]{:S(2)}, u32[]{:S(2)}) async-start(bf16[16,2,2,2,16,128]{5,4,3,2,1,0:T(8,128)(2,1)} %bitcast.4), calls=%async_computation.1 | async-start | bytes 1048576 | tf_op jit(solution)/shard_map/all_to_all | solution.py:362
  22.5 7.9 %legendre_16.1 = (bf16[2,2,2,24,128]{4,3,2,1,0:T(8,128)(2,1)S(1)}, bf16[2,2,2,24,128]{4,3,2,1,0:T(8,128)(2,1)S(1)}, bf16[2,2,2,24,128]{4,3,2,1,0:T(8,128)(2,1)S(...) custom-call(s32[40]{0:T(128)} %waves_ref.3, ...), custom_call_target="tpu_custom_call" | custom-call | flops 1007419392 | bytes 9838080 | tf_op jit(solution)/shard_map/legendre_16/pallas_call | solution.py:111
  30.4 0.5 collective-permute-start
  30.9 1.7 %collective-permute-start.1 = (bf16[2,2,2,24,128]{4,3,2,1,0:T(8,128)(2,1)S(1)}, bf16[2,2,2,24,128]{4,3,2,1,0:T(8,128)(2,1)S(1)}, u32[]{:S(2)}, u32[]{:S(2)}) collective-permute-start(bf16[2,2,2,24,128]{4,3,2,1,0:T(8,128)(2,1)S(1)} %get-tuple-element.26), channel_id=1, source_target_pairs={{0,2},{1,3},{2,0},{3,1},{4,6},{5,7},{6,4},{7,5},{8,10},{9,11},{10,... | collective-permute-start | bytes 147464 | tf_op jit(solution)/shard_map/ppermute | solution.py:366
  32.6 1.7 %collective-permute-start.3 = (bf16[2,2,2,24,128]{4,3,2,1,0:T(8,128)(2,1)S(1)}, bf16[2,2,2,24,128]{4,3,2,1,0:T(8,128)(2,1)S(1)}, u32[]{:S(2)}, u32[]{:S(2)}) collective-permute-start(bf16[2,2,2,24,128]{4,3,2,1,0:T(8,128)(2,1)S(1)} %get-tuple-element.28), channel_id=1, source_target_pairs={{0,4},{1,5},{2,6},{3,7},{4,0},{5,1},{6,2},{7,3},{8,12},{9,13},{10,... | collective-permute-start | bytes 147464 | tf_op jit(solution)/shard_map/ppermute | solution.py:366
  34.7 2.6 %collective-permute-start.5 = (bf16[2,2,2,24,128]{4,3,2,1,0:T(8,128)(2,1)S(1)}, bf16[2,2,2,24,128]{4,3,2,1,0:T(8,128)(2,1)S(1)}, u32[]{:S(2)}, u32[]{:S(2)}) collective-permute-start(bf16[2,2,2,24,128]{4,3,2,1,0:T(8,128)(2,1)S(1)} %get-tuple-element.30), channel_id=1, source_target_pairs={{0,6},{1,7},{2,4},{3,5},{4,2},{5,3},{6,0},{7,1},{8,14},{9,15},{10,... | collective-permute-start | bytes 147464 | tf_op jit(solution)/shard_map/ppermute | solution.py:366
  37.5 2.4 %collective-permute-start.7 = (bf16[2,2,2,24,128]{4,3,2,1,0:T(8,128)(2,1)S(1)}, bf16[2,2,2,24,128]{4,3,2,1,0:T(8,128)(2,1)S(1)}, u32[]{:S(2)}, u32[]{:S(2)}) collective-permute-start(bf16[2,2,2,24,128]{4,3,2,1,0:T(8,128)(2,1)S(1)} %get-tuple-element.32), channel_id=1, source_target_pairs={{0,8},{1,9},{2,10},{3,11},{4,12},{5,13},{6,14},{7,15},{8,0},{9,1},... | collective-permute-start | bytes 147464 | tf_op jit(solution)/shard_map/ppermute | solution.py:366
  39.9 1.0 %collective-permute-start.8 = (bf16[2,2,2,24,128]{4,3,2,1,0:T(8,128)(2,1)S(1)}, bf16[2,2,2,24,128]{4,3,2,1,0:T(8,128)(2,1)S(1)}, u32[]{:S(2)}, u32[]{:S(2)}) collective-permute-start(bf16[2,2,2,24,128]{4,3,2,1,0:T(8,128)(2,1)S(1)} %get-tuple-element.33), channel_id=1, source_target_pairs={{0,9},{1,8},{2,11},{3,10},{4,13},{5,12},{6,15},{7,14},{8,1},{9,0},... | collective-permute-start | bytes 147464 | tf_op jit(solution)/shard_map/ppermute | solution.py:366
  40.9 2.6 %collective-permute-start.9 = (bf16[2,2,2,24,128]{4,3,2,1,0:T(8,128)(2,1)S(1)}, bf16[2,2,2,24,128]{4,3,2,1,0:T(8,128)(2,1)S(1)}, u32[]{:S(2)}, u32[]{:S(2)}) collective-permute-start(bf16[2,2,2,24,128]{4,3,2,1,0:T(8,128)(2,1)S(1)} %get-tuple-element.34), channel_id=1, source_target_pairs={{0,10},{1,11},{2,8},{3,9},{4,14},{5,15},{6,12},{7,13},{8,2},{9,3},... | collective-permute-start | bytes 147464 | tf_op jit(solution)/shard_map/ppermute | solution.py:366
  43.5 0.1 broadcast_in_dim.41.waves_ref
  43.7 8.8 %tables.1.refs_1_.refs_16_ = bf16[2,2,640,1344]{3,2,1,0:T(8,128)(2,1)} custom-call(s32[640,128]{1,0:T(8,128)S(1)} %broadcast_in_dim.41.waves_ref), custom_call_target="tpu_custom_call" | custom-call | flops 13762560 | bytes 6881280 | tf_op jit(solution)/shard_map/tables/pallas_call | solution.py:198
  52.5 0.7 collective-permute-start.10
  53.2 2.8 %collective-permute-start.11 = (bf16[2,2,2,24,128]{4,3,2,1,0:T(8,128)(2,1)S(1)}, bf16[2,2,2,24,128]{4,3,2,1,0:T(8,128)(2,1)S(1)}, u32[]{:S(2)}, u32[]{:S(2)}) collective-permute-start(bf16[2,2,2,24,128]{4,3,2,1,0:T(8,128)(2,1)S(1)} %get-tuple-element.36), channel_id=1, source_target_pairs={{0,12},{1,13},{2,14},{3,15},{4,8},{5,9},{6,10},{7,11},{8,4},{9,5},... | collective-permute-start | bytes 147464 | tf_op jit(solution)/shard_map/ppermute | solution.py:366
  56.0 1.0 %collective-permute-start.12 = (bf16[2,2,2,24,128]{4,3,2,1,0:T(8,128)(2,1)S(1)}, bf16[2,2,2,24,128]{4,3,2,1,0:T(8,128)(2,1)S(1)}, u32[]{:S(2)}, u32[]{:S(2)}) collective-permute-start(bf16[2,2,2,24,128]{4,3,2,1,0:T(8,128)(2,1)S(1)} %get-tuple-element.37), channel_id=1, source_target_pairs={{0,13},{1,12},{2,15},{3,14},{4,9},{5,8},{6,11},{7,10},{8,5},{9,4},... | collective-permute-start | bytes 147464 | tf_op jit(solution)/shard_map/ppermute | solution.py:366
  57.0 3.5 %collective-permute-start.13 = (bf16[2,2,2,24,128]{4,3,2,1,0:T(8,128)(2,1)S(1)}, bf16[2,2,2,24,128]{4,3,2,1,0:T(8,128)(2,1)S(1)}, u32[]{:S(2)}, u32[]{:S(2)}) collective-permute-start(bf16[2,2,2,24,128]{4,3,2,1,0:T(8,128)(2,1)S(1)} %get-tuple-element.38), channel_id=1, source_target_pairs={{0,14},{1,15},{2,12},{3,13},{4,10},{5,11},{6,8},{7,9},{8,6},{9,7},... | collective-permute-start | bytes 147464 | tf_op jit(solution)/shard_map/ppermute | solution.py:366
  60.5 0.7 collective-permute-start.14
  61.2 3.3 %fourier_0.1.refs_17_ = f32[2,256,1344]{2,1,0:T(8,128)S(1)} custom-call(bf16[16,2,2,2,16,128]{5,4,3,2,1,0:T(8,128)(2,1)S(1)} %all-to-all-done.1.refs_0_, bf16[2,2,640,1344]{3,2,1,0:T(8,128)(2,1)} %tables.1.refs_1_.refs_16_), custom_call_target="tpu_custom_call" | custom-call | flops 704643072 | bytes 2752512 | tf_op jit(solution)/shard_map/fourier_0/pallas_call | solution.py:317
  64.5 2.6 %collective-permute-done.14.refs_15_ = bf16[2,2,2,24,128]{4,3,2,1,0:T(8,128)(2,1)S(1)} collective-permute-done((bf16[2,2,2,24,128]{4,3,2,1,0:T(8,128)(2,1)S(1)}, bf16[2,2,2,24,128]{4,3,2,1,0:T(8,128)(2,1)S(1)}, u32[]{:S(2)}, u32[]{:S(2)}) %collective-permute-start.14) | collective-permute-done | bytes 49184 | tf_op jit(solution)/shard_map/ppermute | solution.py:366
  67.1 4.7 %fourier_256.1 = bf16[256,2688]{1,0:T(8,128)(2,1)} custom-call(bf16[2,2,2,24,128]{4,3,2,1,0:T(8,128)(2,1)S(1)} %get-tuple-element.24.refs_0_, bf16[2,2,2,24,128]{4,3,2,1,0:T(8,128)(2,1)S(1)} %collective-permute-done.refs_1_, bf16[2,2,2,24,128]{4,3,2,1,0:T(8,128)(2,1)S(1)} %collective-permute-done.1.refs_2_, ...), custom_call_target="tpu_custom_call" | custom-call | flops 1056964608 | bytes 4128768 | tf_op jit(solution)/shard_map/fourier_256/pallas_call | solution.py:317
  (27 shorter events, 0.9 us)
Async XLA Ops:
  1.3 13.7 %all-to-all-start = ((s32[16,1,128]{2,1,0:T(1,128)}), s32[16,1,128]{2,1,0:T(1,128)S(1)}, u32[]{:S(2)}, u32[]{:S(2)}) async-start(s32[16,1,128]{2,1,0:T(1,128)} %index.1), calls=%async_computation | async-start | bytes 16384 | tf_op jit(solution)/shard_map/all_to_all | solution.py:354
  16.7 44.5 %all-to-all-start.1 = ((bf16[16,2,2,2,16,128]{5,4,3,2,1,0:T(8,128)(2,1)}), bf16[16,2,2,2,16,128]{5,4,3,2,1,0:T(8,128)(2,1)S(1)}, u32[]{:S(2)}, u32[]{:S(2)}) async-start(bf16[16,2,2,2,16,128]{5,4,3,2,1,0:T(8,128)(2,1)} %bitcast.4), calls=%async_computation.1 | async-start | bytes 1048576 | tf_op jit(solution)/shard_map/all_to_all | solution.py:362
  30.4 4.2 %collective-permute-start = (bf16[2,2,2,24,128]{4,3,2,1,0:T(8,128)(2,1)S(1)}, bf16[2,2,2,24,128]{4,3,2,1,0:T(8,128)(2,1)S(1)}, u32[]{:S(2)}, u32[]{:S(2)}) collective-permute-start(bf16[2,2,2,24,128]{4,3,2,1,0:T(8,128)(2,1)S(1)} %get-tuple-element.25), channel_id=1, source_target_pairs={{0,1},{1,0},{2,3},{3,2},{4,5},{5,4},{6,7},{7,6},{8,9},{9,8},{10,11... | collective-permute-start | bytes 147464 | tf_op jit(solution)/shard_map/ppermute | solution.py:366
  30.9 6.4 %collective-permute-start.1 = (bf16[2,2,2,24,128]{4,3,2,1,0:T(8,128)(2,1)S(1)}, bf16[2,2,2,24,128]{4,3,2,1,0:T(8,128)(2,1)S(1)}, u32[]{:S(2)}, u32[]{:S(2)}) collective-permute-start(bf16[2,2,2,24,128]{4,3,2,1,0:T(8,128)(2,1)S(1)} %get-tuple-element.26), channel_id=1, source_target_pairs={{0,2},{1,3},{2,0},{3,1},{4,6},{5,7},{6,4},{7,5},{8,10},{9,11},{10,... | collective-permute-start | bytes 147464 | tf_op jit(solution)/shard_map/ppermute | solution.py:366
  32.6 4.9 %collective-permute-start.2 = (bf16[2,2,2,24,128]{4,3,2,1,0:T(8,128)(2,1)S(1)}, bf16[2,2,2,24,128]{4,3,2,1,0:T(8,128)(2,1)S(1)}, u32[]{:S(2)}, u32[]{:S(2)}) collective-permute-start(bf16[2,2,2,24,128]{4,3,2,1,0:T(8,128)(2,1)S(1)} %get-tuple-element.27), channel_id=1, source_target_pairs={{0,3},{1,2},{2,1},{3,0},{4,7},{5,6},{6,5},{7,4},{8,11},{9,10},{10,... | collective-permute-start | bytes 147464 | tf_op jit(solution)/shard_map/ppermute | solution.py:366
  32.6 7.4 %collective-permute-start.3 = (bf16[2,2,2,24,128]{4,3,2,1,0:T(8,128)(2,1)S(1)}, bf16[2,2,2,24,128]{4,3,2,1,0:T(8,128)(2,1)S(1)}, u32[]{:S(2)}, u32[]{:S(2)}) collective-permute-start(bf16[2,2,2,24,128]{4,3,2,1,0:T(8,128)(2,1)S(1)} %get-tuple-element.28), channel_id=1, source_target_pairs={{0,4},{1,5},{2,6},{3,7},{4,0},{5,1},{6,2},{7,3},{8,12},{9,13},{10,... | collective-permute-start | bytes 147464 | tf_op jit(solution)/shard_map/ppermute | solution.py:366
  34.3 6.7 %collective-permute-start.4 = (bf16[2,2,2,24,128]{4,3,2,1,0:T(8,128)(2,1)S(1)}, bf16[2,2,2,24,128]{4,3,2,1,0:T(8,128)(2,1)S(1)}, u32[]{:S(2)}, u32[]{:S(2)}) collective-permute-start(bf16[2,2,2,24,128]{4,3,2,1,0:T(8,128)(2,1)S(1)} %get-tuple-element.29), channel_id=1, source_target_pairs={{0,5},{1,4},{2,7},{3,6},{4,1},{5,0},{6,3},{7,2},{8,13},{9,12},{10,... | collective-permute-start | bytes 147464 | tf_op jit(solution)/shard_map/ppermute | solution.py:366
  34.7 17.8 %collective-permute-start.5 = (bf16[2,2,2,24,128]{4,3,2,1,0:T(8,128)(2,1)S(1)}, bf16[2,2,2,24,128]{4,3,2,1,0:T(8,128)(2,1)S(1)}, u32[]{:S(2)}, u32[]{:S(2)}) collective-permute-start(bf16[2,2,2,24,128]{4,3,2,1,0:T(8,128)(2,1)S(1)} %get-tuple-element.30), channel_id=1, source_target_pairs={{0,6},{1,7},{2,4},{3,5},{4,2},{5,3},{6,0},{7,1},{8,14},{9,15},{10,... | collective-permute-start | bytes 147464 | tf_op jit(solution)/shard_map/ppermute | solution.py:366
  37.3 15.8 %collective-permute-start.6 = (bf16[2,2,2,24,128]{4,3,2,1,0:T(8,128)(2,1)S(1)}, bf16[2,2,2,24,128]{4,3,2,1,0:T(8,128)(2,1)S(1)}, u32[]{:S(2)}, u32[]{:S(2)}) collective-permute-start(bf16[2,2,2,24,128]{4,3,2,1,0:T(8,128)(2,1)S(1)} %get-tuple-element.31), channel_id=1, source_target_pairs={{0,7},{1,6},{2,5},{3,4},{4,3},{5,2},{6,1},{7,0},{8,15},{9,14},{10,... | collective-permute-start | bytes 147464 | tf_op jit(solution)/shard_map/ppermute | solution.py:366
  37.5 18.5 %collective-permute-start.7 = (bf16[2,2,2,24,128]{4,3,2,1,0:T(8,128)(2,1)S(1)}, bf16[2,2,2,24,128]{4,3,2,1,0:T(8,128)(2,1)S(1)}, u32[]{:S(2)}, u32[]{:S(2)}) collective-permute-start(bf16[2,2,2,24,128]{4,3,2,1,0:T(8,128)(2,1)S(1)} %get-tuple-element.32), channel_id=1, source_target_pairs={{0,8},{1,9},{2,10},{3,11},{4,12},{5,13},{6,14},{7,15},{8,0},{9,1},... | collective-permute-start | bytes 147464 | tf_op jit(solution)/shard_map/ppermute | solution.py:366
  39.9 17.1 %collective-permute-start.8 = (bf16[2,2,2,24,128]{4,3,2,1,0:T(8,128)(2,1)S(1)}, bf16[2,2,2,24,128]{4,3,2,1,0:T(8,128)(2,1)S(1)}, u32[]{:S(2)}, u32[]{:S(2)}) collective-permute-start(bf16[2,2,2,24,128]{4,3,2,1,0:T(8,128)(2,1)S(1)} %get-tuple-element.33), channel_id=1, source_target_pairs={{0,9},{1,8},{2,11},{3,10},{4,13},{5,12},{6,15},{7,14},{8,1},{9,0},... | collective-permute-start | bytes 147464 | tf_op jit(solution)/shard_map/ppermute | solution.py:366
  40.9 19.6 %collective-permute-start.9 = (bf16[2,2,2,24,128]{4,3,2,1,0:T(8,128)(2,1)S(1)}, bf16[2,2,2,24,128]{4,3,2,1,0:T(8,128)(2,1)S(1)}, u32[]{:S(2)}, u32[]{:S(2)}) collective-permute-start(bf16[2,2,2,24,128]{4,3,2,1,0:T(8,128)(2,1)S(1)} %get-tuple-element.34), channel_id=1, source_target_pairs={{0,10},{1,11},{2,8},{3,9},{4,14},{5,15},{6,12},{7,13},{8,2},{9,3},... | collective-permute-start | bytes 147464 | tf_op jit(solution)/shard_map/ppermute | solution.py:366
  52.5 12.0 %collective-permute-start.10 = (bf16[2,2,2,24,128]{4,3,2,1,0:T(8,128)(2,1)S(1)}, bf16[2,2,2,24,128]{4,3,2,1,0:T(8,128)(2,1)S(1)}, u32[]{:S(2)}, u32[]{:S(2)}) collective-permute-start(bf16[2,2,2,24,128]{4,3,2,1,0:T(8,128)(2,1)S(1)} %get-tuple-element.35), channel_id=1, source_target_pairs={{0,11},{1,10},{2,9},{3,8},{4,15},{5,14},{6,13},{7,12},{8,3},{9,2},... | collective-permute-start | bytes 147464 | tf_op jit(solution)/shard_map/ppermute | solution.py:366
  53.2 11.3 %collective-permute-start.11 = (bf16[2,2,2,24,128]{4,3,2,1,0:T(8,128)(2,1)S(1)}, bf16[2,2,2,24,128]{4,3,2,1,0:T(8,128)(2,1)S(1)}, u32[]{:S(2)}, u32[]{:S(2)}) collective-permute-start(bf16[2,2,2,24,128]{4,3,2,1,0:T(8,128)(2,1)S(1)} %get-tuple-element.36), channel_id=1, source_target_pairs={{0,12},{1,13},{2,14},{3,15},{4,8},{5,9},{6,10},{7,11},{8,4},{9,5},... | collective-permute-start | bytes 147464 | tf_op jit(solution)/shard_map/ppermute | solution.py:366
  56.0 8.5 %collective-permute-start.12 = (bf16[2,2,2,24,128]{4,3,2,1,0:T(8,128)(2,1)S(1)}, bf16[2,2,2,24,128]{4,3,2,1,0:T(8,128)(2,1)S(1)}, u32[]{:S(2)}, u32[]{:S(2)}) collective-permute-start(bf16[2,2,2,24,128]{4,3,2,1,0:T(8,128)(2,1)S(1)} %get-tuple-element.37), channel_id=1, source_target_pairs={{0,13},{1,12},{2,15},{3,14},{4,9},{5,8},{6,11},{7,10},{8,5},{9,4},... | collective-permute-start | bytes 147464 | tf_op jit(solution)/shard_map/ppermute | solution.py:366
  57.0 7.5 %collective-permute-start.13 = (bf16[2,2,2,24,128]{4,3,2,1,0:T(8,128)(2,1)S(1)}, bf16[2,2,2,24,128]{4,3,2,1,0:T(8,128)(2,1)S(1)}, u32[]{:S(2)}, u32[]{:S(2)}) collective-permute-start(bf16[2,2,2,24,128]{4,3,2,1,0:T(8,128)(2,1)S(1)} %get-tuple-element.38), channel_id=1, source_target_pairs={{0,14},{1,15},{2,12},{3,13},{4,10},{5,11},{6,8},{7,9},{8,6},{9,7},... | collective-permute-start | bytes 147464 | tf_op jit(solution)/shard_map/ppermute | solution.py:366
  60.5 6.6 %collective-permute-start.14 = (bf16[2,2,2,24,128]{4,3,2,1,0:T(8,128)(2,1)S(1)}, bf16[2,2,2,24,128]{4,3,2,1,0:T(8,128)(2,1)S(1)}, u32[]{:S(2)}, u32[]{:S(2)}) collective-permute-start(bf16[2,2,2,24,128]{4,3,2,1,0:T(8,128)(2,1)S(1)} %get-tuple-element.39), channel_id=1, source_target_pairs={{0,15},{1,14},{2,13},{3,12},{4,11},{5,10},{6,9},{7,8},{8,7},{9,6},... | collective-permute-start | bytes 147464 | tf_op jit(solution)/shard_map/ppermute | solution.py:366

commit v5 on v3

v5 whole, which is shorter than its diff:
```python
import functools
import math

import jax
import jax.numpy as jnp
from jax import lax
from jax.experimental import pallas as pl
from jax.experimental.pallas import tpu as pltpu
from jax.sharding import PartitionSpec as P

M = 1280
NLON = 2688
HALF = NLON // 2
ROWS = 8
LANES = 128


def round_up(value, unit):
    return -(-value // unit) * unit


def legendre_kernel(
    waves_hbm, se_hbm, so_hbm, le_hbm, lo_hbm, out_ref,
    waves_ref, se_ref, so_ref, le_ref, lo_ref, columns_ref, anti_ref, sems, wave_sem,
):
    pairs, lats, he = le_ref.shape
    ho = lo_ref.shape[2]
    groups = pairs // ROWS

    def odd_copies(g):
        at = pl.ds(pl.multiple_of(g * ROWS, ROWS), ROWS)
        return (
            pltpu.make_async_copy(lo_hbm.at[at], lo_ref.at[at], sems.at[0, g]),
            pltpu.make_async_copy(so_hbm.at[at], so_ref.at[at], sems.at[1, g]),
        )

    def even_copies(g):
        at = pl.ds(pl.multiple_of(g * ROWS, ROWS), ROWS)
        return (
            pltpu.make_async_copy(le_hbm.at[at], le_ref.at[at], sems.at[2, g]),
            pltpu.make_async_copy(se_hbm.at[:, at], se_ref.at[g], sems.at[3, g]),
        )

    wave_copy = pltpu.make_async_copy(waves_hbm, waves_ref, wave_sem)
    wave_copy.start()
    for g in range(groups):
        for copy in odd_copies(g) + even_copies(g):
            copy.start()
    wave_copy.wait()

    ids_e = lax.broadcasted_iota(jnp.int32, (lats, he), 1)
    ids_o = lax.broadcasted_iota(jnp.int32, (lats, ho), 1)

    def split(panel, ids, count):
        in_low = ids < count
        zero = jnp.zeros_like(panel)
        lower = jnp.where(in_low, panel, zero)
        upper = jnp.where(in_low, zero, panel)
        return jnp.concatenate([lower, upper], axis=0)

    @pl.loop(0, groups)
    def _(g):
        base = pl.multiple_of(g * ROWS, ROWS)
        for copy in odd_copies(g):
            copy.wait()
        for p in range(ROWS):
            odd = split(lo_ref[base + p], ids_o, (M - waves_ref[base + p]) // 2)
            anti_ref[p] = jnp.dot(odd, so_ref[base + p], preferred_element_type=jnp.float32)
        for copy in even_copies(g):
            copy.wait()
        columns_ref[...] = se_ref[g].astype(jnp.float32).reshape(columns_ref.shape)
        for p in range(ROWS):
            low = waves_ref[base + p]
            parity = low % 2
            even = split(le_ref[base + p], ids_e, (M - low + 1) // 2)
            xe = columns_ref[pl.ds(p, he, stride=ROWS), :].astype(jnp.bfloat16)
            sym = jnp.dot(even, xe, preferred_element_type=jnp.float32)
            anti = anti_ref[p]
            for h, rows in enumerate((sym + anti, sym - anti)):
                for w in range(2):
                    start = (parity ^ w) * (lats * pairs) + base + p
                    out_ref[h, pl.ds(start, lats, stride=pairs), :] = rows[w * lats : (w + 1) * lats]


def in_hbm(x):
    return pltpu.with_memory_space_constraint(x, pltpu.HBM)


def in_vmem(x):
    return pltpu.with_memory_space_constraint(x, pltpu.VMEM)


def legendre_stage(waves, spectra_even, spectra_odd, legendre_even, legendre_odd):
    pairs, he, width = spectra_even.shape
    ho = spectra_odd.shape[1]
    lats = legendre_even.shape[1]
    by_column = jnp.transpose(spectra_even, (1, 0, 2))
    operands = (waves, by_column, spectra_odd, legendre_even, legendre_odd)
    return pl.pallas_call(
        legendre_kernel,
        out_shape=pltpu.VMEM((2, 2 * lats * pairs, width), jnp.float32),
        in_specs=[pl.BlockSpec(memory_space=pl.ANY)] * 5,
        out_specs=pl.BlockSpec(memory_space=pltpu.VMEM),
        scratch_shapes=[
            pltpu.SMEM((pairs,), jnp.int32),
            pltpu.VMEM((pairs // ROWS, he, ROWS, width), jnp.bfloat16),
            pltpu.VMEM((pairs, ho, width), jnp.bfloat16),
            pltpu.VMEM((pairs, lats, he), jnp.bfloat16),
            pltpu.VMEM((pairs, lats, ho), jnp.bfloat16),
            pltpu.VMEM((he * ROWS, width), jnp.float32),
            pltpu.VMEM((ROWS, 2 * lats, width), jnp.float32),
            pltpu.SemaphoreType.DMA((4, pairs // ROWS)),
            pltpu.SemaphoreType.DMA,
        ],
        compiler_params=pltpu.CompilerParams(vmem_limit_bytes=40 * 1024 * 1024),
        cost_estimate=pl.CostEstimate(
            flops=4 * pairs * lats * 2 * (he + ho) * width,
            bytes_accessed=2 * pairs * (he + ho) * (width + lats),
            transcendentals=0,
        ),
        name="legendre",
    )(*(in_hbm(x) for x in operands))


def pick_kernel(bands_ref, rows_ref, out_ref):
    lats, _, _, pairs, _ = out_ref.shape

    def emit(slot, carry):
        band = bands_ref[slot]
        for h in range(2):
            for w in range(2):
                start = pl.multiple_of((w * lats + band) * pairs, ROWS)
                out_ref[slot, h, w] = rows_ref[h, pl.ds(start, pairs), :].astype(jnp.bfloat16)
        return carry

    lax.fori_loop(0, lats, emit, 0, unroll=8)


def pick_latitudes(bands, rows, pairs):
    lats = bands.shape[0]
    width = rows.shape[2]
    return pl.pallas_call(
        pick_kernel,
        out_shape=jax.ShapeDtypeStruct((lats, 2, 2, pairs, width), jnp.bfloat16),
        grid_spec=pltpu.PrefetchScalarGridSpec(
            num_scalar_prefetch=1,
            grid=(),
            in_specs=[pl.BlockSpec(memory_space=pltpu.VMEM)],
            out_specs=pl.BlockSpec(memory_space=pltpu.VMEM),
        ),
        compiler_params=pltpu.CompilerParams(vmem_limit_bytes=16 * 1024 * 1024),
        name=f"pick_{pairs}",
    )(bands, in_vmem(rows))


def table_kernel(waves_ref, out_ref):
    low = waves_ref[...]
    even = jnp.where(low % 2 == 0, low, M - 1 - low)
    odd = M - 1 - even
    lane = lax.broadcasted_iota(jnp.int32, low.shape, 1).astype(jnp.float32)
    unit = 2.0 * math.pi / NLON

    def angle(product):
        turns = jnp.floor(product * (1.0 / NLON))
        return (product - turns * NLON) * unit

    for w, wave in enumerate((even, odd)):
        number = wave.astype(jnp.float32)
        factor = jnp.where(wave == 0, 1.0, 2.0)
        start = angle(number * lane)
        step = angle(number * LANES)
        c, s = factor * jnp.cos(start), -factor * jnp.sin(start)
        dc, ds = jnp.cos(step), jnp.sin(step)
        for b in range(0, HALF, LANES):
            size = min(LANES, HALF - b)
            out_ref[w, 0, :, b : b + size] = c[:, :size].astype(jnp.bfloat16)
            out_ref[w, 1, :, b : b + size] = s[:, :size].astype(jnp.bfloat16)
            c, s = c * dc + s * ds, s * dc - c * ds


def wave_tables(waves):
    total = waves.shape[0]
    rows = 64
    return pl.pallas_call(
        table_kernel,
        out_shape=pltpu.HBM((2, 2, total, HALF), jnp.bfloat16),
        grid=(total // rows,),
        in_specs=[pl.BlockSpec((rows, LANES), lambda i: (i, 0))],
        out_specs=pl.BlockSpec((2, 2, rows, HALF), lambda i: (0, 0, i, 0)),
        compiler_params=pltpu.CompilerParams(vmem_limit_bytes=32 * 1024 * 1024),
        cost_estimate=pl.CostEstimate(
            flops=4 * 4 * total * HALF, bytes_accessed=8 * total * HALF, transcendentals=8 * total * LANES
        ),
        name="tables",
    )(jnp.broadcast_to(waves[:, None], (total, LANES)))


def fourier_kernel(arrived_ref, table_hbm, out_hbm, left_ref, table_ref, row_ref, sems, out_sems):
    devices, slots, _, _, pairs, width = arrived_ref.shape
    fields = width // 2
    total = devices * pairs
    chunk = 256
    ends = list(range(0, HALF, chunk)) + [HALF]
    spans = list(zip(ends[:-1], ends[1:]))

    def load(i):
        at = slice(*spans[i])
        return pltpu.make_async_copy(table_hbm.at[:, :, :, at], table_ref.at[:, :, :, at], sems.at[i])

    for i in range(len(spans)):
        load(i).start()

    for w in range(2):
        for s in range(slots):
            for h in range(2):
                x = jnp.concatenate([arrived_ref[d, s, h, w] for d in range(devices)], axis=0)
                xt = x.T
                r = (s * 2 + h) * fields
                left_ref[w, r : r + fields, :total] = xt[:fields]
                left_ref[w, r : r + fields, total:] = xt[fields:]

    stores = []
    sent = [0, round_up(HALF, LANES)]
    for i, (lo, hi) in enumerate(spans):
        load(i).wait()
        e, o = [
            jnp.dot(
                left_ref[w],
                jnp.concatenate([table_ref[w, 0, :, lo:hi], table_ref[w, 1, :, lo:hi]], axis=0),
                preferred_element_type=jnp.float32,
            )
            for w in range(2)
        ]
        row_ref[:, lo:hi] = (e + o).astype(jnp.bfloat16)
        row_ref[:, HALF + lo : HALF + hi] = (e - o).astype(jnp.bfloat16)
        done = hi == HALF
        reach = (round_up(HALF, LANES) if done else hi, NLON if done else (HALF + hi) // LANES * LANES)
        for part in range(2):
            at = slice(sent[part], reach[part])
            copy = pltpu.make_async_copy(row_ref.at[:, at], out_hbm.at[:, at], out_sems.at[part, i])
            copy.start()
            stores.append(copy)
            sent[part] = reach[part]
    for copy in stores:
        copy.wait()


def fourier_stage(arrived, table):
    devices, slots, _, _, pairs, width = arrived.shape
    fields = width // 2
    total = devices * pairs
    rows = slots * 2 * fields
    spans = pl.cdiv(HALF, 256)
    out = pl.pallas_call(
        fourier_kernel,
        out_shape=jax.ShapeDtypeStruct((rows, NLON), jnp.bfloat16),
        in_specs=[pl.BlockSpec(memory_space=pltpu.VMEM), pl.BlockSpec(memory_space=pl.ANY)],
        out_specs=pl.BlockSpec(memory_space=pl.ANY),
        scratch_shapes=[
            pltpu.VMEM((2, rows, 2 * total), jnp.bfloat16),
            pltpu.VMEM((2, 2, total, HALF), jnp.bfloat16),
            pltpu.VMEM((rows, NLON), jnp.bfloat16),
            pltpu.SemaphoreType.DMA((spans,)),
            pltpu.SemaphoreType.DMA((2, spans)),
        ],
        compiler_params=pltpu.CompilerParams(vmem_limit_bytes=40 * 1024 * 1024),
        cost_estimate=pl.CostEstimate(
            flops=8 * rows * total * HALF, bytes_accessed=8 * total * HALF, transcendentals=0
        ),
        name="fourier",
    )(in_vmem(arrived), in_hbm(table))
    return out.reshape(slots, 2, fields, NLON)


def on_device(wave_pairs, band_owner, spectra_even, spectra_odd, legendre_even, legendre_odd):
    devices = lax.axis_size("wave")
    pairs = round_up(wave_pairs.shape[0], ROWS)
    extra = pairs - wave_pairs.shape[0]
    slots = band_owner.shape[0]
    width = spectra_even.shape[2]
    if extra:
        wave_pairs = jnp.pad(wave_pairs, (0, extra))
        spectra_even, spectra_odd, legendre_even, legendre_odd = (
            jnp.pad(a, ((0, extra), (0, 0), (0, 0)))
            for a in (spectra_even, spectra_odd, legendre_even, legendre_odd)
        )

    own = jnp.pad(jnp.concatenate([wave_pairs, band_owner]), (0, round_up(pairs + slots, LANES) - pairs - slots))
    block = lax.optimization_barrier(jnp.broadcast_to(own, (32,) + own.shape))
    index = lax.optimization_barrier(lax.all_gather(block, "wave", axis=0))[:, 0]
    all_pairs = index[:, :pairs].reshape(-1)
    all_bands = index[:, pairs : pairs + slots].reshape(-1)

    rows = legendre_stage(wave_pairs, spectra_even, spectra_odd, legendre_even, legendre_odd)
    picked = pick_latitudes(all_bands, rows, pairs).reshape(devices, slots, 2, 2, pairs, width)
    arrived = lax.all_to_all(picked, "wave", 0, 0, tiled=True)
    return fourier_stage(arrived, wave_tables(all_pairs))


def solution(mesh):
    return jax.shard_map(
        on_device,
        mesh=mesh,
        in_specs=(
            P("wave"),
            P("wave"),
            P("wave", None, "grp"),
            P("wave", None, "grp"),
            P("wave", None, None),
            P("wave", None, None),
        ),
        out_specs=P("wave", None, "grp", None),
        check_vma=False,
    )
```

time: 65.5 us -> 74 us (1.13)
  blocking collectives: 0 us -> 16.3 us
  Pallas kernels: 34 us -> 24.4 us
  waiting for transfers between devices: 12.5 us -> 21.6 us
  starting transfers between devices: 17.6 us -> 10.2 us
  other arithmetic: 0.01 us -> 0.75 us
    all_gather x0 -> x1, blocking collectives: none -> 16.3 us  [on_device(): lax.all_gather(block, 'wave', axis=0)]
    all_to_all x3 -> x1, waiting for transfers between devices: 12.5 us -> 21.6 us  [on_device(): arrived = lax.all_to_all(picked, 'wave', 0, 0, tiled=True)]
    pallas_call x5 -> x2, Pallas kernels: 22.3 us -> 13.9 us  [the longest x1 8.35 us: legendre_stage(): pl.pallas_call(legendre_kernel, out_shape=pltpu.VMEM((2, 2 * lats * pairs...]
    all_to_all x3 -> x1, starting transfers between devices: 17.6 us -> 10.2 us  [on_device(): arrived = lax.all_to_all(picked, 'wave', 0, 0, tiled=True)]
    pallas_call x2 -> x1, Pallas kernels: 2.95 us -> 1.76 us  [pick_latitudes(): pl.pallas_call(pick_kernel, out_shape=jax.ShapeDtypeStruct((lats, 2, 2, p...]
  transfers between devices with their start and end apart: 3 -> 1, of which waited for: 2 -> 1; matrix products, arithmetic and copies ran while one was open for 1% -> 0% of each run, Pallas kernels for 39% -> 12%
where the time goes in v5:
time: 74 us; the launch traced here: 73.8 us
  Pallas kernels  24.4 us (33%)
  waiting for transfers between devices  21.6 us (29%)
  blocking collectives  16.3 us (22%)
  starting transfers between devices  10.2 us (14%)
  other arithmetic  0.75 us (1%)
    all_to_all x1, waiting for transfers between devices, on_device(): arrived = lax.all_to_all(picked, 'wave', 0, 0, tiled=True)  21.6 us
    all_gather x1, blocking collectives, on_device(): lax.all_gather(block, 'wave', axis=0)  16.3 us
    all_to_all x1, starting transfers between devices, on_device(): arrived = lax.all_to_all(picked, 'wave', 0, 0, tiled=True)  10.2 us
    pallas_call x1, Pallas kernels, wave_tables(): pl.pallas_call(table_kernel, out_shape=pltpu.HBM((2, 2, total, HALF), jnp...  8.72 us
    pallas_call x1, Pallas kernels, legendre_stage(): pl.pallas_call(legendre_kernel, out_shape=pltpu.VMEM((2, 2 * lats * pairs...  8.35 us
    pallas_call x1, Pallas kernels, fourier_stage(): pl.pallas_call(fourier_kernel, out_shape=jax.ShapeDtypeStruct((rows, NLON...  5.59 us
    pallas_call x1, Pallas kernels, pick_latitudes(): pl.pallas_call(pick_kernel, out_shape=jax.ShapeDtypeStruct((lats, 2, 2, p...  1.76 us
  transfers between devices with their start and end apart: 1, of which 1 were waited for; matrix products, arithmetic and copies ran while one was open for 0% of the time, Pallas kernels for 12%

profile of v5, /device:TPU:13, one launch (start us, length us, event | category | flops | bytes accessed | tf_op | source)
XLA Modules:
  0.0 73.8 jit_solution(870413543916739693)
XLA Ops:
  0.0 0.7 %pad_add_fusion = s32[42]{0:T(128)S(1)} fusion(s32[2]{0:T(128)} %param.7, s32[40]{0:T(128)} %waves_hbm.1), kind=kLoop, calls=%fused_computation | loop fusion | flops 42 | bytes 336 | tf_op jit(solution)/shard_map/concatenate | solution.py:288
  0.8 16.3 %all-gather = s32[512,128]{1,0:T(8,128)S(1)} all-gather(s32[32,128]{1,0:T(8,128)S(1)} %broadcast_in_dim.10), channel_id=2, replica_groups=mesh['grp'=2,'wave'=16] {'wave'}, dimensions={0}, use_global_device_ids=true | all-gather | bytes 278528 | tf_op jit(solution)/shard_map/all_gather | solution.py:290
  17.1 0.1 slice.13
  17.2 0.1 reshape.10.bands_ref
  17.3 8.3 %legendre.1.rows_ref = f32[2,2560,128]{2,1,0:T(8,128)S(1)} custom-call(s32[40]{0:T(128)} %waves_hbm.1, bf16[641,40,128]{2,1,0:T(8,128)(2,1)} %bitcast.6, bf16[40,640,128]{2,1,0:T(8,128)(2,1)} %so_hbm.1, bf16[40,32,641]{2,1,0:T(8,128)(2,1)} %le_hbm.1, bf16[40,32,640]{2,1,0:T(8,128)(2,1)} %lo_hbm.1), custom_call_target="tpu_custom_call" | custom-call | flops 1679032320 | bytes 16396800 | tf_op jit(solution)/shard_map/legendre/pallas_call | solution.py:99
  25.6 1.8 %pick_40.1 = bf16[32,2,2,40,128]{4,3,2,1,0:T(8,128)(2,1)} custom-call(s32[32]{0:T(128)S(1)} %reshape.10.bands_ref, f32[2,2560,128]{2,1,0:T(8,128)S(1)} %legendre.1.rows_ref), custom_call_target="tpu_custom_call" | custom-call | tf_op jit(solution)/shard_map/pick_40/pallas_call | solution.py:142
  27.4 10.2 %all-to-all-start = ((bf16[16,2,2,2,40,128]{5,4,3,2,1,0:T(8,128)(2,1)}), bf16[16,2,2,2,40,128]{5,4,3,2,1,0:T(8,128)(2,1)S(1)}, u32[]{:S(2)}, u32[]{:S(2)}) async-start(bf16[16,2,2,2,40,128]{5,4,3,2,1,0:T(8,128)(2,1)} %bitcast.3), calls=%async_computation | async-start | bytes 2621440 | tf_op jit(solution)/shard_map/all_to_all | solution.py:296
  37.6 0.1 broadcast_in_dim.11
  37.7 0.1 broadcast_in_dim.12.waves_ref
  37.9 8.7 %tables.1.table_hbm = bf16[2,2,640,1344]{3,2,1,0:T(8,128)(2,1)} custom-call(s32[640,128]{1,0:T(8,128)S(1)} %broadcast_in_dim.12.waves_ref), custom_call_target="tpu_custom_call" | custom-call | flops 13762560 | bytes 6881280 | tf_op jit(solution)/shard_map/tables/pallas_call | solution.py:184
  46.6 21.6 %all-to-all-done.arrived_ref = bf16[16,2,2,2,40,128]{5,4,3,2,1,0:T(8,128)(2,1)S(1)} async-done(((bf16[16,2,2,2,40,128]{5,4,3,2,1,0:T(8,128)(2,1)}), bf16[16,2,2,2,40,128]{5,4,3,2,1,0:T(8,128)(2,1)S(1)}, u32[]{:S(2)}, u32[]{:S(2)}) %all-to-all-start) | async-done | bytes 1310752 | tf_op jit(solution)/shard_map/all_to_all | solution.py:296
  68.2 5.6 %fourier.1 = bf16[256,2688]{1,0:T(8,128)(2,1)} custom-call(bf16[16,2,2,2,40,128]{5,4,3,2,1,0:T(8,128)(2,1)S(1)} %all-to-all-done.arrived_ref, bf16[2,2,640,1344]{3,2,1,0:T(8,128)(2,1)} %tables.1.table_hbm), custom_call_target="tpu_custom_call" | custom-call | flops 1761607680 | bytes 6881280 | tf_op jit(solution)/shard_map/fourier/pallas_call | solution.py:254
  (3 shorter events, 0.0 us)
Async XLA Ops:
  27.4 40.8 %all-to-all-start = ((bf16[16,2,2,2,40,128]{5,4,3,2,1,0:T(8,128)(2,1)}), bf16[16,2,2,2,40,128]{5,4,3,2,1,0:T(8,128)(2,1)S(1)}, u32[]{:S(2)}, u32[]{:S(2)}) async-start(bf16[16,2,2,2,40,128]{5,4,3,2,1,0:T(8,128)(2,1)} %bitcast.3), calls=%async_computation | async-start | bytes 2621440 | tf_op jit(solution)/shard_map/all_to_all | solution.py:296

commit v6 on v5

--- a/solution.py
+++ b/solution.py
@@ -122,8 +122,11 @@
     )(*(in_hbm(x) for x in operands))
 
 
-def pick_kernel(bands_ref, rows_ref, out_ref):
+def pick_kernel(bands_ref, rows_ref, out_hbm, out_ref, sems):
     lats, _, _, pairs, _ = out_ref.shape
+
+    def store(slot):
+        return pltpu.make_async_copy(out_ref.at[slot], out_hbm.at[slot], sems.at[slot])
 
     def emit(slot, carry):
         band = bands_ref[slot]
@@ -131,63 +134,73 @@
             for w in range(2):
                 start = pl.multiple_of((w * lats + band) * pairs, ROWS)
                 out_ref[slot, h, w] = rows_ref[h, pl.ds(start, pairs), :].astype(jnp.bfloat16)
+        store(slot).start()
         return carry
 
-    lax.fori_loop(0, lats, emit, 0, unroll=8)
+    def finish(slot, carry):
+        store(slot).wait()
+        return carry
+
+    lax.fori_loop(0, lats, emit, 0, unroll=4)
+    lax.fori_loop(0, lats, finish, 0)
 
 
 def pick_latitudes(bands, rows, pairs):
     lats = bands.shape[0]
     width = rows.shape[2]
+    shape = (lats, 2, 2, pairs, width)
     return pl.pallas_call(
         pick_kernel,
-        out_shape=jax.ShapeDtypeStruct((lats, 2, 2, pairs, width), jnp.bfloat16),
+        out_shape=jax.ShapeDtypeStruct(shape, jnp.bfloat16),
         grid_spec=pltpu.PrefetchScalarGridSpec(
             num_scalar_prefetch=1,
             grid=(),
             in_specs=[pl.BlockSpec(memory_space=pltpu.VMEM)],
-            out_specs=pl.BlockSpec(memory_space=pltpu.VMEM),
+            out_specs=pl.BlockSpec(memory_space=pl.ANY),
+            scratch_shapes=[pltpu.VMEM(shape, jnp.bfloat16), pltpu.SemaphoreType.DMA((lats,))],
         ),
         compiler_params=pltpu.CompilerParams(vmem_limit_bytes=16 * 1024 * 1024),
-        name=f"pick_{pairs}",
+        name="pick",
     )(bands, in_vmem(rows))
 
 
 def table_kernel(waves_ref, out_ref):
-    low = waves_ref[...]
-    even = jnp.where(low % 2 == 0, low, M - 1 - low)
-    odd = M - 1 - even
-    lane = lax.broadcasted_iota(jnp.int32, low.shape, 1).astype(jnp.float32)
     unit = 2.0 * math.pi / NLON
+    block = 64
 
     def angle(product):
         turns = jnp.floor(product * (1.0 / NLON))
         return (product - turns * NLON) * unit
 
-    for w, wave in enumerate((even, odd)):
-        number = wave.astype(jnp.float32)
-        factor = jnp.where(wave == 0, 1.0, 2.0)
-        start = angle(number * lane)
-        step = angle(number * LANES)
-        c, s = factor * jnp.cos(start), -factor * jnp.sin(start)
-        dc, ds = jnp.cos(step), jnp.sin(step)
-        for b in range(0, HALF, LANES):
-            size = min(LANES, HALF - b)
-            out_ref[w, 0, :, b : b + size] = c[:, :size].astype(jnp.bfloat16)
-            out_ref[w, 1, :, b : b + size] = s[:, :size].astype(jnp.bfloat16)
-            c, s = c * dc + s * ds, s * dc - c * ds
+    @pl.loop(0, waves_ref.shape[0] // block)
+    def _(i):
+        at = pl.ds(pl.multiple_of(i * block, block), block)
+        low = waves_ref[at, :]
+        even = jnp.where(low % 2 == 0, low, M - 1 - low)
+        odd = M - 1 - even
+        lane = lax.broadcasted_iota(jnp.int32, low.shape, 1).astype(jnp.float32)
+        for w, wave in enumerate((even, odd)):
+            number = wave.astype(jnp.float32)
+            factor = jnp.where(wave == 0, 1.0, 2.0)
+            start = angle(number * lane)
+            step = angle(number * LANES)
+            c, s = factor * jnp.cos(start), -factor * jnp.sin(start)
+            dc, ds = jnp.cos(step), jnp.sin(step)
+            for b in range(0, HALF, LANES):
+                size = min(LANES, HALF - b)
+                out_ref[w, 0, at, b : b + size] = c[:, :size].astype(jnp.bfloat16)
+                out_ref[w, 1, at, b : b + size] = s[:, :size].astype(jnp.bfloat16)
+                c, s = c * dc + s * ds, s * dc - c * ds
 
 
 def wave_tables(waves):
     total = waves.shape[0]
-    rows = 64
     return pl.pallas_call(
         table_kernel,
-        out_shape=pltpu.HBM((2, 2, total, HALF), jnp.bfloat16),
-        grid=(total // rows,),
-        in_specs=[pl.BlockSpec((rows, LANES), lambda i: (i, 0))],
-        out_specs=pl.BlockSpec((2, 2, rows, HALF), lambda i: (0, 0, i, 0)),
-        compiler_params=pltpu.CompilerParams(vmem_limit_bytes=32 * 1024 * 1024),
+        out_shape=pltpu.VMEM((2, 2, total, HALF), jnp.bfloat16),
+        in_specs=[pl.BlockSpec(memory_space=pltpu.VMEM)],
+        out_specs=pl.BlockSpec(memory_space=pltpu.VMEM),
+        compiler_params=pltpu.CompilerParams(vmem_limit_bytes=16 * 1024 * 1024),
         cost_estimate=pl.CostEstimate(
             flops=4 * 4 * total * HALF, bytes_accessed=8 * total * HALF, transcendentals=8 * total * LANES
         ),
@@ -195,34 +208,33 @@
     )(jnp.broadcast_to(waves[:, None], (total, LANES)))
 
 
-def fourier_kernel(arrived_ref, table_hbm, out_hbm, left_ref, table_ref, row_ref, sems, out_sems):
+def fourier_kernel(arrived_hbm, table_ref, out_hbm, left_ref, arrived_ref, row_ref, sems, out_sems):
     devices, slots, _, _, pairs, width = arrived_ref.shape
     fields = width // 2
     total = devices * pairs
     chunk = 256
     ends = list(range(0, HALF, chunk)) + [HALF]
     spans = list(zip(ends[:-1], ends[1:]))
+    quarters = [(s, h) for s in range(slots) for h in range(2)]
 
     def load(i):
-        at = slice(*spans[i])
-        return pltpu.make_async_copy(table_hbm.at[:, :, :, at], table_ref.at[:, :, :, at], sems.at[i])
-
-    for i in range(len(spans)):
+        s, h = quarters[i]
+        return pltpu.make_async_copy(arrived_hbm.at[:, s, h], arrived_ref.at[:, s, h], sems.at[i])
+
+    for i in range(len(quarters)):
         load(i).start()
 
-    for w in range(2):
-        for s in range(slots):
-            for h in range(2):
-                x = jnp.concatenate([arrived_ref[d, s, h, w] for d in range(devices)], axis=0)
-                xt = x.T
-                r = (s * 2 + h) * fields
-                left_ref[w, r : r + fields, :total] = xt[:fields]
-                left_ref[w, r : r + fields, total:] = xt[fields:]
+    for i, (s, h) in enumerate(quarters):
+        load(i).wait()
+        for w in range(2):
+            x = jnp.concatenate([arrived_ref[d, s, h, w] for d in range(devices)], axis=0)
+            xt = x.T
+            left_ref[w, i * fields : (i + 1) * fields, :total] = xt[:fields]
+            left_ref[w, i * fields : (i + 1) * fields, total:] = xt[fields:]
 
     stores = []
     sent = [0, round_up(HALF, LANES)]
     for i, (lo, hi) in enumerate(spans):
-        load(i).wait()
         e, o = [
             jnp.dot(
                 left_ref[w],
@@ -254,21 +266,21 @@
     out = pl.pallas_call(
         fourier_kernel,
         out_shape=jax.ShapeDtypeStruct((rows, NLON), jnp.bfloat16),
-        in_specs=[pl.BlockSpec(memory_space=pltpu.VMEM), pl.BlockSpec(memory_space=pl.ANY)],
+        in_specs=[pl.BlockSpec(memory_space=pl.ANY), pl.BlockSpec(memory_space=pltpu.VMEM)],
         out_specs=pl.BlockSpec(memory_space=pl.ANY),
         scratch_shapes=[
             pltpu.VMEM((2, rows, 2 * total), jnp.bfloat16),
-            pltpu.VMEM((2, 2, total, HALF), jnp.bfloat16),
+            pltpu.VMEM(arrived.shape, jnp.bfloat16),
             pltpu.VMEM((rows, NLON), jnp.bfloat16),
-            pltpu.SemaphoreType.DMA((spans,)),
+            pltpu.SemaphoreType.DMA((slots * 2,)),
             pltpu.SemaphoreType.DMA((2, spans)),
         ],
-        compiler_params=pltpu.CompilerParams(vmem_limit_bytes=40 * 1024 * 1024),
+        compiler_params=pltpu.CompilerParams(vmem_limit_bytes=24 * 1024 * 1024),
         cost_estimate=pl.CostEstimate(
             flops=8 * rows * total * HALF, bytes_accessed=8 * total * HALF, transcendentals=0
         ),
         name="fourier",
-    )(in_vmem(arrived), in_hbm(table))
+    )(in_hbm(arrived), in_vmem(table))
     return out.reshape(slots, 2, fields, NLON)
 
 
@@ -285,9 +297,12 @@
             for a in (spectra_even, spectra_odd, legendre_even, legendre_odd)
         )
 
-    own = jnp.pad(jnp.concatenate([wave_pairs, band_owner]), (0, round_up(pairs + slots, LANES) - pairs - slots))
-    block = lax.optimization_barrier(jnp.broadcast_to(own, (32,) + own.shape))
-    index = lax.optimization_barrier(lax.all_gather(block, "wave", axis=0))[:, 0]
+    lanes = round_up(pairs + slots, LANES)
+    entries = [
+        jnp.broadcast_to(x, (devices, 1) + x.shape)
+        for x in (wave_pairs, band_owner, jnp.zeros(lanes - pairs - slots, jnp.int32))
+    ]
+    index = lax.all_to_all(jnp.concatenate(entries, axis=2), "wave", 0, 0, tiled=True)[:, 0]
     all_pairs = index[:, :pairs].reshape(-1)
     all_bands = index[:, pairs : pairs + slots].reshape(-1)
 

time: 74 us -> 66.1 us (0.89)
  blocking collectives: 16.3 us -> 0 us
  local copies, waits for them, and re-layouts: 0.4 us -> 9.11 us
  starting transfers between devices: 10.2 us -> 12.6 us
  Pallas kernels: 24.4 us -> 23 us
  waiting for transfers between devices: 21.6 us -> 20.3 us
    all_gather x1 -> x0, blocking collectives: 16.3 us -> none  [on_device(): lax.all_gather(block, 'wave', axis=0)]
    unnamed x0 -> x8, local copies, waits for them, and re-layouts: none -> 8.12 us
    all_to_all x0 -> x1, starting transfers between devices: none -> 6.55 us  [on_device(): lax.all_to_all(jnp.concatenate(entries, axis=2), 'wave', 0, 0, tiled=True)]
    all_to_all x1, starting transfers between devices: 10.2 us -> 6.02 us  [on_device(): arrived = lax.all_to_all(picked, 'wave', 0, 0, tiled=True)]
    all_to_all x1, waiting for transfers between devices: 21.6 us -> 20.3 us  [on_device(): arrived = lax.all_to_all(picked, 'wave', 0, 0, tiled=True)]
    pallas_call x1, Pallas kernels: 5.59 us -> 4.47 us  [fourier_stage(): pl.pallas_call(fourier_kernel, out_shape=jax.ShapeDtypeStruct((rows, NLON...]
  transfers between devices with their start and end apart: 1 -> 2, of which waited for: 1 -> 1; matrix products, arithmetic and copies ran while one was open for 0% -> 0% of each run, Pallas kernels for 12% -> 23%
where the time goes in v6:
time: 66.1 us; the launch traced here: 65.8 us
  Pallas kernels  23 us (35%)
  waiting for transfers between devices  20.3 us (31%)
  starting transfers between devices  12.6 us (19%)
  local copies, waits for them, and re-layouts  9.11 us (14%)
  other arithmetic  0.75 us (1%)
    all_to_all x1, waiting for transfers between devices, on_device(): arrived = lax.all_to_all(picked, 'wave', 0, 0, tiled=True)  20.3 us
    pallas_call x1, Pallas kernels, legendre_stage(): pl.pallas_call(legendre_kernel, out_shape=pltpu.VMEM((2, 2 * lats * pairs...  8.34 us
    unnamed x8, local copies, waits for them, and re-layouts  8.12 us
    pallas_call x1, Pallas kernels, wave_tables(): pl.pallas_call(table_kernel, out_shape=pltpu.VMEM((2, 2, total, HALF), jn...  7.12 us
    all_to_all x1, starting transfers between devices, on_device(): lax.all_to_all(jnp.concatenate(entries, axis=2), 'wave', 0, 0, tiled=True)  6.55 us
    all_to_all x1, starting transfers between devices, on_device(): arrived = lax.all_to_all(picked, 'wave', 0, 0, tiled=True)  6.02 us
    pallas_call x1, Pallas kernels, fourier_stage(): pl.pallas_call(fourier_kernel, out_shape=jax.ShapeDtypeStruct((rows, NLON...  4.47 us
    pallas_call x1, Pallas kernels, pick_latitudes(): pl.pallas_call(pick_kernel, out_shape=jax.ShapeDtypeStruct(shape, jnp.bfl...  3.09 us
  transfers between devices with their start and end apart: 2, of which 1 were waited for; matrix products, arithmetic and copies ran while one was open for 0% of the time, Pallas kernels for 23%

profile of v6, /device:TPU:13, one launch (start us, length us, event | category | flops | bytes accessed | tf_op | source)
XLA Modules:
  0.0 65.8 jit_solution(1852342626104388919)
XLA Ops:
  0.0 0.7 %add_add_fusion = s32[128]{0:T(128)S(1)} fusion(s32[86]{0:T(128)S(1)} %broadcast_in_dim_broadcast_in_dim.3, s32[2]{0:T(128)} %param.7, s32[40]{0:T(128)} %waves_hbm.1), kind=kLoop, calls=%fused_computation | loop fusion | flops 256 | bytes 1024 | tf_op jit(solution)/shard_map/concatenate | solution.py:305
  0.7 0.6 broadcast.4
  1.4 6.6 %all-to-all-start = ((s32[16,1,128]{2,1,0:T(1,128)}), s32[16,1,128]{2,1,0:T(1,128)S(1)}, u32[]{:S(2)}, u32[]{:S(2)}) async-start(s32[16,1,128]{2,1,0:T(1,128)} %broadcast.4), calls=%async_computation | async-start | bytes 16384 | tf_op jit(solution)/shard_map/all_to_all | solution.py:305
  7.9 8.3 %legendre.1.rows_ref = f32[2,2560,128]{2,1,0:T(8,128)S(1)} custom-call(s32[40]{0:T(128)} %waves_hbm.1, bf16[641,40,128]{2,1,0:T(8,128)(2,1)} %bitcast.6, bf16[40,640,128]{2,1,0:T(8,128)(2,1)} %so_hbm.1, bf16[40,32,641]{2,1,0:T(8,128)(2,1)} %le_hbm.1, bf16[40,32,640]{2,1,0:T(8,128)(2,1)} %lo_hbm.1), custom_call_target="tpu_custom_call" | custom-call | flops 1679032320 | bytes 16396800 | tf_op jit(solution)/shard_map/legendre/pallas_call | solution.py:99
  16.3 0.0 all-to-all-done
  16.3 0.1 slice.8
  16.3 0.1 reshape.10.bands_ref
  16.4 3.1 %pick.1 = bf16[32,2,2,40,128]{4,3,2,1,0:T(8,128)(2,1)S(1)} custom-call(s32[32]{0:T(128)S(1)} %reshape.10.bands_ref, f32[2,2560,128]{2,1,0:T(8,128)S(1)} %legendre.1.rows_ref), custom_call_target="tpu_custom_call" | custom-call | tf_op jit(solution)/shard_map/pick/pallas_call | solution.py:152
  19.5 0.0 copy-start.2
  19.5 1.0 %copy-done.2 = bf16[32,2,2,40,128]{4,3,2,1,0:T(8,128)(2,1)} copy-done((bf16[32,2,2,40,128]{4,3,2,1,0:T(8,128)(2,1)}, bf16[32,2,2,40,128]{4,3,2,1,0:T(8,128)(2,1)S(1)}, u32[]{:S(2)}) %copy-start.2) | copy-done | bytes 1310744
  20.6 6.0 %all-to-all-start.1 = ((bf16[16,2,2,2,40,128]{5,4,3,2,1,0:T(8,128)(2,1)}), bf16[16,2,2,2,40,128]{5,4,3,2,1,0:T(8,128)(2,1)S(1)}, u32[]{:S(2)}, u32[]{:S(2)}) async-start(bf16[16,2,2,2,40,128]{5,4,3,2,1,0:T(8,128)(2,1)} %bitcast.5), calls=%async_computation.1 | async-start | bytes 2621440 | tf_op jit(solution)/shard_map/all_to_all | solution.py:311
  26.6 0.1 broadcast_in_dim.15
  26.7 0.1 broadcast_in_dim.16.waves_ref
  26.9 7.1 %tables.1.table_ref = bf16[2,2,640,1344]{3,2,1,0:T(8,128)(2,1)S(1)} custom-call(s32[640,128]{1,0:T(8,128)S(1)} %broadcast_in_dim.16.waves_ref), custom_call_target="tpu_custom_call" | custom-call | flops 13762560 | bytes 6881280 | tf_op jit(solution)/shard_map/tables/pallas_call | solution.py:198
  34.0 0.0 copy-start
  34.0 2.9 %copy-done = bf16[2,2,640,1344]{3,2,1,0:T(8,128)(2,1)} copy-done((bf16[2,2,640,1344]{3,2,1,0:T(8,128)(2,1)}, bf16[2,2,640,1344]{3,2,1,0:T(8,128)(2,1)S(1)}, u32[]{:S(2)}) %copy-start) | copy-done | bytes 6881304
  36.9 20.3 %all-to-all-done.1.arrived_hbm = bf16[16,2,2,2,40,128]{5,4,3,2,1,0:T(8,128)(2,1)S(1)} async-done(((bf16[16,2,2,2,40,128]{5,4,3,2,1,0:T(8,128)(2,1)}), bf16[16,2,2,2,40,128]{5,4,3,2,1,0:T(8,128)(2,1)S(1)}, u32[]{:S(2)}, u32[]{:S(2)}) %all-to-all-start.1) | async-done | bytes 1310752 | tf_op jit(solution)/shard_map/all_to_all | solution.py:311
  57.2 0.0 copy-start.3
  57.2 1.1 %copy-done.3 = bf16[16,2,2,2,40,128]{5,4,3,2,1,0:T(8,128)(2,1)} copy-done((bf16[16,2,2,2,40,128]{5,4,3,2,1,0:T(8,128)(2,1)}, bf16[16,2,2,2,40,128]{5,4,3,2,1,0:T(8,128)(2,1)S(1)}, u32[]{:S(2)}) %copy-start.3) | copy-done | bytes 1310744
  58.3 0.0 copy-start.1
  58.3 3.0 %copy-done.1 = bf16[2,2,640,1344]{3,2,1,0:T(8,128)(2,1)S(1)} copy-done((bf16[2,2,640,1344]{3,2,1,0:T(8,128)(2,1)S(1)}, bf16[2,2,640,1344]{3,2,1,0:T(8,128)(2,1)}, u32[]{:S(2)}) %copy-start.1) | copy-done | bytes 6881304
  61.3 4.5 %fourier.1 = bf16[256,2688]{1,0:T(8,128)(2,1)} custom-call(bf16[16,2,2,2,40,128]{5,4,3,2,1,0:T(8,128)(2,1)} %copy-done.3, bf16[2,2,640,1344]{3,2,1,0:T(8,128)(2,1)S(1)} %copy-done.1), custom_call_target="tpu_custom_call" | custom-call | flops 1761607680 | bytes 6881280 | tf_op jit(solution)/shard_map/fourier/pallas_call | solution.py:266
  (1 shorter events, 0.0 us)
Async XLA Ops:
  1.4 14.9 %all-to-all-start = ((s32[16,1,128]{2,1,0:T(1,128)}), s32[16,1,128]{2,1,0:T(1,128)S(1)}, u32[]{:S(2)}, u32[]{:S(2)}) async-start(s32[16,1,128]{2,1,0:T(1,128)} %broadcast.4), calls=%async_computation | async-start | bytes 16384 | tf_op jit(solution)/shard_map/all_to_all | solution.py:305
  19.5 1.1 %copy-start.2 = (bf16[32,2,2,40,128]{4,3,2,1,0:T(8,128)(2,1)}, bf16[32,2,2,40,128]{4,3,2,1,0:T(8,128)(2,1)S(1)}, u32[]{:S(2)}) copy-start(bf16[32,2,2,40,128]{4,3,2,1,0:T(8,128)(2,1)S(1)} %pick.1) | copy-start | bytes 3932164
  20.6 36.6 %all-to-all-start.1 = ((bf16[16,2,2,2,40,128]{5,4,3,2,1,0:T(8,128)(2,1)}), bf16[16,2,2,2,40,128]{5,4,3,2,1,0:T(8,128)(2,1)S(1)}, u32[]{:S(2)}, u32[]{:S(2)}) async-start(bf16[16,2,2,2,40,128]{5,4,3,2,1,0:T(8,128)(2,1)} %bitcast.5), calls=%async_computation.1 | async-start | bytes 2621440 | tf_op jit(solution)/shard_map/all_to_all | solution.py:311
  34.0 2.9 %copy-start = (bf16[2,2,640,1344]{3,2,1,0:T(8,128)(2,1)}, bf16[2,2,640,1344]{3,2,1,0:T(8,128)(2,1)S(1)}, u32[]{:S(2)}) copy-start(bf16[2,2,640,1344]{3,2,1,0:T(8,128)(2,1)S(1)} %tables.1.table_ref) | copy-start | bytes 20643844
  57.2 1.1 %copy-start.3 = (bf16[16,2,2,2,40,128]{5,4,3,2,1,0:T(8,128)(2,1)}, bf16[16,2,2,2,40,128]{5,4,3,2,1,0:T(8,128)(2,1)S(1)}, u32[]{:S(2)}) copy-start(bf16[16,2,2,2,40,128]{5,4,3,2,1,0:T(8,128)(2,1)S(1)} %all-to-all-done.1.arrived_hbm) | copy-start | bytes 3932164
  58.3 3.0 %copy-start.1 = (bf16[2,2,640,1344]{3,2,1,0:T(8,128)(2,1)S(1)}, bf16[2,2,640,1344]{3,2,1,0:T(8,128)(2,1)}, u32[]{:S(2)}) copy-start(bf16[2,2,640,1344]{3,2,1,0:T(8,128)(2,1)} %copy-done) | copy-start | bytes 20643844

commit v7 on v5

--- a/solution.py
+++ b/solution.py
@@ -122,72 +122,82 @@
     )(*(in_hbm(x) for x in operands))
 
 
-def pick_kernel(bands_ref, rows_ref, out_ref):
+def pick_kernel(crossed, column, *refs):
+    *index_refs, rows_ref, out_ref = refs
     lats, _, _, pairs, _ = out_ref.shape
-
-    def emit(slot, carry):
-        band = bands_ref[slot]
-        for h in range(2):
-            for w in range(2):
-                start = pl.multiple_of((w * lats + band) * pairs, ROWS)
-                out_ref[slot, h, w] = rows_ref[h, pl.ds(start, pairs), :].astype(jnp.bfloat16)
-        return carry
-
-    lax.fori_loop(0, lats, emit, 0, unroll=8)
-
-
-def pick_latitudes(bands, rows, pairs):
-    lats = bands.shape[0]
+    me = lax.axis_index("wave") if crossed else 0
+    first = 0
+    for index_ref in index_refs:
+        count = index_ref.shape[0]
+        slots = lats // (count * len(index_refs))
+
+        def emit(row, carry, index_ref=index_ref, first=first, slots=slots):
+            owner = me ^ (first + row)
+            for s in range(slots):
+                band = index_ref[row, column + s]
+                for h in range(2):
+                    for w in range(2):
+                        start = pl.multiple_of((w * lats + band) * pairs, ROWS)
+                        out_ref[owner * slots + s, h, w] = rows_ref[h, pl.ds(start, pairs), :].astype(jnp.bfloat16)
+            return carry
+
+        lax.fori_loop(0, count, emit, 0, unroll=4)
+        first += count
+
+
+def pick_latitudes(crossed, column, index, rows, lats, pairs):
     width = rows.shape[2]
     return pl.pallas_call(
-        pick_kernel,
+        functools.partial(pick_kernel, crossed, column),
         out_shape=jax.ShapeDtypeStruct((lats, 2, 2, pairs, width), jnp.bfloat16),
         grid_spec=pltpu.PrefetchScalarGridSpec(
-            num_scalar_prefetch=1,
+            num_scalar_prefetch=len(index),
             grid=(),
             in_specs=[pl.BlockSpec(memory_space=pltpu.VMEM)],
             out_specs=pl.BlockSpec(memory_space=pltpu.VMEM),
         ),
         compiler_params=pltpu.CompilerParams(vmem_limit_bytes=16 * 1024 * 1024),
-        name=f"pick_{pairs}",
-    )(bands, in_vmem(rows))
+        name="pick",
+    )(*index, in_vmem(rows))
 
 
 def table_kernel(waves_ref, out_ref):
-    low = waves_ref[...]
-    even = jnp.where(low % 2 == 0, low, M - 1 - low)
-    odd = M - 1 - even
-    lane = lax.broadcasted_iota(jnp.int32, low.shape, 1).astype(jnp.float32)
     unit = 2.0 * math.pi / NLON
+    block = 64
 
     def angle(product):
         turns = jnp.floor(product * (1.0 / NLON))
         return (product - turns * NLON) * unit
 
-    for w, wave in enumerate((even, odd)):
-        number = wave.astype(jnp.float32)
-        factor = jnp.where(wave == 0, 1.0, 2.0)
-        start = angle(number * lane)
-        step = angle(number * LANES)
-        c, s = factor * jnp.cos(start), -factor * jnp.sin(start)
-        dc, ds = jnp.cos(step), jnp.sin(step)
-        for b in range(0, HALF, LANES):
-            size = min(LANES, HALF - b)
-            out_ref[w, 0, :, b : b + size] = c[:, :size].astype(jnp.bfloat16)
-            out_ref[w, 1, :, b : b + size] = s[:, :size].astype(jnp.bfloat16)
-            c, s = c * dc + s * ds, s * dc - c * ds
+    @pl.loop(0, waves_ref.shape[0] // block)
+    def _(i):
+        at = pl.ds(pl.multiple_of(i * block, block), block)
+        low = waves_ref[at, :]
+        even = jnp.where(low % 2 == 0, low, M - 1 - low)
+        odd = M - 1 - even
+        lane = lax.broadcasted_iota(jnp.int32, low.shape, 1).astype(jnp.float32)
+        for w, wave in enumerate((even, odd)):
+            number = wave.astype(jnp.float32)
+            factor = jnp.where(wave == 0, 1.0, 2.0)
+            start = angle(number * lane)
+            step = angle(number * LANES)
+            c, s = factor * jnp.cos(start), -factor * jnp.sin(start)
+            dc, ds = jnp.cos(step), jnp.sin(step)
+            for b in range(0, HALF, LANES):
+                size = min(LANES, HALF - b)
+                out_ref[w, 0, at, b : b + size] = c[:, :size].astype(jnp.bfloat16)
+                out_ref[w, 1, at, b : b + size] = s[:, :size].astype(jnp.bfloat16)
+                c, s = c * dc + s * ds, s * dc - c * ds
 
 
 def wave_tables(waves):
     total = waves.shape[0]
-    rows = 64
     return pl.pallas_call(
         table_kernel,
-        out_shape=pltpu.HBM((2, 2, total, HALF), jnp.bfloat16),
-        grid=(total // rows,),
-        in_specs=[pl.BlockSpec((rows, LANES), lambda i: (i, 0))],
-        out_specs=pl.BlockSpec((2, 2, rows, HALF), lambda i: (0, 0, i, 0)),
-        compiler_params=pltpu.CompilerParams(vmem_limit_bytes=32 * 1024 * 1024),
+        out_shape=jax.ShapeDtypeStruct((2, 2, total, HALF), jnp.bfloat16),
+        in_specs=[pl.BlockSpec(memory_space=pltpu.VMEM)],
+        out_specs=pl.BlockSpec(memory_space=pltpu.VMEM),
+        compiler_params=pltpu.CompilerParams(vmem_limit_bytes=16 * 1024 * 1024),
         cost_estimate=pl.CostEstimate(
             flops=4 * 4 * total * HALF, bytes_accessed=8 * total * HALF, transcendentals=8 * total * LANES
         ),
@@ -268,7 +278,7 @@
             flops=8 * rows * total * HALF, bytes_accessed=8 * total * HALF, transcendentals=0
         ),
         name="fourier",
-    )(in_vmem(arrived), in_hbm(table))
+    )(arrived, table)
     return out.reshape(slots, 2, fields, NLON)
 
 
@@ -285,16 +295,32 @@
             for a in (spectra_even, spectra_odd, legendre_even, legendre_odd)
         )
 
-    own = jnp.pad(jnp.concatenate([wave_pairs, band_owner]), (0, round_up(pairs + slots, LANES) - pairs - slots))
-    block = lax.optimization_barrier(jnp.broadcast_to(own, (32,) + own.shape))
-    index = lax.optimization_barrier(lax.all_gather(block, "wave", axis=0))[:, 0]
-    all_pairs = index[:, :pairs].reshape(-1)
-    all_bands = index[:, pairs : pairs + slots].reshape(-1)
-
+    crossed = devices == 16
+    index = gather_index(devices, crossed, wave_pairs, band_owner)
     rows = legendre_stage(wave_pairs, spectra_even, spectra_odd, legendre_even, legendre_odd)
-    picked = pick_latitudes(all_bands, rows, pairs).reshape(devices, slots, 2, 2, pairs, width)
-    arrived = lax.all_to_all(picked, "wave", 0, 0, tiled=True)
-    return fourier_stage(arrived, wave_tables(all_pairs))
+    picked = pick_latitudes(crossed, pairs, index, rows, devices * slots, pairs)
+    index, picked = lax.optimization_barrier((index, picked))
+    arrived = lax.all_to_all(picked.reshape(devices, slots, 2, 2, pairs, width), "wave", 0, 0, tiled=True)
+    all_pairs = jnp.concatenate(index, axis=0)[:, :pairs]
+    if crossed:
+        order = lax.axis_index("wave") ^ jnp.arange(devices)
+        chosen = (order[:, None] == jnp.arange(devices)[None])[:, :, None]
+        all_pairs = jnp.sum(jnp.where(chosen, all_pairs[None], 0), axis=1)
+    return fourier_stage(arrived, wave_tables(all_pairs.reshape(-1)))
+
+
+def gather_index(devices, crossed, waves, bands):
+    rest = round_up(waves.shape[0] + bands.shape[0], LANES) - waves.shape[0] - bands.shape[0]
+    own = jnp.concatenate([waves, bands, jnp.zeros(rest, jnp.int32)])
+    if not crossed:
+        own = jnp.broadcast_to(own, (devices, 1) + own.shape)
+        return [lax.all_to_all(own, "wave", 0, 0, tiled=True)[:, 0]]
+
+    def send(x, k):
+        return lax.ppermute(x, "wave", [(i, i ^ k) for i in range(devices)])
+
+    near = jnp.concatenate([own[None]] + [send(own[None], k) for k in (1, 2, 3)], axis=0)
+    return [near] + [send(near, k) for k in (4, 8, 12)]
 
 
 def solution(mesh):

time: 74 us -> 64.7 us (0.87)
  blocking collectives: 16.3 us -> 0 us
  local copies, waits for them, and re-layouts: 0.4 us -> 6.19 us
  starting transfers between devices: 10.2 us -> 13.6 us
  Pallas kernels: 24.4 us -> 22.5 us
    all_gather x1 -> x0, blocking collectives: 16.3 us -> none  [on_device(): lax.all_gather(block, 'wave', axis=0)]
    unnamed x0 -> x4, local copies, waits for them, and re-layouts: none -> 5.97 us
    ppermute x0 -> x6, starting transfers between devices: none -> 5.7 us  [send(): return lax.ppermute(x, 'wave', [(i, i ^ k) for i in range(devices)])]
    all_to_all x1, starting transfers between devices: 10.2 us -> 7.9 us  [on_device(): lax.all_to_all(picked.reshape(devices, slots, 2, 2, pairs, width), 'wave'...]
    all_to_all x1, waiting for transfers between devices: 21.6 us -> 20.1 us  [on_device(): lax.all_to_all(picked.reshape(devices, slots, 2, 2, pairs, width), 'wave'...]
    pallas_call x2, Pallas kernels: 10.5 us -> 8.99 us  [the longest x1 7.12 us: wave_tables(): pl.pallas_call(table_kernel, out_shape=jax.ShapeDtypeStruct((2, 2, total,...]
    ppermute x0 -> x6, waiting for transfers between devices: none -> 1.05 us  [send(): return lax.ppermute(x, 'wave', [(i, i ^ k) for i in range(devices)])]
    broadcast_in_dim x0 -> x1, other arithmetic: none -> 0.75 us  [gather_index(): own[None]]
  transfers between devices with their start and end apart: 1 -> 7, of which waited for: 1 -> 3; matrix products, arithmetic and copies ran while one was open for 0% -> 1% of each run, Pallas kernels for 12% -> 24%
where the time goes in v7:
time: 64.7 us; the launch traced here: 64.5 us
  Pallas kernels  22.5 us (35%)
  waiting for transfers between devices  21.1 us (33%)
  starting transfers between devices  13.6 us (21%)
  local copies, waits for them, and re-layouts  6.19 us (10%)
  other arithmetic  0.96 us (1%)
    all_to_all x1, waiting for transfers between devices, on_device(): lax.all_to_all(picked.reshape(devices, slots, 2, 2, pairs, width), 'wave'...  20.1 us
    pallas_call x1, Pallas kernels, legendre_stage(): pl.pallas_call(legendre_kernel, out_shape=pltpu.VMEM((2, 2 * lats * pairs...  8.34 us
    all_to_all x1, starting transfers between devices, on_device(): lax.all_to_all(picked.reshape(devices, slots, 2, 2, pairs, width), 'wave'...  7.9 us
    pallas_call x1, Pallas kernels, wave_tables(): pl.pallas_call(table_kernel, out_shape=jax.ShapeDtypeStruct((2, 2, total,...  7.12 us
    unnamed x4, local copies, waits for them, and re-layouts  5.97 us
    ppermute x6, starting transfers between devices, send(): return lax.ppermute(x, 'wave', [(i, i ^ k) for i in range(devices)])  5.7 us
    pallas_call x1, Pallas kernels, fourier_stage(): pl.pallas_call(fourier_kernel, out_shape=jax.ShapeDtypeStruct((rows, NLON...  5.2 us
    pallas_call x1, Pallas kernels, pick_latitudes(): pl.pallas_call(functools.partial(pick_kernel, crossed, column), out_shape...  1.88 us
  transfers between devices with their start and end apart: 7, of which 3 were waited for; matrix products, arithmetic and copies ran while one was open for 1% of the time, Pallas kernels for 24%

profile of v7, /device:TPU:13, one launch (start us, length us, event | category | flops | bytes accessed | tf_op | source)
XLA Modules:
  0.0 64.5 jit_solution(6919829807028818975)
XLA Ops:
  0.0 0.7 %add_bitcast_fusion = s32[1,128]{1,0:T(1,128)S(1)} fusion(s32[86]{0:T(128)S(1)} %broadcast_in_dim.40, s32[2]{0:T(128)} %param.7, s32[40]{0:T(128)} %waves_hbm.1), kind=kLoop, calls=%fused_computation.6 | loop fusion | flops 256 | bytes 1024 | tf_op jit(solution)/shard_map/broadcast_in_dim | solution.py:322
  0.7 0.8 %collective-permute-start.2 = (s32[1,128]{1,0:T(1,128)S(1)}, s32[1,128]{1,0:T(1,128)S(1)}, u32[]{:S(2)}, u32[]{:S(2)}) collective-permute-start(s32[1,128]{1,0:T(1,128)S(1)} %add_bitcast_fusion), channel_id=1, source_target_pairs={{0,3},{1,2},{2,1},{3,0},{4,7},{5,6},{6,5},{7,4},{8,11},{9,10},{10,... | collective-permute-start | bytes 1544 | tf_op jit(solution)/shard_map/ppermute | solution.py:320
  1.5 1.2 %collective-permute-start.1 = (s32[1,128]{1,0:T(1,128)S(1)}, s32[1,128]{1,0:T(1,128)S(1)}, u32[]{:S(2)}, u32[]{:S(2)}) collective-permute-start(s32[1,128]{1,0:T(1,128)S(1)} %add_bitcast_fusion), channel_id=1, source_target_pairs={{0,2},{1,3},{2,0},{3,1},{4,6},{5,7},{6,4},{7,5},{8,10},{9,11},{10,... | collective-permute-start | bytes 1544 | tf_op jit(solution)/shard_map/ppermute | solution.py:320
  2.8 0.1 collective-permute-start
  2.9 0.8 %collective-permute-done.2 = s32[1,128]{1,0:T(1,128)S(1)} collective-permute-done((s32[1,128]{1,0:T(1,128)S(1)}, s32[1,128]{1,0:T(1,128)S(1)}, u32[]{:S(2)}, u32[]{:S(2)}) %collective-permute-start.2) | collective-permute-done | bytes 544 | tf_op jit(solution)/shard_map/ppermute | solution.py:320
  3.7 0.2 collective-permute-done.1
  3.9 0.0 collective-permute-done
  3.9 1.4 %collective-permute-start.5 = (s32[4,128]{1,0:T(4,128)S(1)}, s32[4,128]{1,0:T(4,128)S(1)}, u32[]{:S(2)}, u32[]{:S(2)}) collective-permute-start(s32[4,128]{1,0:T(4,128)S(1)} %pad_add_fusion.3.refs_0_), channel_id=1, source_target_pairs={{0,12},{1,13},{2,14},{3,15},{4,8},{5,9},{6,10},{7,11},{8,4},{9,5},... | collective-permute-start | bytes 6152 | tf_op jit(solution)/shard_map/ppermute | solution.py:320
  5.3 1.1 %collective-permute-start.4 = (s32[4,128]{1,0:T(4,128)S(1)}, s32[4,128]{1,0:T(4,128)S(1)}, u32[]{:S(2)}, u32[]{:S(2)}) collective-permute-start(s32[4,128]{1,0:T(4,128)S(1)} %pad_add_fusion.3.refs_0_), channel_id=1, source_target_pairs={{0,8},{1,9},{2,10},{3,11},{4,12},{5,13},{6,14},{7,15},{8,0},{9,1},... | collective-permute-start | bytes 6152 | tf_op jit(solution)/shard_map/ppermute | solution.py:320
  6.4 1.1 %collective-permute-start.3 = (s32[4,128]{1,0:T(4,128)S(1)}, s32[4,128]{1,0:T(4,128)S(1)}, u32[]{:S(2)}, u32[]{:S(2)}) collective-permute-start(s32[4,128]{1,0:T(4,128)S(1)} %pad_add_fusion.3.refs_0_), channel_id=1, source_target_pairs={{0,4},{1,5},{2,6},{3,7},{4,0},{5,1},{6,2},{7,3},{8,12},{9,13},{10,... | collective-permute-start | bytes 6152 | tf_op jit(solution)/shard_map/ppermute | solution.py:320
  7.5 8.3 %legendre.1.refs_4_ = f32[2,2560,128]{2,1,0:T(8,128)S(1)} custom-call(s32[40]{0:T(128)} %waves_hbm.1, bf16[641,40,128]{2,1,0:T(8,128)(2,1)} %bitcast.5, bf16[40,640,128]{2,1,0:T(8,128)(2,1)} %so_hbm.1, bf16[40,32,641]{2,1,0:T(8,128)(2,1)} %le_hbm.1, bf16[40,32,640]{2,1,0:T(8,128)(2,1)} %lo_hbm.1), custom_call_target="tpu_custom_call" | custom-call | flops 1679032320 | bytes 16396800 | tf_op jit(solution)/shard_map/legendre/pallas_call | solution.py:99
  15.9 0.0 collective-permute-done.4.refs_2_
  15.9 0.0 collective-permute-done.3.refs_1_
  15.9 1.9 %pick.1 = bf16[32,2,2,40,128]{4,3,2,1,0:T(8,128)(2,1)} custom-call(s32[4,128]{1,0:T(4,128)S(1)} %pad_add_fusion.3.refs_0_, s32[4,128]{1,0:T(4,128)S(1)} %collective-permute-done.3.refs_1_, s32[4,128]{1,0:T(4,128)S(1)} %collective-permute-done.4.refs_2_, s32[4,128]{1,0:T(4,128)S(1)} %collective-permute-done.5.refs_3_, f32[2,2560,128]{2,1,0:T(8,128)S(1)} %legendre.1.refs_4_), custom_call_target="tpu_custom_call" | custom-call | tf_op jit(solution)/shard_map/pick/pallas_call | solution.py:150
  17.8 7.9 %all-to-all-start = ((bf16[16,2,2,2,40,128]{5,4,3,2,1,0:T(8,128)(2,1)}), bf16[16,2,2,2,40,128]{5,4,3,2,1,0:T(8,128)(2,1)S(1)}, u32[]{:S(2)}, u32[]{:S(2)}) async-start(bf16[16,2,2,2,40,128]{5,4,3,2,1,0:T(8,128)(2,1)} %bitcast.2), calls=%async_computation | async-start | bytes 2621440 | tf_op jit(solution)/shard_map/all_to_all | solution.py:303
  25.7 0.1 iota_compare_fusion
  25.7 0.1 select_reduce_fusion
  25.9 0.1 broadcast_in_dim.45
  26.0 0.1 broadcast_in_dim.46.waves_ref
  26.1 7.1 %tables.1.table_hbm = bf16[2,2,640,1344]{3,2,1,0:T(8,128)(2,1)S(1)} custom-call(s32[640,128]{1,0:T(8,128)S(1)} %broadcast_in_dim.46.waves_ref), custom_call_target="tpu_custom_call" | custom-call | flops 13762560 | bytes 6881280 | tf_op jit(solution)/shard_map/tables/pallas_call | solution.py:195
  33.2 2.9 %copy-done = bf16[2,2,640,1344]{3,2,1,0:T(8,128)(2,1)} copy-done((bf16[2,2,640,1344]{3,2,1,0:T(8,128)(2,1)}, bf16[2,2,640,1344]{3,2,1,0:T(8,128)(2,1)S(1)}, u32[]{:S(2)}) %copy-start) | copy-done | bytes 6881304
  36.2 20.1 %all-to-all-done.arrived_ref = bf16[16,2,2,2,40,128]{5,4,3,2,1,0:T(8,128)(2,1)S(1)} async-done(((bf16[16,2,2,2,40,128]{5,4,3,2,1,0:T(8,128)(2,1)}), bf16[16,2,2,2,40,128]{5,4,3,2,1,0:T(8,128)(2,1)S(1)}, u32[]{:S(2)}, u32[]{:S(2)}) %all-to-all-start) | async-done | bytes 1310752 | tf_op jit(solution)/shard_map/all_to_all | solution.py:303
  56.2 3.0 %copy-done.1 = bf16[2,2,640,1344]{3,2,1,0:T(8,128)(2,1)S(1)} copy-done((bf16[2,2,640,1344]{3,2,1,0:T(8,128)(2,1)S(1)}, bf16[2,2,640,1344]{3,2,1,0:T(8,128)(2,1)}, u32[]{:S(2)}) %copy-start.1) | copy-done | bytes 6881304
  59.3 5.2 %fourier.1 = bf16[256,2688]{1,0:T(8,128)(2,1)} custom-call(bf16[16,2,2,2,40,128]{5,4,3,2,1,0:T(8,128)(2,1)S(1)} %all-to-all-done.arrived_ref, bf16[2,2,640,1344]{3,2,1,0:T(8,128)(2,1)S(1)} %copy-done.1), custom_call_target="tpu_custom_call" | custom-call | flops 1761607680 | bytes 6881280 | tf_op jit(solution)/shard_map/fourier/pallas_call | solution.py:264
  (7 shorter events, 0.0 us)
Async XLA Ops:
  0.7 3.0 %collective-permute-start.2 = (s32[1,128]{1,0:T(1,128)S(1)}, s32[1,128]{1,0:T(1,128)S(1)}, u32[]{:S(2)}, u32[]{:S(2)}) collective-permute-start(s32[1,128]{1,0:T(1,128)S(1)} %add_bitcast_fusion), channel_id=1, source_target_pairs={{0,3},{1,2},{2,1},{3,0},{4,7},{5,6},{6,5},{7,4},{8,11},{9,10},{10,... | collective-permute-start | bytes 1544 | tf_op jit(solution)/shard_map/ppermute | solution.py:320
  1.5 2.4 %collective-permute-start.1 = (s32[1,128]{1,0:T(1,128)S(1)}, s32[1,128]{1,0:T(1,128)S(1)}, u32[]{:S(2)}, u32[]{:S(2)}) collective-permute-start(s32[1,128]{1,0:T(1,128)S(1)} %add_bitcast_fusion), channel_id=1, source_target_pairs={{0,2},{1,3},{2,0},{3,1},{4,6},{5,7},{6,4},{7,5},{8,10},{9,11},{10,... | collective-permute-start | bytes 1544 | tf_op jit(solution)/shard_map/ppermute | solution.py:320
  2.8 1.2 %collective-permute-start = (s32[1,128]{1,0:T(1,128)S(1)}, s32[1,128]{1,0:T(1,128)S(1)}, u32[]{:S(2)}, u32[]{:S(2)}) collective-permute-start(s32[1,128]{1,0:T(1,128)S(1)} %add_bitcast_fusion), channel_id=1, source_target_pairs={{0,1},{1,0},{2,3},{3,2},{4,5},{5,4},{6,7},{7,6},{8,9},{9,8},{10,11... | collective-permute-start | bytes 1544 | tf_op jit(solution)/shard_map/ppermute | solution.py:320
  3.9 11.9 %collective-permute-start.5 = (s32[4,128]{1,0:T(4,128)S(1)}, s32[4,128]{1,0:T(4,128)S(1)}, u32[]{:S(2)}, u32[]{:S(2)}) collective-permute-start(s32[4,128]{1,0:T(4,128)S(1)} %pad_add_fusion.3.refs_0_), channel_id=1, source_target_pairs={{0,12},{1,13},{2,14},{3,15},{4,8},{5,9},{6,10},{7,11},{8,4},{9,5},... | collective-permute-start | bytes 6152 | tf_op jit(solution)/shard_map/ppermute | solution.py:320
  5.3 10.6 %collective-permute-start.4 = (s32[4,128]{1,0:T(4,128)S(1)}, s32[4,128]{1,0:T(4,128)S(1)}, u32[]{:S(2)}, u32[]{:S(2)}) collective-permute-start(s32[4,128]{1,0:T(4,128)S(1)} %pad_add_fusion.3.refs_0_), channel_id=1, source_target_pairs={{0,8},{1,9},{2,10},{3,11},{4,12},{5,13},{6,14},{7,15},{8,0},{9,1},... | collective-permute-start | bytes 6152 | tf_op jit(solution)/shard_map/ppermute | solution.py:320
  6.4 9.5 %collective-permute-start.3 = (s32[4,128]{1,0:T(4,128)S(1)}, s32[4,128]{1,0:T(4,128)S(1)}, u32[]{:S(2)}, u32[]{:S(2)}) collective-permute-start(s32[4,128]{1,0:T(4,128)S(1)} %pad_add_fusion.3.refs_0_), channel_id=1, source_target_pairs={{0,4},{1,5},{2,6},{3,7},{4,0},{5,1},{6,2},{7,3},{8,12},{9,13},{10,... | collective-permute-start | bytes 6152 | tf_op jit(solution)/shard_map/ppermute | solution.py:320
  17.8 38.5 %all-to-all-start = ((bf16[16,2,2,2,40,128]{5,4,3,2,1,0:T(8,128)(2,1)}), bf16[16,2,2,2,40,128]{5,4,3,2,1,0:T(8,128)(2,1)S(1)}, u32[]{:S(2)}, u32[]{:S(2)}) async-start(bf16[16,2,2,2,40,128]{5,4,3,2,1,0:T(8,128)(2,1)} %bitcast.2), calls=%async_computation | async-start | bytes 2621440 | tf_op jit(solution)/shard_map/all_to_all | solution.py:303
  33.2 2.9 %copy-start = (bf16[2,2,640,1344]{3,2,1,0:T(8,128)(2,1)}, bf16[2,2,640,1344]{3,2,1,0:T(8,128)(2,1)S(1)}, u32[]{:S(2)}) copy-start(bf16[2,2,640,1344]{3,2,1,0:T(8,128)(2,1)S(1)} %tables.1.table_hbm) | copy-start | bytes 20643844
  56.2 3.0 %copy-start.1 = (bf16[2,2,640,1344]{3,2,1,0:T(8,128)(2,1)S(1)}, bf16[2,2,640,1344]{3,2,1,0:T(8,128)(2,1)}, u32[]{:S(2)}) copy-start(bf16[2,2,640,1344]{3,2,1,0:T(8,128)(2,1)} %copy-done) | copy-start | bytes 20643844

commit v8 on v5

--- a/solution.py
+++ b/solution.py
@@ -10,7 +10,8 @@
 
 M = 1280
 NLON = 2688
-HALF = NLON // 2
+QUARTER = NLON // 4
+CHUNK = 256
 ROWS = 8
 LANES = 128
 
@@ -43,7 +44,8 @@
 
     wave_copy = pltpu.make_async_copy(waves_hbm, waves_ref, wave_sem)
     wave_copy.start()
-    for g in range(groups):
+    ahead = 2
+    for g in range(min(ahead, groups)):
         for copy in odd_copies(g) + even_copies(g):
             copy.start()
     wave_copy.wait()
@@ -63,6 +65,12 @@
         base = pl.multiple_of(g * ROWS, ROWS)
         for copy in odd_copies(g):
             copy.wait()
+
+        @pl.when(g + ahead < groups)
+        def _():
+            for copy in odd_copies(g + ahead) + even_copies(g + ahead):
+                copy.start()
+
         for p in range(ROWS):
             odd = split(lo_ref[base + p], ids_o, (M - waves_ref[base + p]) // 2)
             anti_ref[p] = jnp.dot(odd, so_ref[base + p], preferred_element_type=jnp.float32)
@@ -122,8 +130,13 @@
     )(*(in_hbm(x) for x in operands))
 
 
-def pick_kernel(bands_ref, rows_ref, out_ref):
+def pick_kernel(bands_ref, rows_ref, out_hbm, out_ref, sems):
     lats, _, _, pairs, _ = out_ref.shape
+    piece = lats // sems.shape[0]
+
+    def store(i):
+        at = pl.ds(i * piece, piece)
+        return pltpu.make_async_copy(out_ref.at[at], out_hbm.at[at], sems.at[i])
 
     def emit(slot, carry):
         band = bands_ref[slot]
@@ -133,31 +146,40 @@
                 out_ref[slot, h, w] = rows_ref[h, pl.ds(start, pairs), :].astype(jnp.bfloat16)
         return carry
 
-    lax.fori_loop(0, lats, emit, 0, unroll=8)
+    for i in range(sems.shape[0]):
+        lax.fori_loop(i * piece, (i + 1) * piece, emit, 0, unroll=4)
+        store(i).start()
+    for i in range(sems.shape[0]):
+        store(i).wait()
 
 
 def pick_latitudes(bands, rows, pairs):
     lats = bands.shape[0]
     width = rows.shape[2]
+    shape = (lats, 2, 2, pairs, width)
     return pl.pallas_call(
         pick_kernel,
-        out_shape=jax.ShapeDtypeStruct((lats, 2, 2, pairs, width), jnp.bfloat16),
+        out_shape=pltpu.HBM(shape, jnp.bfloat16),
         grid_spec=pltpu.PrefetchScalarGridSpec(
             num_scalar_prefetch=1,
             grid=(),
             in_specs=[pl.BlockSpec(memory_space=pltpu.VMEM)],
-            out_specs=pl.BlockSpec(memory_space=pltpu.VMEM),
+            out_specs=pl.BlockSpec(memory_space=pl.ANY),
+            scratch_shapes=[pltpu.VMEM(shape, jnp.bfloat16), pltpu.SemaphoreType.DMA((4,))],
         ),
         compiler_params=pltpu.CompilerParams(vmem_limit_bytes=16 * 1024 * 1024),
-        name=f"pick_{pairs}",
+        name="pick",
     )(bands, in_vmem(rows))
 
 
+def even_wave(low):
+    return jnp.where(low % 2 == 0, low, M - 1 - low)
+
+
 def table_kernel(waves_ref, out_ref):
-    low = waves_ref[...]
-    even = jnp.where(low % 2 == 0, low, M - 1 - low)
+    even = even_wave(waves_ref[...])
     odd = M - 1 - even
-    lane = lax.broadcasted_iota(jnp.int32, low.shape, 1).astype(jnp.float32)
+    lane = lax.broadcasted_iota(jnp.int32, even.shape, 1).astype(jnp.float32)
     unit = 2.0 * math.pi / NLON
 
     def angle(product):
@@ -171,104 +193,116 @@
         step = angle(number * LANES)
         c, s = factor * jnp.cos(start), -factor * jnp.sin(start)
         dc, ds = jnp.cos(step), jnp.sin(step)
-        for b in range(0, HALF, LANES):
-            size = min(LANES, HALF - b)
-            out_ref[w, 0, :, b : b + size] = c[:, :size].astype(jnp.bfloat16)
-            out_ref[w, 1, :, b : b + size] = s[:, :size].astype(jnp.bfloat16)
+        for b in range(0, QUARTER, LANES):
+            at = slice(b % CHUNK, b % CHUNK + LANES)
+            out_ref[b // CHUNK, w, 0, :, at] = c.astype(jnp.bfloat16)
+            out_ref[b // CHUNK, w, 1, :, at] = s.astype(jnp.bfloat16)
             c, s = c * dc + s * ds, s * dc - c * ds
 
 
 def wave_tables(waves):
     total = waves.shape[0]
     rows = 64
+    chunks = pl.cdiv(QUARTER, CHUNK)
     return pl.pallas_call(
         table_kernel,
-        out_shape=pltpu.HBM((2, 2, total, HALF), jnp.bfloat16),
+        out_shape=pltpu.HBM((chunks, 2, 2, total, CHUNK), jnp.bfloat16),
         grid=(total // rows,),
         in_specs=[pl.BlockSpec((rows, LANES), lambda i: (i, 0))],
-        out_specs=pl.BlockSpec((2, 2, rows, HALF), lambda i: (0, 0, i, 0)),
+        out_specs=pl.BlockSpec((chunks, 2, 2, rows, CHUNK), lambda i: (0, 0, 0, i, 0)),
         compiler_params=pltpu.CompilerParams(vmem_limit_bytes=32 * 1024 * 1024),
         cost_estimate=pl.CostEstimate(
-            flops=4 * 4 * total * HALF, bytes_accessed=8 * total * HALF, transcendentals=8 * total * LANES
+            flops=16 * total * QUARTER, bytes_accessed=8 * total * QUARTER, transcendentals=8 * total * LANES
         ),
         name="tables",
     )(jnp.broadcast_to(waves[:, None], (total, LANES)))
 
 
-def fourier_kernel(arrived_ref, table_hbm, out_hbm, left_ref, table_ref, row_ref, sems, out_sems):
+def fourier_kernel(
+    arrived_ref, sign_hbm, table_hbm, out_hbm, left_ref, sign_ref, table_ref, row_ref, sems, sign_sem, out_sems
+):
     devices, slots, _, _, pairs, width = arrived_ref.shape
     fields = width // 2
     total = devices * pairs
-    chunk = 256
-    ends = list(range(0, HALF, chunk)) + [HALF]
-    spans = list(zip(ends[:-1], ends[1:]))
+    chunks = table_ref.shape[0]
+    rows = 2 * fields
 
     def load(i):
-        at = slice(*spans[i])
-        return pltpu.make_async_copy(table_hbm.at[:, :, :, at], table_ref.at[:, :, :, at], sems.at[i])
-
-    for i in range(len(spans)):
+        return pltpu.make_async_copy(table_hbm.at[i], table_ref.at[i], sems.at[i])
+
+    sign_copy = pltpu.make_async_copy(sign_hbm, sign_ref, sign_sem)
+    sign_copy.start()
+    for i in range(chunks):
         load(i).start()
 
-    for w in range(2):
-        for s in range(slots):
-            for h in range(2):
+    stores = []
+    for s in range(slots):
+        turned = []
+        for h in range(2):
+            for w in range(2):
                 x = jnp.concatenate([arrived_ref[d, s, h, w] for d in range(devices)], axis=0)
                 xt = x.T
-                r = (s * 2 + h) * fields
-                left_ref[w, r : r + fields, :total] = xt[:fields]
-                left_ref[w, r : r + fields, total:] = xt[fields:]
-
-    stores = []
-    sent = [0, round_up(HALF, LANES)]
-    for i, (lo, hi) in enumerate(spans):
-        load(i).wait()
-        e, o = [
-            jnp.dot(
-                left_ref[w],
-                jnp.concatenate([table_ref[w, 0, :, lo:hi], table_ref[w, 1, :, lo:hi]], axis=0),
-                preferred_element_type=jnp.float32,
-            )
-            for w in range(2)
-        ]
-        row_ref[:, lo:hi] = (e + o).astype(jnp.bfloat16)
-        row_ref[:, HALF + lo : HALF + hi] = (e - o).astype(jnp.bfloat16)
-        done = hi == HALF
-        reach = (round_up(HALF, LANES) if done else hi, NLON if done else (HALF + hi) // LANES * LANES)
-        for part in range(2):
-            at = slice(sent[part], reach[part])
-            copy = pltpu.make_async_copy(row_ref.at[:, at], out_hbm.at[:, at], out_sems.at[part, i])
-            copy.start()
-            stores.append(copy)
-            sent[part] = reach[part]
+                at = slice(h * fields, (h + 1) * fields)
+                left_ref[s, w, at, :total] = xt[:fields]
+                left_ref[s, w, at, total:] = xt[fields:]
+                turned.append((h, w, xt))
+        if s == 0:
+            sign_copy.wait()
+        sign = sign_ref[0:1, :]
+        for h, w, xt in turned:
+            at = slice(rows + h * fields, rows + (h + 1) * fields)
+            signed = (xt.astype(jnp.float32) * sign).astype(jnp.bfloat16)
+            re, im = signed[:fields], signed[fields:]
+            left_ref[s, w, at, :total] = im if w else re
+            left_ref[s, w, at, total:] = -re if w else im
+        base = slice(s * rows, (s + 1) * rows)
+        for i in range(chunks):
+            if s == 0:
+                load(i).wait()
+            lo, hi = i * CHUNK, min((i + 1) * CHUNK, QUARTER)
+            e, o = [
+                jnp.dot(
+                    left_ref[s, w],
+                    table_ref[i, w].reshape(2 * total, CHUNK),
+                    preferred_element_type=jnp.float32,
+                )[:, : hi - lo]
+                for w in range(2)
+            ]
+            plus, minus = e + o, e - o
+            for k, part in enumerate((plus[:rows], plus[rows:], minus[:rows], minus[rows:])):
+                row_ref[base, k * QUARTER + lo : k * QUARTER + hi] = part.astype(jnp.bfloat16)
+        copy = pltpu.make_async_copy(row_ref.at[base], out_hbm.at[base], out_sems.at[s])
+        copy.start()
+        stores.append(copy)
     for copy in stores:
         copy.wait()
 
 
-def fourier_stage(arrived, table):
+def fourier_stage(arrived, sign, table):
     devices, slots, _, _, pairs, width = arrived.shape
     fields = width // 2
     total = devices * pairs
     rows = slots * 2 * fields
-    spans = pl.cdiv(HALF, 256)
     out = pl.pallas_call(
         fourier_kernel,
         out_shape=jax.ShapeDtypeStruct((rows, NLON), jnp.bfloat16),
-        in_specs=[pl.BlockSpec(memory_space=pltpu.VMEM), pl.BlockSpec(memory_space=pl.ANY)],
+        in_specs=[pl.BlockSpec(memory_space=pltpu.VMEM)] + [pl.BlockSpec(memory_space=pl.ANY)] * 2,
         out_specs=pl.BlockSpec(memory_space=pl.ANY),
         scratch_shapes=[
-            pltpu.VMEM((2, rows, 2 * total), jnp.bfloat16),
-            pltpu.VMEM((2, 2, total, HALF), jnp.bfloat16),
+            pltpu.VMEM((slots, 2, 4 * fields, 2 * total), jnp.bfloat16),
+            pltpu.VMEM(sign.shape, jnp.float32),
+            pltpu.VMEM(table.shape, jnp.bfloat16),
             pltpu.VMEM((rows, NLON), jnp.bfloat16),
-            pltpu.SemaphoreType.DMA((spans,)),
-            pltpu.SemaphoreType.DMA((2, spans)),
+            pltpu.SemaphoreType.DMA((table.shape[0],)),
+            pltpu.SemaphoreType.DMA,
+            pltpu.SemaphoreType.DMA((slots,)),
         ],
-        compiler_params=pltpu.CompilerParams(vmem_limit_bytes=40 * 1024 * 1024),
+        compiler_params=pltpu.CompilerParams(vmem_limit_bytes=32 * 1024 * 1024),
         cost_estimate=pl.CostEstimate(
-            flops=8 * rows * total * HALF, bytes_accessed=8 * total * HALF, transcendentals=0
+            flops=16 * rows * total * QUARTER, bytes_accessed=8 * total * QUARTER, transcendentals=0
         ),
         name="fourier",
-    )(in_vmem(arrived), in_hbm(table))
+    )(arrived, in_hbm(sign), in_hbm(table))
     return out.reshape(slots, 2, fields, NLON)
 
 
@@ -285,16 +319,19 @@
             for a in (spectra_even, spectra_odd, legendre_even, legendre_odd)
         )
 
-    own = jnp.pad(jnp.concatenate([wave_pairs, band_owner]), (0, round_up(pairs + slots, LANES) - pairs - slots))
-    block = lax.optimization_barrier(jnp.broadcast_to(own, (32,) + own.shape))
-    index = lax.optimization_barrier(lax.all_gather(block, "wave", axis=0))[:, 0]
+    rest = round_up(pairs + slots, LANES) - pairs - slots
+    own = jnp.concatenate([wave_pairs, band_owner, jnp.zeros(rest, jnp.int32)])
+    own = jnp.broadcast_to(own, (devices, 1) + own.shape)
+    index = lax.all_to_all(own, "wave", 0, 0, tiled=True)[:, 0]
+    all_bands = index[:, pairs : pairs + slots].reshape(-1)
+    rows = legendre_stage(wave_pairs, spectra_even, spectra_odd, legendre_even, legendre_odd)
+    picked = pick_latitudes(all_bands, rows, pairs)
+    index, picked = lax.optimization_barrier((index, picked))
+    arrived = lax.all_to_all(picked.reshape(devices, slots, 2, 2, pairs, width), "wave", 0, 0, tiled=True)
     all_pairs = index[:, :pairs].reshape(-1)
-    all_bands = index[:, pairs : pairs + slots].reshape(-1)
-
-    rows = legendre_stage(wave_pairs, spectra_even, spectra_odd, legendre_even, legendre_odd)
-    picked = pick_latitudes(all_bands, rows, pairs).reshape(devices, slots, 2, 2, pairs, width)
-    arrived = lax.all_to_all(picked, "wave", 0, 0, tiled=True)
-    return fourier_stage(arrived, wave_tables(all_pairs))
+    sign = jnp.where(even_wave(all_pairs) % 4 == 0, 1.0, -1.0).astype(jnp.float32)
+    sign = jnp.broadcast_to(sign, (ROWS,) + sign.shape)
+    return fourier_stage(arrived, sign, wave_tables(all_pairs))
 
 
 def solution(mesh):

time: 74 us -> 60.9 us (0.82)
  blocking collectives: 16.3 us -> 0 us
  starting transfers between devices: 10.2 us -> 12.6 us
  Pallas kernels: 24.4 us -> 22.9 us
  local copies, waits for them, and re-layouts: 0.4 us -> 1.59 us
  waiting for transfers between devices: 21.6 us -> 22.7 us
    all_gather x1 -> x0, blocking collectives: 16.3 us -> none  [on_device(): lax.all_gather(block, 'wave', axis=0)]
    all_to_all x1 -> x2, starting transfers between devices: 10.2 us -> 12.6 us  [the longest x1 6.55 us: on_device(): index = lax.all_to_all(own, 'wave', 0, 0, tiled=True)[:, 0]]
    pallas_call x2, Pallas kernels: 10.5 us -> 9.25 us  [the longest x1 7.58 us: wave_tables(): pl.pallas_call(table_kernel, out_shape=pltpu.HBM((chunks, 2, 2, total, CH...]
    broadcast_in_dim x1 -> x3, local copies, waits for them, and re-layouts: 0.01 us -> 1.21 us  [the longest x1 0.61 us: on_device(): own = jnp.broadcast_to(own, (devices, 1) + own.shape)]
    all_to_all x1 -> x2, waiting for transfers between devices: 21.6 us -> 22.7 us  [the longest x1 22.7 us: on_device(): lax.all_to_all(picked.reshape(devices, slots, 2, 2, pairs, width), 'wave'...]
  transfers between devices with their start and end apart: 1 -> 2, of which waited for: 1 -> 1; matrix products, arithmetic and copies ran while one was open for 0% -> 0% of each run, Pallas kernels for 12% -> 26%
where the time goes in v8:
time: 60.9 us; the launch traced here: 60.6 us
  Pallas kernels  22.9 us (38%)
  waiting for transfers between devices  22.7 us (37%)
  starting transfers between devices  12.6 us (21%)
  local copies, waits for them, and re-layouts  1.59 us (3%)
  other arithmetic  0.76 us (1%)
    all_to_all x1, waiting for transfers between devices, on_device(): lax.all_to_all(picked.reshape(devices, slots, 2, 2, pairs, width), 'wave'...  22.7 us
    pallas_call x1, Pallas kernels, legendre_stage(): pl.pallas_call(legendre_kernel, out_shape=pltpu.VMEM((2, 2 * lats * pairs...  8.35 us
    pallas_call x1, Pallas kernels, wave_tables(): pl.pallas_call(table_kernel, out_shape=pltpu.HBM((chunks, 2, 2, total, CH...  7.58 us
    all_to_all x1, starting transfers between devices, on_device(): index = lax.all_to_all(own, 'wave', 0, 0, tiled=True)[:, 0]  6.55 us
    all_to_all x1, starting transfers between devices, on_device(): lax.all_to_all(picked.reshape(devices, slots, 2, 2, pairs, width), 'wave'...  6.03 us
    pallas_call x1, Pallas kernels, fourier_stage(): pl.pallas_call(fourier_kernel, out_shape=jax.ShapeDtypeStruct((rows, NLON...  5.3 us
    pallas_call x1, Pallas kernels, pick_latitudes(): pl.pallas_call(pick_kernel, out_shape=pltpu.HBM(shape, jnp.bfloat16), gri...  1.67 us
  transfers between devices with their start and end apart: 2, of which 1 were waited for; matrix products, arithmetic and copies ran while one was open for 0% of the time, Pallas kernels for 26%

profile of v8, /device:TPU:13, one launch (start us, length us, event | category | flops | bytes accessed | tf_op | source)
XLA Modules:
  0.0 60.6 jit_solution(8044586733019582062)
XLA Ops:
  0.0 0.7 %pad_add_fusion = s32[128]{0:T(128)S(1)} fusion(s32[86]{0:T(128)S(1)} %broadcast_in_dim.22, s32[2]{0:T(128)} %param.7, s32[40]{0:T(128)} %waves_hbm.1), kind=kLoop, calls=%fused_computation.13 | loop fusion | flops 256 | bytes 1024 | tf_op jit(solution)/shard_map/concatenate | solution.py:323
  0.7 0.6 %broadcast_in_dim.23 = s32[16,1,128]{2,1,0:T(1,128)} broadcast(s32[128]{0:T(128)S(1)} %pad_add_fusion), dimensions={2} | broadcast | bytes 8704 | tf_op jit(solution)/shard_map/broadcast_in_dim | solution.py:324
  1.4 6.6 %all-to-all-start = ((s32[16,1,128]{2,1,0:T(1,128)}), s32[16,1,128]{2,1,0:T(1,128)S(1)}, u32[]{:S(2)}, u32[]{:S(2)}) async-start(s32[16,1,128]{2,1,0:T(1,128)} %broadcast_in_dim.23), calls=%async_computation | async-start | bytes 16384 | tf_op jit(solution)/shard_map/all_to_all | solution.py:325
  7.9 8.4 %legendre.1.rows_ref = f32[2,2560,128]{2,1,0:T(8,128)S(1)} custom-call(s32[40]{0:T(128)} %waves_hbm.1, bf16[641,40,128]{2,1,0:T(8,128)(2,1)} %bitcast.5, bf16[40,640,128]{2,1,0:T(8,128)(2,1)} %so_hbm.1, bf16[40,32,641]{2,1,0:T(8,128)(2,1)} %le_hbm.1, bf16[40,32,640]{2,1,0:T(8,128)(2,1)} %lo_hbm.1), custom_call_target="tpu_custom_call" | custom-call | flops 1679032320 | bytes 16396800 | tf_op jit(solution)/shard_map/legendre/pallas_call | solution.py:107
  16.3 0.0 all-to-all-done
  16.3 0.1 slice.8
  16.4 0.1 reshape.13.bands_ref
  16.4 1.7 %pick.1 = bf16[32,2,2,40,128]{4,3,2,1,0:T(8,128)(2,1)} custom-call(s32[32]{0:T(128)S(1)} %reshape.13.bands_ref, f32[2,2560,128]{2,1,0:T(8,128)S(1)} %legendre.1.rows_ref), custom_call_target="tpu_custom_call" | custom-call | tf_op jit(solution)/shard_map/pick/pallas_call | solution.py:160
  18.1 6.0 %all-to-all-start.1 = ((bf16[16,2,2,2,40,128]{5,4,3,2,1,0:T(8,128)(2,1)}), bf16[16,2,2,2,40,128]{5,4,3,2,1,0:T(8,128)(2,1)S(1)}, u32[]{:S(2)}, u32[]{:S(2)}) async-start(bf16[16,2,2,2,40,128]{5,4,3,2,1,0:T(8,128)(2,1)} %bitcast.6), calls=%async_computation.1 | async-start | bytes 2621440 | tf_op jit(solution)/shard_map/all_to_all | solution.py:330
  24.2 0.1 reshape.15
  24.2 0.1 broadcast_in_dim.27.waves_ref
  24.4 7.6 %tables.1.table_hbm = bf16[3,2,2,640,256]{4,3,2,1,0:T(8,128)(2,1)} custom-call(s32[640,128]{1,0:T(8,128)S(1)} %broadcast_in_dim.27.waves_ref), custom_call_target="tpu_custom_call" | custom-call | flops 6881280 | bytes 3440640 | tf_op jit(solution)/shard_map/tables/pallas_call | solution.py:207
  32.0 22.7 %all-to-all-done.1.arrived_ref = bf16[16,2,2,2,40,128]{5,4,3,2,1,0:T(8,128)(2,1)S(1)} async-done(((bf16[16,2,2,2,40,128]{5,4,3,2,1,0:T(8,128)(2,1)}), bf16[16,2,2,2,40,128]{5,4,3,2,1,0:T(8,128)(2,1)S(1)}, u32[]{:S(2)}, u32[]{:S(2)}) %all-to-all-start.1) | async-done | bytes 1310752 | tf_op jit(solution)/shard_map/all_to_all | solution.py:330
  54.7 0.6 broadcast_in_dim.26.sign_hbm
  55.3 5.3 %fourier.1 = bf16[256,2688]{1,0:T(8,128)(2,1)} custom-call(bf16[16,2,2,2,40,128]{5,4,3,2,1,0:T(8,128)(2,1)S(1)} %all-to-all-done.1.arrived_ref, f32[8,640]{1,0:T(8,128)} %broadcast_in_dim.26.sign_hbm, bf16[3,2,2,640,256]{4,3,2,1,0:T(8,128)(2,1)} %tables.1.table_hbm), custom_call_target="tpu_custom_call" | custom-call | flops 1761607680 | bytes 3440640 | tf_op jit(solution)/shard_map/fourier/pallas_call | solution.py:286
  (2 shorter events, 0.0 us)
Async XLA Ops:
  1.4 14.9 %all-to-all-start = ((s32[16,1,128]{2,1,0:T(1,128)}), s32[16,1,128]{2,1,0:T(1,128)S(1)}, u32[]{:S(2)}, u32[]{:S(2)}) async-start(s32[16,1,128]{2,1,0:T(1,128)} %broadcast_in_dim.23), calls=%async_computation | async-start | bytes 16384 | tf_op jit(solution)/shard_map/all_to_all | solution.py:325
  18.1 36.6 %all-to-all-start.1 = ((bf16[16,2,2,2,40,128]{5,4,3,2,1,0:T(8,128)(2,1)}), bf16[16,2,2,2,40,128]{5,4,3,2,1,0:T(8,128)(2,1)S(1)}, u32[]{:S(2)}, u32[]{:S(2)}) async-start(bf16[16,2,2,2,40,128]{5,4,3,2,1,0:T(8,128)(2,1)} %bitcast.6), calls=%async_computation.1 | async-start | bytes 2621440 | tf_op jit(solution)/shard_map/all_to_all | solution.py:330

commit v9 on v8

--- a/solution.py
+++ b/solution.py
@@ -50,15 +50,13 @@
             copy.start()
     wave_copy.wait()
 
-    ids_e = lax.broadcasted_iota(jnp.int32, (lats, he), 1)
-    ids_o = lax.broadcasted_iota(jnp.int32, (lats, ho), 1)
+    ids_e = lax.broadcasted_iota(jnp.int32, (1, he), 1)
+    ids_o = lax.broadcasted_iota(jnp.int32, (1, ho), 1)
 
     def split(panel, ids, count):
-        in_low = ids < count
-        zero = jnp.zeros_like(panel)
-        lower = jnp.where(in_low, panel, zero)
-        upper = jnp.where(in_low, zero, panel)
-        return jnp.concatenate([lower, upper], axis=0)
+        in_low = jnp.where(ids < count, 1.0, 0.0).astype(jnp.bfloat16)
+        lower = panel * in_low
+        return jnp.concatenate([lower, panel - lower], axis=0)
 
     @pl.loop(0, groups)
     def _(g):
@@ -206,11 +204,11 @@
     chunks = pl.cdiv(QUARTER, CHUNK)
     return pl.pallas_call(
         table_kernel,
-        out_shape=pltpu.HBM((chunks, 2, 2, total, CHUNK), jnp.bfloat16),
+        out_shape=jax.ShapeDtypeStruct((chunks, 2, 2, total, CHUNK), jnp.bfloat16),
         grid=(total // rows,),
         in_specs=[pl.BlockSpec((rows, LANES), lambda i: (i, 0))],
         out_specs=pl.BlockSpec((chunks, 2, 2, rows, CHUNK), lambda i: (0, 0, 0, i, 0)),
-        compiler_params=pltpu.CompilerParams(vmem_limit_bytes=32 * 1024 * 1024),
+        compiler_params=pltpu.CompilerParams(vmem_limit_bytes=16 * 1024 * 1024),
         cost_estimate=pl.CostEstimate(
             flops=16 * total * QUARTER, bytes_accessed=8 * total * QUARTER, transcendentals=8 * total * LANES
         ),
@@ -219,7 +217,7 @@
 
 
 def fourier_kernel(
-    arrived_ref, sign_hbm, table_hbm, out_hbm, left_ref, sign_ref, table_ref, row_ref, sems, sign_sem, out_sems
+    arrived_ref, table_ref, sign_hbm, out_hbm, left_ref, sign_ref, row_ref, sign_sem, out_sems
 ):
     devices, slots, _, _, pairs, width = arrived_ref.shape
     fields = width // 2
@@ -227,13 +225,8 @@
     chunks = table_ref.shape[0]
     rows = 2 * fields
 
-    def load(i):
-        return pltpu.make_async_copy(table_hbm.at[i], table_ref.at[i], sems.at[i])
-
     sign_copy = pltpu.make_async_copy(sign_hbm, sign_ref, sign_sem)
     sign_copy.start()
-    for i in range(chunks):
-        load(i).start()
 
     stores = []
     for s in range(slots):
@@ -257,8 +250,6 @@
             left_ref[s, w, at, total:] = -re if w else im
         base = slice(s * rows, (s + 1) * rows)
         for i in range(chunks):
-            if s == 0:
-                load(i).wait()
             lo, hi = i * CHUNK, min((i + 1) * CHUNK, QUARTER)
             e, o = [
                 jnp.dot(
@@ -286,23 +277,21 @@
     out = pl.pallas_call(
         fourier_kernel,
         out_shape=jax.ShapeDtypeStruct((rows, NLON), jnp.bfloat16),
-        in_specs=[pl.BlockSpec(memory_space=pltpu.VMEM)] + [pl.BlockSpec(memory_space=pl.ANY)] * 2,
+        in_specs=[pl.BlockSpec(memory_space=pltpu.VMEM)] * 2 + [pl.BlockSpec(memory_space=pl.ANY)],
         out_specs=pl.BlockSpec(memory_space=pl.ANY),
         scratch_shapes=[
             pltpu.VMEM((slots, 2, 4 * fields, 2 * total), jnp.bfloat16),
             pltpu.VMEM(sign.shape, jnp.float32),
-            pltpu.VMEM(table.shape, jnp.bfloat16),
             pltpu.VMEM((rows, NLON), jnp.bfloat16),
-            pltpu.SemaphoreType.DMA((table.shape[0],)),
             pltpu.SemaphoreType.DMA,
             pltpu.SemaphoreType.DMA((slots,)),
         ],
-        compiler_params=pltpu.CompilerParams(vmem_limit_bytes=32 * 1024 * 1024),
+        compiler_params=pltpu.CompilerParams(vmem_limit_bytes=16 * 1024 * 1024),
         cost_estimate=pl.CostEstimate(
             flops=16 * rows * total * QUARTER, bytes_accessed=8 * total * QUARTER, transcendentals=0
         ),
         name="fourier",
-    )(arrived, in_hbm(sign), in_hbm(table))
+    )(arrived, table, in_hbm(sign))
     return out.reshape(slots, 2, fields, NLON)
 
 
@@ -330,7 +319,7 @@
     arrived = lax.all_to_all(picked.reshape(devices, slots, 2, 2, pairs, width), "wave", 0, 0, tiled=True)
     all_pairs = index[:, :pairs].reshape(-1)
     sign = jnp.where(even_wave(all_pairs) % 4 == 0, 1.0, -1.0).astype(jnp.float32)
-    sign = jnp.broadcast_to(sign, (ROWS,) + sign.shape)
+    sign, all_pairs = lax.optimization_barrier((jnp.broadcast_to(sign, (ROWS,) + sign.shape), all_pairs))
     return fourier_stage(arrived, sign, wave_tables(all_pairs))
 
 

time: 60.9 us -> 61.1 us (level)
  local copies, waits for them, and re-layouts: 1.59 us -> 5.56 us
  Pallas kernels: 22.9 us -> 20.6 us
  waiting for transfers between devices: 22.7 us -> 21.2 us
    unnamed x0 -> x4, local copies, waits for them, and re-layouts: none -> 3.97 us
    all_to_all x1, waiting for transfers between devices: 22.7 us -> 21.2 us  [on_device(): lax.all_to_all(picked.reshape(devices, slots, 2, 2, pairs, width), 'wave'...]
    pallas_call x1, Pallas kernels: 5.3 us -> 3.91 us  [fourier_stage(): pl.pallas_call(fourier_kernel, out_shape=jax.ShapeDtypeStruct((rows, NLON...]
    pallas_call x1, Pallas kernels: 7.58 us -> 6.64 us  [wave_tables(): pl.pallas_call(table_kernel, out_shape=jax.ShapeDtypeStruct((chunks, 2, 2...]
  transfers between devices with their start and end apart: 2 -> 2, of which waited for: 1 -> 1; matrix products, arithmetic and copies ran while one was open for 0% -> 1% of each run, Pallas kernels for 26% -> 25%
where the time goes in v9:
time: 61.1 us; the launch traced here: 60.7 us
  waiting for transfers between devices  21.2 us (35%)
  Pallas kernels  20.6 us (34%)
  starting transfers between devices  12.6 us (21%)
  local copies, waits for them, and re-layouts  5.56 us (9%)
  other arithmetic  0.76 us (1%)
    all_to_all x1, waiting for transfers between devices, on_device(): lax.all_to_all(picked.reshape(devices, slots, 2, 2, pairs, width), 'wave'...  21.2 us
    pallas_call x1, Pallas kernels, legendre_stage(): pl.pallas_call(legendre_kernel, out_shape=pltpu.VMEM((2, 2 * lats * pairs...  8.35 us
    pallas_call x1, Pallas kernels, wave_tables(): pl.pallas_call(table_kernel, out_shape=jax.ShapeDtypeStruct((chunks, 2, 2...  6.64 us
    all_to_all x1, starting transfers between devices, on_device(): index = lax.all_to_all(own, 'wave', 0, 0, tiled=True)[:, 0]  6.55 us
    all_to_all x1, starting transfers between devices, on_device(): lax.all_to_all(picked.reshape(devices, slots, 2, 2, pairs, width), 'wave'...  6.03 us
    unnamed x4, local copies, waits for them, and re-layouts  3.97 us
    pallas_call x1, Pallas kernels, fourier_stage(): pl.pallas_call(fourier_kernel, out_shape=jax.ShapeDtypeStruct((rows, NLON...  3.91 us
    pallas_call x1, Pallas kernels, pick_latitudes(): pl.pallas_call(pick_kernel, out_shape=pltpu.HBM(shape, jnp.bfloat16), gri...  1.67 us
  transfers between devices with their start and end apart: 2, of which 1 were waited for; matrix products, arithmetic and copies ran while one was open for 1% of the time, Pallas kernels for 25%

profile of v9, /device:TPU:13, one launch (start us, length us, event | category | flops | bytes accessed | tf_op | source)
XLA Modules:
  0.0 60.7 jit_solution(15826590981467899045)
XLA Ops:
  0.0 0.7 %pad_add_fusion = s32[128]{0:T(128)S(1)} fusion(s32[86]{0:T(128)S(1)} %broadcast_in_dim.23, s32[2]{0:T(128)} %param.7, s32[40]{0:T(128)} %waves_hbm.1), kind=kLoop, calls=%fused_computation.13 | loop fusion | flops 256 | bytes 1024 | tf_op jit(solution)/shard_map/concatenate | solution.py:312
  0.7 0.6 broadcast_in_dim.24
  1.4 6.6 %all-to-all-start = ((s32[16,1,128]{2,1,0:T(1,128)}), s32[16,1,128]{2,1,0:T(1,128)S(1)}, u32[]{:S(2)}, u32[]{:S(2)}) async-start(s32[16,1,128]{2,1,0:T(1,128)} %broadcast_in_dim.24), calls=%async_computation | async-start | bytes 16384 | tf_op jit(solution)/shard_map/all_to_all | solution.py:314
  7.9 8.4 %legendre.1.rows_ref = f32[2,2560,128]{2,1,0:T(8,128)S(1)} custom-call(s32[40]{0:T(128)} %waves_hbm.1, bf16[641,40,128]{2,1,0:T(8,128)(2,1)} %bitcast.5, bf16[40,640,128]{2,1,0:T(8,128)(2,1)} %so_hbm.1, bf16[40,32,641]{2,1,0:T(8,128)(2,1)} %le_hbm.1, bf16[40,32,640]{2,1,0:T(8,128)(2,1)} %lo_hbm.1), custom_call_target="tpu_custom_call" | custom-call | flops 1679032320 | bytes 16396800 | tf_op jit(solution)/shard_map/legendre/pallas_call | solution.py:105
  16.3 0.0 all-to-all-done
  16.3 0.1 slice.8
  16.4 0.1 reshape.13.bands_ref
  16.4 1.7 %pick.1 = bf16[32,2,2,40,128]{4,3,2,1,0:T(8,128)(2,1)} custom-call(s32[32]{0:T(128)S(1)} %reshape.13.bands_ref, f32[2,2560,128]{2,1,0:T(8,128)S(1)} %legendre.1.rows_ref), custom_call_target="tpu_custom_call" | custom-call | tf_op jit(solution)/shard_map/pick/pallas_call | solution.py:158
  18.1 6.0 %all-to-all-start.1 = ((bf16[16,2,2,2,40,128]{5,4,3,2,1,0:T(8,128)(2,1)}), bf16[16,2,2,2,40,128]{5,4,3,2,1,0:T(8,128)(2,1)S(1)}, u32[]{:S(2)}, u32[]{:S(2)}) async-start(bf16[16,2,2,2,40,128]{5,4,3,2,1,0:T(8,128)(2,1)} %bitcast.6), calls=%async_computation.1 | async-start | bytes 2621440 | tf_op jit(solution)/shard_map/all_to_all | solution.py:319
  24.2 0.1 reshape.15
  24.3 0.6 %broadcast_in_dim.27.sign_hbm = f32[8,640]{1,0:T(8,128)} broadcast(f32[640]{0:T(1024)S(1)} %fusion.4), dimensions={1} | broadcast | bytes 23040 | tf_op jit(solution)/shard_map/broadcast_in_dim | solution.py:322
  24.9 0.1 broadcast_in_dim.28.waves_ref
  25.0 6.6 %tables.1.table_ref = bf16[3,2,2,640,256]{4,3,2,1,0:T(8,128)(2,1)S(1)} custom-call(s32[640,128]{1,0:T(8,128)S(1)} %broadcast_in_dim.28.waves_ref), custom_call_target="tpu_custom_call" | custom-call | flops 6881280 | bytes 3440640 | tf_op jit(solution)/shard_map/tables/pallas_call | solution.py:205
  31.7 0.0 copy-start
  31.7 1.9 %copy-done = bf16[3,2,2,640,256]{4,3,2,1,0:T(8,128)(2,1)} copy-done((bf16[3,2,2,640,256]{4,3,2,1,0:T(8,128)(2,1)}, bf16[3,2,2,640,256]{4,3,2,1,0:T(8,128)(2,1)S(1)}, u32[]{:S(2)}) %copy-start) | copy-done | bytes 3932184
  33.5 21.2 %all-to-all-done.1.arrived_ref = bf16[16,2,2,2,40,128]{5,4,3,2,1,0:T(8,128)(2,1)S(1)} async-done(((bf16[16,2,2,2,40,128]{5,4,3,2,1,0:T(8,128)(2,1)}), bf16[16,2,2,2,40,128]{5,4,3,2,1,0:T(8,128)(2,1)S(1)}, u32[]{:S(2)}, u32[]{:S(2)}) %all-to-all-start.1) | async-done | bytes 1310752 | tf_op jit(solution)/shard_map/all_to_all | solution.py:319
  54.7 0.0 copy-start.1
  54.7 2.1 %copy-done.1 = bf16[3,2,2,640,256]{4,3,2,1,0:T(8,128)(2,1)S(1)} copy-done((bf16[3,2,2,640,256]{4,3,2,1,0:T(8,128)(2,1)S(1)}, bf16[3,2,2,640,256]{4,3,2,1,0:T(8,128)(2,1)}, u32[]{:S(2)}) %copy-start.1) | copy-done | bytes 3932184
  56.8 3.9 %fourier.1 = bf16[256,2688]{1,0:T(8,128)(2,1)} custom-call(bf16[16,2,2,2,40,128]{5,4,3,2,1,0:T(8,128)(2,1)S(1)} %all-to-all-done.1.arrived_ref, bf16[3,2,2,640,256]{4,3,2,1,0:T(8,128)(2,1)S(1)} %copy-done.1, f32[8,640]{1,0:T(8,128)} %broadcast_in_dim.27.sign_hbm), custom_call_target="tpu_custom_call" | custom-call | flops 1761607680 | bytes 3440640 | tf_op jit(solution)/shard_map/fourier/pallas_call | solution.py:277
  (2 shorter events, 0.0 us)
Async XLA Ops:
  1.4 14.9 %all-to-all-start = ((s32[16,1,128]{2,1,0:T(1,128)}), s32[16,1,128]{2,1,0:T(1,128)S(1)}, u32[]{:S(2)}, u32[]{:S(2)}) async-start(s32[16,1,128]{2,1,0:T(1,128)} %broadcast_in_dim.24), calls=%async_computation | async-start | bytes 16384 | tf_op jit(solution)/shard_map/all_to_all | solution.py:314
  18.1 36.6 %all-to-all-start.1 = ((bf16[16,2,2,2,40,128]{5,4,3,2,1,0:T(8,128)(2,1)}), bf16[16,2,2,2,40,128]{5,4,3,2,1,0:T(8,128)(2,1)S(1)}, u32[]{:S(2)}, u32[]{:S(2)}) async-start(bf16[16,2,2,2,40,128]{5,4,3,2,1,0:T(8,128)(2,1)} %bitcast.6), calls=%async_computation.1 | async-start | bytes 2621440 | tf_op jit(solution)/shard_map/all_to_all | solution.py:319
  31.7 1.9 %copy-start = (bf16[3,2,2,640,256]{4,3,2,1,0:T(8,128)(2,1)}, bf16[3,2,2,640,256]{4,3,2,1,0:T(8,128)(2,1)S(1)}, u32[]{:S(2)}) copy-start(bf16[3,2,2,640,256]{4,3,2,1,0:T(8,128)(2,1)S(1)} %tables.1.table_ref) | copy-start | bytes 11796484
  54.7 2.1 %copy-start.1 = (bf16[3,2,2,640,256]{4,3,2,1,0:T(8,128)(2,1)S(1)}, bf16[3,2,2,640,256]{4,3,2,1,0:T(8,128)(2,1)}, u32[]{:S(2)}) copy-start(bf16[3,2,2,640,256]{4,3,2,1,0:T(8,128)(2,1)} %copy-done) | copy-start | bytes 11796484

commit v10 on v9

--- a/solution.py
+++ b/solution.py
@@ -174,7 +174,7 @@
     return jnp.where(low % 2 == 0, low, M - 1 - low)
 
 
-def table_kernel(waves_ref, out_ref):
+def table_kernel(waves_ref, first_ref, rest_ref):
     even = even_wave(waves_ref[...])
     odd = M - 1 - even
     lane = lax.broadcasted_iota(jnp.int32, even.shape, 1).astype(jnp.float32)
@@ -193,21 +193,28 @@
         dc, ds = jnp.cos(step), jnp.sin(step)
         for b in range(0, QUARTER, LANES):
             at = slice(b % CHUNK, b % CHUNK + LANES)
-            out_ref[b // CHUNK, w, 0, :, at] = c.astype(jnp.bfloat16)
-            out_ref[b // CHUNK, w, 1, :, at] = s.astype(jnp.bfloat16)
+            out_ref = rest_ref.at[b // CHUNK - 1] if b >= CHUNK else first_ref
+            out_ref[w, 0, :, at] = c.astype(jnp.bfloat16)
+            out_ref[w, 1, :, at] = s.astype(jnp.bfloat16)
             c, s = c * dc + s * ds, s * dc - c * ds
 
 
 def wave_tables(waves):
     total = waves.shape[0]
     rows = 64
-    chunks = pl.cdiv(QUARTER, CHUNK)
+    rest = pl.cdiv(QUARTER, CHUNK) - 1
     return pl.pallas_call(
         table_kernel,
-        out_shape=jax.ShapeDtypeStruct((chunks, 2, 2, total, CHUNK), jnp.bfloat16),
+        out_shape=[
+            jax.ShapeDtypeStruct((2, 2, total, CHUNK), jnp.bfloat16),
+            pltpu.HBM((rest, 2, 2, total, CHUNK), jnp.bfloat16),
+        ],
         grid=(total // rows,),
         in_specs=[pl.BlockSpec((rows, LANES), lambda i: (i, 0))],
-        out_specs=pl.BlockSpec((chunks, 2, 2, rows, CHUNK), lambda i: (0, 0, 0, i, 0)),
+        out_specs=[
+            pl.BlockSpec((2, 2, rows, CHUNK), lambda i: (0, 0, i, 0)),
+            pl.BlockSpec((rest, 2, 2, rows, CHUNK), lambda i: (0, 0, 0, i, 0)),
+        ],
         compiler_params=pltpu.CompilerParams(vmem_limit_bytes=16 * 1024 * 1024),
         cost_estimate=pl.CostEstimate(
             flops=16 * total * QUARTER, bytes_accessed=8 * total * QUARTER, transcendentals=8 * total * LANES
@@ -217,16 +224,22 @@
 
 
 def fourier_kernel(
-    arrived_ref, table_ref, sign_hbm, out_hbm, left_ref, sign_ref, row_ref, sign_sem, out_sems
+    arrived_ref, first_ref, rest_hbm, sign_hbm, out_hbm,
+    left_ref, rest_ref, sign_ref, row_ref, sems, sign_sem, out_sems,
 ):
     devices, slots, _, _, pairs, width = arrived_ref.shape
     fields = width // 2
     total = devices * pairs
-    chunks = table_ref.shape[0]
+    chunks = 1 + rest_ref.shape[0]
     rows = 2 * fields
+
+    def load(i):
+        return pltpu.make_async_copy(rest_hbm.at[i - 1], rest_ref.at[i - 1], sems.at[i - 1])
 
     sign_copy = pltpu.make_async_copy(sign_hbm, sign_ref, sign_sem)
     sign_copy.start()
+    for i in range(1, chunks):
+        load(i).start()
 
     stores = []
     for s in range(slots):
@@ -250,11 +263,14 @@
             left_ref[s, w, at, total:] = -re if w else im
         base = slice(s * rows, (s + 1) * rows)
         for i in range(chunks):
+            if s == 0 and i > 0:
+                load(i).wait()
+            table_ref = rest_ref.at[i - 1] if i else first_ref
             lo, hi = i * CHUNK, min((i + 1) * CHUNK, QUARTER)
             e, o = [
                 jnp.dot(
                     left_ref[s, w],
-                    table_ref[i, w].reshape(2 * total, CHUNK),
+                    table_ref[w].reshape(2 * total, CHUNK),
                     preferred_element_type=jnp.float32,
                 )[:, : hi - lo]
                 for w in range(2)
@@ -269,7 +285,7 @@
         copy.wait()
 
 
-def fourier_stage(arrived, sign, table):
+def fourier_stage(arrived, sign, first, rest):
     devices, slots, _, _, pairs, width = arrived.shape
     fields = width // 2
     total = devices * pairs
@@ -277,12 +293,14 @@
     out = pl.pallas_call(
         fourier_kernel,
         out_shape=jax.ShapeDtypeStruct((rows, NLON), jnp.bfloat16),
-        in_specs=[pl.BlockSpec(memory_space=pltpu.VMEM)] * 2 + [pl.BlockSpec(memory_space=pl.ANY)],
+        in_specs=[pl.BlockSpec(memory_space=pltpu.VMEM)] * 2 + [pl.BlockSpec(memory_space=pl.ANY)] * 2,
         out_specs=pl.BlockSpec(memory_space=pl.ANY),
         scratch_shapes=[
             pltpu.VMEM((slots, 2, 4 * fields, 2 * total), jnp.bfloat16),
+            pltpu.VMEM(rest.shape, jnp.bfloat16),
             pltpu.VMEM(sign.shape, jnp.float32),
             pltpu.VMEM((rows, NLON), jnp.bfloat16),
+            pltpu.SemaphoreType.DMA((rest.shape[0],)),
             pltpu.SemaphoreType.DMA,
             pltpu.SemaphoreType.DMA((slots,)),
         ],
@@ -291,7 +309,7 @@
             flops=16 * rows * total * QUARTER, bytes_accessed=8 * total * QUARTER, transcendentals=0
         ),
         name="fourier",
-    )(arrived, table, in_hbm(sign))
+    )(arrived, first, in_hbm(rest), in_hbm(sign))
     return out.reshape(slots, 2, fields, NLON)
 
 
@@ -320,7 +338,7 @@
     all_pairs = index[:, :pairs].reshape(-1)
     sign = jnp.where(even_wave(all_pairs) % 4 == 0, 1.0, -1.0).astype(jnp.float32)
     sign, all_pairs = lax.optimization_barrier((jnp.broadcast_to(sign, (ROWS,) + sign.shape), all_pairs))
-    return fourier_stage(arrived, sign, wave_tables(all_pairs))
+    return fourier_stage(arrived, sign, *wave_tables(all_pairs))
 
 
 def solution(mesh):

time: 61.1 us -> 59.9 us (0.980)
  local copies, waits for them, and re-layouts: 5.56 us -> 1.59 us
  Pallas kernels: 20.6 us -> 22.4 us
  waiting for transfers between devices: 21.2 us -> 22.2 us
    unnamed x4 -> x0, local copies, waits for them, and re-layouts: 3.97 us -> none
    all_to_all x1, waiting for transfers between devices: 21.2 us -> 22.2 us  [on_device(): lax.all_to_all(picked.reshape(devices, slots, 2, 2, pairs, width), 'wave'...]
    pallas_call x1, Pallas kernels: 3.91 us -> 4.87 us  [fourier_stage(): pl.pallas_call(fourier_kernel, out_shape=jax.ShapeDtypeStruct((rows, NLON...]
    pallas_call x1, Pallas kernels: 6.64 us -> 7.48 us  [wave_tables(): pl.pallas_call(table_kernel, out_shape=[jax.ShapeDtypeStruct((2, 2, total...]
  transfers between devices with their start and end apart: 2 -> 2, of which waited for: 1 -> 1; matrix products, arithmetic and copies ran while one was open for 1% -> 1% of each run, Pallas kernels for 25% -> 27%
where the time goes in v10:
time: 59.9 us; the launch traced here: 59.6 us
  Pallas kernels  22.4 us (37%)
  waiting for transfers between devices  22.2 us (37%)
  starting transfers between devices  12.6 us (21%)
  local copies, waits for them, and re-layouts  1.59 us (3%)
  other arithmetic  0.76 us (1%)
    all_to_all x1, waiting for transfers between devices, on_device(): lax.all_to_all(picked.reshape(devices, slots, 2, 2, pairs, width), 'wave'...  22.2 us
    pallas_call x1, Pallas kernels, legendre_stage(): pl.pallas_call(legendre_kernel, out_shape=pltpu.VMEM((2, 2 * lats * pairs...  8.35 us
    pallas_call x1, Pallas kernels, wave_tables(): pl.pallas_call(table_kernel, out_shape=[jax.ShapeDtypeStruct((2, 2, total...  7.48 us
    all_to_all x1, starting transfers between devices, on_device(): index = lax.all_to_all(own, 'wave', 0, 0, tiled=True)[:, 0]  6.55 us
    all_to_all x1, starting transfers between devices, on_device(): lax.all_to_all(picked.reshape(devices, slots, 2, 2, pairs, width), 'wave'...  6.03 us
    pallas_call x1, Pallas kernels, fourier_stage(): pl.pallas_call(fourier_kernel, out_shape=jax.ShapeDtypeStruct((rows, NLON...  4.87 us
    pallas_call x1, Pallas kernels, pick_latitudes(): pl.pallas_call(pick_kernel, out_shape=pltpu.HBM(shape, jnp.bfloat16), gri...  1.67 us
  transfers between devices with their start and end apart: 2, of which 1 were waited for; matrix products, arithmetic and copies ran while one was open for 1% of the time, Pallas kernels for 27%

profile of v10, /device:TPU:13, one launch (start us, length us, event | category | flops | bytes accessed | tf_op | source)
XLA Modules:
  0.0 59.6 jit_solution(11216634220795205901)
XLA Ops:
  0.0 0.7 %pad_add_fusion = s32[128]{0:T(128)S(1)} fusion(s32[86]{0:T(128)S(1)} %broadcast_in_dim.23, s32[2]{0:T(128)} %param.7, s32[40]{0:T(128)} %waves_hbm.1), kind=kLoop, calls=%fused_computation.13 | loop fusion | flops 256 | bytes 1024 | tf_op jit(solution)/shard_map/concatenate | solution.py:330
  0.7 0.6 %broadcast_in_dim.24 = s32[16,1,128]{2,1,0:T(1,128)} broadcast(s32[128]{0:T(128)S(1)} %pad_add_fusion), dimensions={2} | broadcast | bytes 8704 | tf_op jit(solution)/shard_map/broadcast_in_dim | solution.py:331
  1.4 6.6 %all-to-all-start = ((s32[16,1,128]{2,1,0:T(1,128)}), s32[16,1,128]{2,1,0:T(1,128)S(1)}, u32[]{:S(2)}, u32[]{:S(2)}) async-start(s32[16,1,128]{2,1,0:T(1,128)} %broadcast_in_dim.24), calls=%async_computation | async-start | bytes 16384 | tf_op jit(solution)/shard_map/all_to_all | solution.py:332
  7.9 8.4 %legendre.1.rows_ref = f32[2,2560,128]{2,1,0:T(8,128)S(1)} custom-call(s32[40]{0:T(128)} %waves_hbm.1, bf16[641,40,128]{2,1,0:T(8,128)(2,1)} %bitcast.5, bf16[40,640,128]{2,1,0:T(8,128)(2,1)} %so_hbm.1, bf16[40,32,641]{2,1,0:T(8,128)(2,1)} %le_hbm.1, bf16[40,32,640]{2,1,0:T(8,128)(2,1)} %lo_hbm.1), custom_call_target="tpu_custom_call" | custom-call | flops 1679032320 | bytes 16396800 | tf_op jit(solution)/shard_map/legendre/pallas_call | solution.py:105
  16.3 0.0 all-to-all-done
  16.3 0.1 slice.8
  16.4 0.1 reshape.13.bands_ref
  16.4 1.7 %pick.1 = bf16[32,2,2,40,128]{4,3,2,1,0:T(8,128)(2,1)} custom-call(s32[32]{0:T(128)S(1)} %reshape.13.bands_ref, f32[2,2560,128]{2,1,0:T(8,128)S(1)} %legendre.1.rows_ref), custom_call_target="tpu_custom_call" | custom-call | tf_op jit(solution)/shard_map/pick/pallas_call | solution.py:158
  18.1 6.0 %all-to-all-start.1 = ((bf16[16,2,2,2,40,128]{5,4,3,2,1,0:T(8,128)(2,1)}), bf16[16,2,2,2,40,128]{5,4,3,2,1,0:T(8,128)(2,1)S(1)}, u32[]{:S(2)}, u32[]{:S(2)}) async-start(bf16[16,2,2,2,40,128]{5,4,3,2,1,0:T(8,128)(2,1)} %bitcast.6), calls=%async_computation.1 | async-start | bytes 2621440 | tf_op jit(solution)/shard_map/all_to_all | solution.py:337
  24.2 0.1 reshape.15
  24.3 0.6 %broadcast_in_dim.27.sign_hbm = f32[8,640]{1,0:T(8,128)} broadcast(f32[640]{0:T(1024)S(1)} %fusion.4), dimensions={1} | broadcast | bytes 23040 | tf_op jit(solution)/shard_map/broadcast_in_dim | solution.py:340
  24.9 0.1 broadcast_in_dim.28.waves_ref
  25.0 7.5 %tables.1 = (bf16[2,2,640,256]{3,2,1,0:T(8,128)(2,1)S(1)}, bf16[2,2,2,640,256]{4,3,2,1,0:T(8,128)(2,1)}) custom-call(s32[640,128]{1,0:T(8,128)S(1)} %broadcast_in_dim.28.waves_ref), custom_call_target="tpu_custom_call" | custom-call | flops 6881280 | bytes 3440640 | tf_op jit(solution)/shard_map/tables/pallas_call | solution.py:206
  32.5 22.2 %all-to-all-done.1.arrived_ref = bf16[16,2,2,2,40,128]{5,4,3,2,1,0:T(8,128)(2,1)S(1)} async-done(((bf16[16,2,2,2,40,128]{5,4,3,2,1,0:T(8,128)(2,1)}), bf16[16,2,2,2,40,128]{5,4,3,2,1,0:T(8,128)(2,1)S(1)}, u32[]{:S(2)}, u32[]{:S(2)}) %all-to-all-start.1) | async-done | bytes 1310752 | tf_op jit(solution)/shard_map/all_to_all | solution.py:337
  54.7 4.9 %fourier.1 = bf16[256,2688]{1,0:T(8,128)(2,1)} custom-call(bf16[16,2,2,2,40,128]{5,4,3,2,1,0:T(8,128)(2,1)S(1)} %all-to-all-done.1.arrived_ref, bf16[2,2,640,256]{3,2,1,0:T(8,128)(2,1)S(1)} %get-tuple-element.14.first_ref, bf16[2,2,2,640,256]{4,3,2,1,0:T(8,128)(2,1)} %get-tuple-element.15.rest_hbm, f32[8,640]{1,0:T(8,128)} %broadcast_in_dim.27.sign_hbm), custom_call_target="tpu_custom_call" | custom-call | flops 1761607680 | bytes 3440640 | tf_op jit(solution)/shard_map/fourier/pallas_call | solution.py:293
  (2 shorter events, 0.0 us)
Async XLA Ops:
  1.4 14.9 %all-to-all-start = ((s32[16,1,128]{2,1,0:T(1,128)}), s32[16,1,128]{2,1,0:T(1,128)S(1)}, u32[]{:S(2)}, u32[]{:S(2)}) async-start(s32[16,1,128]{2,1,0:T(1,128)} %broadcast_in_dim.24), calls=%async_computation | async-start | bytes 16384 | tf_op jit(solution)/shard_map/all_to_all | solution.py:332
  18.1 36.6 %all-to-all-start.1 = ((bf16[16,2,2,2,40,128]{5,4,3,2,1,0:T(8,128)(2,1)}), bf16[16,2,2,2,40,128]{5,4,3,2,1,0:T(8,128)(2,1)S(1)}, u32[]{:S(2)}, u32[]{:S(2)}) async-start(bf16[16,2,2,2,40,128]{5,4,3,2,1,0:T(8,128)(2,1)} %bitcast.6), calls=%async_computation.1 | async-start | bytes 2621440 | tf_op jit(solution)/shard_map/all_to_all | solution.py:337

commit v11 on v10

--- a/solution.py
+++ b/solution.py
@@ -22,7 +22,7 @@
 
 def legendre_kernel(
     waves_hbm, se_hbm, so_hbm, le_hbm, lo_hbm, out_ref,
-    waves_ref, se_ref, so_ref, le_ref, lo_ref, columns_ref, anti_ref, sems, wave_sem,
+    waves_ref, se_ref, so_ref, le_ref, lo_ref, columns_ref, sym_ref, sems, wave_sem,
 ):
     pairs, lats, he = le_ref.shape
     ho = lo_ref.shape[2]
@@ -46,7 +46,7 @@
     wave_copy.start()
     ahead = 2
     for g in range(min(ahead, groups)):
-        for copy in odd_copies(g) + even_copies(g):
+        for copy in even_copies(g) + odd_copies(g):
             copy.start()
     wave_copy.wait()
 
@@ -61,27 +61,27 @@
     @pl.loop(0, groups)
     def _(g):
         base = pl.multiple_of(g * ROWS, ROWS)
+        for copy in even_copies(g):
+            copy.wait()
+
+        @pl.when(g + ahead < groups)
+        def _():
+            for copy in even_copies(g + ahead) + odd_copies(g + ahead):
+                copy.start()
+
+        columns_ref[...] = se_ref[g].astype(jnp.float32).reshape(columns_ref.shape)
+        for p in range(ROWS):
+            even = split(le_ref[base + p], ids_e, (M - waves_ref[base + p] + 1) // 2)
+            xe = columns_ref[pl.ds(p, he, stride=ROWS), :].astype(jnp.bfloat16)
+            sym_ref[p] = jnp.dot(even, xe, preferred_element_type=jnp.float32)
         for copy in odd_copies(g):
             copy.wait()
-
-        @pl.when(g + ahead < groups)
-        def _():
-            for copy in odd_copies(g + ahead) + even_copies(g + ahead):
-                copy.start()
-
-        for p in range(ROWS):
-            odd = split(lo_ref[base + p], ids_o, (M - waves_ref[base + p]) // 2)
-            anti_ref[p] = jnp.dot(odd, so_ref[base + p], preferred_element_type=jnp.float32)
-        for copy in even_copies(g):
-            copy.wait()
-        columns_ref[...] = se_ref[g].astype(jnp.float32).reshape(columns_ref.shape)
         for p in range(ROWS):
             low = waves_ref[base + p]
             parity = low % 2
-            even = split(le_ref[base + p], ids_e, (M - low + 1) // 2)
-            xe = columns_ref[pl.ds(p, he, stride=ROWS), :].astype(jnp.bfloat16)
-            sym = jnp.dot(even, xe, preferred_element_type=jnp.float32)
-            anti = anti_ref[p]
+            odd = split(lo_ref[base + p], ids_o, (M - low) // 2)
+            anti = jnp.dot(odd, so_ref[base + p], preferred_element_type=jnp.float32)
+            sym = sym_ref[p]
             for h, rows in enumerate((sym + anti, sym - anti)):
                 for w in range(2):
                     start = (parity ^ w) * (lats * pairs) + base + p
@@ -236,6 +236,22 @@
     def load(i):
         return pltpu.make_async_copy(rest_hbm.at[i - 1], rest_ref.at[i - 1], sems.at[i - 1])
 
+    def block(s, i):
+        table_ref = rest_ref.at[i - 1] if i else first_ref
+        lo, hi = i * CHUNK, min((i + 1) * CHUNK, QUARTER)
+        e, o = [
+            jnp.dot(
+                left_ref[s, w],
+                table_ref[w].reshape(2 * total, CHUNK),
+                preferred_element_type=jnp.float32,
+            )[:, : hi - lo]
+            for w in range(2)
+        ]
+        plus, minus = e + o, e - o
+        for k, part in enumerate((plus[:rows], plus[rows:], minus[:rows], minus[rows:])):
+            at = slice(k * QUARTER + lo, k * QUARTER + hi)
+            row_ref[s * rows : (s + 1) * rows, at] = part.astype(jnp.bfloat16)
+
     sign_copy = pltpu.make_async_copy(sign_hbm, sign_ref, sign_sem)
     sign_copy.start()
     for i in range(1, chunks):
@@ -261,23 +277,13 @@
             re, im = signed[:fields], signed[fields:]
             left_ref[s, w, at, :total] = im if w else re
             left_ref[s, w, at, total:] = -re if w else im
+        block(s, 0)
+    for i in range(1, chunks):
+        load(i).wait()
+    for s in range(slots):
+        for i in range(1, chunks):
+            block(s, i)
         base = slice(s * rows, (s + 1) * rows)
-        for i in range(chunks):
-            if s == 0 and i > 0:
-                load(i).wait()
-            table_ref = rest_ref.at[i - 1] if i else first_ref
-            lo, hi = i * CHUNK, min((i + 1) * CHUNK, QUARTER)
-            e, o = [
-                jnp.dot(
-                    left_ref[s, w],
-                    table_ref[w].reshape(2 * total, CHUNK),
-                    preferred_element_type=jnp.float32,
-                )[:, : hi - lo]
-                for w in range(2)
-            ]
-            plus, minus = e + o, e - o
-            for k, part in enumerate((plus[:rows], plus[rows:], minus[:rows], minus[rows:])):
-                row_ref[base, k * QUARTER + lo : k * QUARTER + hi] = part.astype(jnp.bfloat16)
         copy = pltpu.make_async_copy(row_ref.at[base], out_hbm.at[base], out_sems.at[s])
         copy.start()
         stores.append(copy)

time: 59.9 us -> 59.7 us (level)
  no operation moved by 1% of the time
where the time goes in v11:
time: 59.7 us; the launch traced here: 59.4 us
  Pallas kernels  22.2 us (37%)
  waiting for transfers between devices  22.2 us (37%)
  starting transfers between devices  12.6 us (21%)
  local copies, waits for them, and re-layouts  1.59 us (3%)
  other arithmetic  0.76 us (1%)
    all_to_all x1, waiting for transfers between devices, on_device(): lax.all_to_all(picked.reshape(devices, slots, 2, 2, pairs, width), 'wave'...  22.2 us
    pallas_call x1, Pallas kernels, legendre_stage(): pl.pallas_call(legendre_kernel, out_shape=pltpu.VMEM((2, 2 * lats * pairs...  8.44 us
    pallas_call x1, Pallas kernels, wave_tables(): pl.pallas_call(table_kernel, out_shape=[jax.ShapeDtypeStruct((2, 2, total...  7.48 us
    all_to_all x1, starting transfers between devices, on_device(): index = lax.all_to_all(own, 'wave', 0, 0, tiled=True)[:, 0]  6.55 us
    all_to_all x1, starting transfers between devices, on_device(): lax.all_to_all(picked.reshape(devices, slots, 2, 2, pairs, width), 'wave'...  6.03 us
    pallas_call x1, Pallas kernels, fourier_stage(): pl.pallas_call(fourier_kernel, out_shape=jax.ShapeDtypeStruct((rows, NLON...  4.64 us
    pallas_call x1, Pallas kernels, pick_latitudes(): pl.pallas_call(pick_kernel, out_shape=pltpu.HBM(shape, jnp.bfloat16), gri...  1.67 us
  transfers between devices with their start and end apart: 2, of which 1 were waited for; matrix products, arithmetic and copies ran while one was open for 1% of the time, Pallas kernels for 27%

profile of v11, /device:TPU:13, one launch (start us, length us, event | category | flops | bytes accessed | tf_op | source)
XLA Modules:
  0.0 59.4 jit_solution(5032068915963135059)
XLA Ops:
  0.0 0.7 %pad_add_fusion = s32[128]{0:T(128)S(1)} fusion(s32[86]{0:T(128)S(1)} %broadcast_in_dim.23, s32[2]{0:T(128)} %param.7, s32[40]{0:T(128)} %waves_hbm.1), kind=kLoop, calls=%fused_computation.13 | loop fusion | flops 256 | bytes 1024 | tf_op jit(solution)/shard_map/concatenate | solution.py:336
  0.7 0.6 %broadcast_in_dim.24 = s32[16,1,128]{2,1,0:T(1,128)} broadcast(s32[128]{0:T(128)S(1)} %pad_add_fusion), dimensions={2} | broadcast | bytes 8704 | tf_op jit(solution)/shard_map/broadcast_in_dim | solution.py:337
  1.4 6.6 %all-to-all-start = ((s32[16,1,128]{2,1,0:T(1,128)}), s32[16,1,128]{2,1,0:T(1,128)S(1)}, u32[]{:S(2)}, u32[]{:S(2)}) async-start(s32[16,1,128]{2,1,0:T(1,128)} %broadcast_in_dim.24), calls=%async_computation | async-start | bytes 16384 | tf_op jit(solution)/shard_map/all_to_all | solution.py:338
  7.9 8.4 %legendre.1.rows_ref = f32[2,2560,128]{2,1,0:T(8,128)S(1)} custom-call(s32[40]{0:T(128)} %waves_hbm.1, bf16[641,40,128]{2,1,0:T(8,128)(2,1)} %bitcast.5, bf16[40,640,128]{2,1,0:T(8,128)(2,1)} %so_hbm.1, bf16[40,32,641]{2,1,0:T(8,128)(2,1)} %le_hbm.1, bf16[40,32,640]{2,1,0:T(8,128)(2,1)} %lo_hbm.1), custom_call_target="tpu_custom_call" | custom-call | flops 1679032320 | bytes 16396800 | tf_op jit(solution)/shard_map/legendre/pallas_call | solution.py:105
  16.4 0.0 all-to-all-done
  16.4 0.1 slice.8
  16.4 0.1 reshape.13.bands_ref
  16.5 1.7 %pick.1 = bf16[32,2,2,40,128]{4,3,2,1,0:T(8,128)(2,1)} custom-call(s32[32]{0:T(128)S(1)} %reshape.13.bands_ref, f32[2,2560,128]{2,1,0:T(8,128)S(1)} %legendre.1.rows_ref), custom_call_target="tpu_custom_call" | custom-call | tf_op jit(solution)/shard_map/pick/pallas_call | solution.py:158
  18.2 6.0 %all-to-all-start.1 = ((bf16[16,2,2,2,40,128]{5,4,3,2,1,0:T(8,128)(2,1)}), bf16[16,2,2,2,40,128]{5,4,3,2,1,0:T(8,128)(2,1)S(1)}, u32[]{:S(2)}, u32[]{:S(2)}) async-start(bf16[16,2,2,2,40,128]{5,4,3,2,1,0:T(8,128)(2,1)} %bitcast.6), calls=%async_computation.1 | async-start | bytes 2621440 | tf_op jit(solution)/shard_map/all_to_all | solution.py:343
  24.2 0.1 reshape.15
  24.3 0.6 %broadcast_in_dim.27.sign_hbm = f32[8,640]{1,0:T(8,128)} broadcast(f32[640]{0:T(1024)S(1)} %fusion.4), dimensions={1} | broadcast | bytes 23040 | tf_op jit(solution)/shard_map/broadcast_in_dim | solution.py:346
  25.0 0.1 broadcast_in_dim.28.waves_ref
  25.1 7.5 %tables.1 = (bf16[2,2,640,256]{3,2,1,0:T(8,128)(2,1)S(1)}, bf16[2,2,2,640,256]{4,3,2,1,0:T(8,128)(2,1)}) custom-call(s32[640,128]{1,0:T(8,128)S(1)} %broadcast_in_dim.28.waves_ref), custom_call_target="tpu_custom_call" | custom-call | flops 6881280 | bytes 3440640 | tf_op jit(solution)/shard_map/tables/pallas_call | solution.py:206
  32.6 22.2 %all-to-all-done.1.arrived_ref = bf16[16,2,2,2,40,128]{5,4,3,2,1,0:T(8,128)(2,1)S(1)} async-done(((bf16[16,2,2,2,40,128]{5,4,3,2,1,0:T(8,128)(2,1)}), bf16[16,2,2,2,40,128]{5,4,3,2,1,0:T(8,128)(2,1)S(1)}, u32[]{:S(2)}, u32[]{:S(2)}) %all-to-all-start.1) | async-done | bytes 1310752 | tf_op jit(solution)/shard_map/all_to_all | solution.py:343
  54.8 4.6 %fourier.1 = bf16[256,2688]{1,0:T(8,128)(2,1)} custom-call(bf16[16,2,2,2,40,128]{5,4,3,2,1,0:T(8,128)(2,1)S(1)} %all-to-all-done.1.arrived_ref, bf16[2,2,640,256]{3,2,1,0:T(8,128)(2,1)S(1)} %get-tuple-element.14.first_ref, bf16[2,2,2,640,256]{4,3,2,1,0:T(8,128)(2,1)} %get-tuple-element.15.rest_hbm, f32[8,640]{1,0:T(8,128)} %broadcast_in_dim.27.sign_hbm), custom_call_target="tpu_custom_call" | custom-call | flops 1761607680 | bytes 3440640 | tf_op jit(solution)/shard_map/fourier/pallas_call | solution.py:299
  (2 shorter events, 0.0 us)
Async XLA Ops:
  1.4 15.0 %all-to-all-start = ((s32[16,1,128]{2,1,0:T(1,128)}), s32[16,1,128]{2,1,0:T(1,128)S(1)}, u32[]{:S(2)}, u32[]{:S(2)}) async-start(s32[16,1,128]{2,1,0:T(1,128)} %broadcast_in_dim.24), calls=%async_computation | async-start | bytes 16384 | tf_op jit(solution)/shard_map/all_to_all | solution.py:338
  18.2 36.6 %all-to-all-start.1 = ((bf16[16,2,2,2,40,128]{5,4,3,2,1,0:T(8,128)(2,1)}), bf16[16,2,2,2,40,128]{5,4,3,2,1,0:T(8,128)(2,1)S(1)}, u32[]{:S(2)}, u32[]{:S(2)}) async-start(bf16[16,2,2,2,40,128]{5,4,3,2,1,0:T(8,128)(2,1)} %bitcast.6), calls=%async_computation.1 | async-start | bytes 2621440 | tf_op jit(solution)/shard_map/all_to_all | solution.py:343

commit v12 on v11

--- a/solution.py
+++ b/solution.py
@@ -58,6 +58,15 @@
         lower = panel * in_low
         return jnp.concatenate([lower, panel - lower], axis=0)
 
+    def both(panels, spectra):
+        rows, width = panels[0].shape[0], spectra[0].shape[1]
+        product = jnp.dot(
+            jnp.concatenate(panels, axis=0),
+            jnp.concatenate(spectra, axis=1),
+            preferred_element_type=jnp.float32,
+        )
+        return product[:rows, :width], product[rows:, width:]
+
     @pl.loop(0, groups)
     def _(g):
         base = pl.multiple_of(g * ROWS, ROWS)
@@ -70,22 +79,23 @@
                 copy.start()
 
         columns_ref[...] = se_ref[g].astype(jnp.float32).reshape(columns_ref.shape)
-        for p in range(ROWS):
-            even = split(le_ref[base + p], ids_e, (M - waves_ref[base + p] + 1) // 2)
-            xe = columns_ref[pl.ds(p, he, stride=ROWS), :].astype(jnp.bfloat16)
-            sym_ref[p] = jnp.dot(even, xe, preferred_element_type=jnp.float32)
+        for p in range(0, ROWS, 2):
+            even = [split(le_ref[base + q], ids_e, (M - waves_ref[base + q] + 1) // 2) for q in (p, p + 1)]
+            xe = [columns_ref[pl.ds(q, he, stride=ROWS), :].astype(jnp.bfloat16) for q in (p, p + 1)]
+            sym_ref[p], sym_ref[p + 1] = both(even, xe)
         for copy in odd_copies(g):
             copy.wait()
-        for p in range(ROWS):
-            low = waves_ref[base + p]
-            parity = low % 2
-            odd = split(lo_ref[base + p], ids_o, (M - low) // 2)
-            anti = jnp.dot(odd, so_ref[base + p], preferred_element_type=jnp.float32)
-            sym = sym_ref[p]
-            for h, rows in enumerate((sym + anti, sym - anti)):
-                for w in range(2):
-                    start = (parity ^ w) * (lats * pairs) + base + p
-                    out_ref[h, pl.ds(start, lats, stride=pairs), :] = rows[w * lats : (w + 1) * lats]
+        for p in range(0, ROWS, 2):
+            lows = [waves_ref[base + q] for q in (p, p + 1)]
+            odd = [split(lo_ref[base + p + i], ids_o, (M - low) // 2) for i, low in enumerate(lows)]
+            antis = both(odd, [so_ref[base + p], so_ref[base + p + 1]])
+            for i, (low, anti) in enumerate(zip(lows, antis)):
+                parity = low % 2
+                sym = sym_ref[p + i]
+                for h, rows in enumerate((sym + anti, sym - anti)):
+                    for w in range(2):
+                        start = (parity ^ w) * (lats * pairs) + base + p + i
+                        out_ref[h, pl.ds(start, lats, stride=pairs), :] = rows[w * lats : (w + 1) * lats]
 
 
 def in_hbm(x):

time: 59.7 us -> 58.8 us (0.985)
  Pallas kernels: 22.2 us -> 21.3 us
    pallas_call x1, Pallas kernels: 8.44 us -> 7.54 us  [legendre_stage(): pl.pallas_call(legendre_kernel, out_shape=pltpu.VMEM((2, 2 * lats * pairs...]
  transfers between devices with their start and end apart: 2 -> 2, of which waited for: 1 -> 1; matrix products, arithmetic and copies ran while one was open for 1% -> 1% of each run, Pallas kernels for 27% -> 26%
where the time goes in v12:
time: 58.8 us; the launch traced here: 58.6 us
  waiting for transfers between devices  22.2 us (38%)
  Pallas kernels  21.3 us (36%)
  starting transfers between devices  12.6 us (21%)
  local copies, waits for them, and re-layouts  1.59 us (3%)
  other arithmetic  0.76 us (1%)
    all_to_all x1, waiting for transfers between devices, on_device(): lax.all_to_all(picked.reshape(devices, slots, 2, 2, pairs, width), 'wave'...  22.2 us
    pallas_call x1, Pallas kernels, legendre_stage(): pl.pallas_call(legendre_kernel, out_shape=pltpu.VMEM((2, 2 * lats * pairs...  7.54 us
    pallas_call x1, Pallas kernels, wave_tables(): pl.pallas_call(table_kernel, out_shape=[jax.ShapeDtypeStruct((2, 2, total...  7.48 us
    all_to_all x1, starting transfers between devices, on_device(): index = lax.all_to_all(own, 'wave', 0, 0, tiled=True)[:, 0]  6.55 us
    all_to_all x1, starting transfers between devices, on_device(): lax.all_to_all(picked.reshape(devices, slots, 2, 2, pairs, width), 'wave'...  6.05 us
    pallas_call x1, Pallas kernels, fourier_stage(): pl.pallas_call(fourier_kernel, out_shape=jax.ShapeDtypeStruct((rows, NLON...  4.64 us
    pallas_call x1, Pallas kernels, pick_latitudes(): pl.pallas_call(pick_kernel, out_shape=pltpu.HBM(shape, jnp.bfloat16), gri...  1.67 us
  transfers between devices with their start and end apart: 2, of which 1 were waited for; matrix products, arithmetic and copies ran while one was open for 1% of the time, Pallas kernels for 26%

profile of v12, /device:TPU:13, one launch (start us, length us, event | category | flops | bytes accessed | tf_op | source)
XLA Modules:
  0.0 58.6 jit_solution(16061747472252163481)
XLA Ops:
  0.0 0.7 %pad_add_fusion = s32[128]{0:T(128)S(1)} fusion(s32[86]{0:T(128)S(1)} %broadcast_in_dim.23, s32[2]{0:T(128)} %param.7, s32[40]{0:T(128)} %waves_hbm.1), kind=kLoop, calls=%fused_computation.13 | loop fusion | flops 256 | bytes 1024 | tf_op jit(solution)/shard_map/concatenate | solution.py:346
  0.7 0.6 %broadcast_in_dim.24 = s32[16,1,128]{2,1,0:T(1,128)} broadcast(s32[128]{0:T(128)S(1)} %pad_add_fusion), dimensions={2} | broadcast | bytes 8704 | tf_op jit(solution)/shard_map/broadcast_in_dim | solution.py:347
  1.4 6.6 %all-to-all-start = ((s32[16,1,128]{2,1,0:T(1,128)}), s32[16,1,128]{2,1,0:T(1,128)S(1)}, u32[]{:S(2)}, u32[]{:S(2)}) async-start(s32[16,1,128]{2,1,0:T(1,128)} %broadcast_in_dim.24), calls=%async_computation | async-start | bytes 16384 | tf_op jit(solution)/shard_map/all_to_all | solution.py:348
  7.9 7.5 %legendre.1.rows_ref = f32[2,2560,128]{2,1,0:T(8,128)S(1)} custom-call(s32[40]{0:T(128)} %waves_hbm.1, bf16[641,40,128]{2,1,0:T(8,128)(2,1)} %bitcast.5, bf16[40,640,128]{2,1,0:T(8,128)(2,1)} %so_hbm.1, bf16[40,32,641]{2,1,0:T(8,128)(2,1)} %le_hbm.1, bf16[40,32,640]{2,1,0:T(8,128)(2,1)} %lo_hbm.1), custom_call_target="tpu_custom_call" | custom-call | flops 1679032320 | bytes 16396800 | tf_op jit(solution)/shard_map/legendre/pallas_call | solution.py:115
  15.5 0.0 all-to-all-done
  15.5 0.1 slice.8
  15.5 0.1 reshape.13.bands_ref
  15.6 1.7 %pick.1 = bf16[32,2,2,40,128]{4,3,2,1,0:T(8,128)(2,1)} custom-call(s32[32]{0:T(128)S(1)} %reshape.13.bands_ref, f32[2,2560,128]{2,1,0:T(8,128)S(1)} %legendre.1.rows_ref), custom_call_target="tpu_custom_call" | custom-call | tf_op jit(solution)/shard_map/pick/pallas_call | solution.py:168
  17.3 6.0 %all-to-all-start.1 = ((bf16[16,2,2,2,40,128]{5,4,3,2,1,0:T(8,128)(2,1)}), bf16[16,2,2,2,40,128]{5,4,3,2,1,0:T(8,128)(2,1)S(1)}, u32[]{:S(2)}, u32[]{:S(2)}) async-start(bf16[16,2,2,2,40,128]{5,4,3,2,1,0:T(8,128)(2,1)} %bitcast.6), calls=%async_computation.1 | async-start | bytes 2621440 | tf_op jit(solution)/shard_map/all_to_all | solution.py:353
  23.4 0.1 reshape.15
  23.5 0.6 %broadcast_in_dim.27.sign_hbm = f32[8,640]{1,0:T(8,128)} broadcast(f32[640]{0:T(1024)S(1)} %fusion.4), dimensions={1} | broadcast | bytes 23040 | tf_op jit(solution)/shard_map/broadcast_in_dim | solution.py:356
  24.1 0.1 broadcast_in_dim.28.waves_ref
  24.2 7.5 %tables.1 = (bf16[2,2,640,256]{3,2,1,0:T(8,128)(2,1)S(1)}, bf16[2,2,2,640,256]{4,3,2,1,0:T(8,128)(2,1)}) custom-call(s32[640,128]{1,0:T(8,128)S(1)} %broadcast_in_dim.28.waves_ref), custom_call_target="tpu_custom_call" | custom-call | flops 6881280 | bytes 3440640 | tf_op jit(solution)/shard_map/tables/pallas_call | solution.py:216
  31.7 22.2 %all-to-all-done.1.arrived_ref = bf16[16,2,2,2,40,128]{5,4,3,2,1,0:T(8,128)(2,1)S(1)} async-done(((bf16[16,2,2,2,40,128]{5,4,3,2,1,0:T(8,128)(2,1)}), bf16[16,2,2,2,40,128]{5,4,3,2,1,0:T(8,128)(2,1)S(1)}, u32[]{:S(2)}, u32[]{:S(2)}) %all-to-all-start.1) | async-done | bytes 1310752 | tf_op jit(solution)/shard_map/all_to_all | solution.py:353
  53.9 4.6 %fourier.1 = bf16[256,2688]{1,0:T(8,128)(2,1)} custom-call(bf16[16,2,2,2,40,128]{5,4,3,2,1,0:T(8,128)(2,1)S(1)} %all-to-all-done.1.arrived_ref, bf16[2,2,640,256]{3,2,1,0:T(8,128)(2,1)S(1)} %get-tuple-element.14.first_ref, bf16[2,2,2,640,256]{4,3,2,1,0:T(8,128)(2,1)} %get-tuple-element.15.rest_hbm, f32[8,640]{1,0:T(8,128)} %broadcast_in_dim.27.sign_hbm), custom_call_target="tpu_custom_call" | custom-call | flops 1761607680 | bytes 3440640 | tf_op jit(solution)/shard_map/fourier/pallas_call | solution.py:309
  (2 shorter events, 0.0 us)
Async XLA Ops:
  1.4 14.1 %all-to-all-start = ((s32[16,1,128]{2,1,0:T(1,128)}), s32[16,1,128]{2,1,0:T(1,128)S(1)}, u32[]{:S(2)}, u32[]{:S(2)}) async-start(s32[16,1,128]{2,1,0:T(1,128)} %broadcast_in_dim.24), calls=%async_computation | async-start | bytes 16384 | tf_op jit(solution)/shard_map/all_to_all | solution.py:348
  17.3 36.6 %all-to-all-start.1 = ((bf16[16,2,2,2,40,128]{5,4,3,2,1,0:T(8,128)(2,1)}), bf16[16,2,2,2,40,128]{5,4,3,2,1,0:T(8,128)(2,1)S(1)}, u32[]{:S(2)}, u32[]{:S(2)}) async-start(bf16[16,2,2,2,40,128]{5,4,3,2,1,0:T(8,128)(2,1)} %bitcast.6), calls=%async_computation.1 | async-start | bytes 2621440 | tf_op jit(solution)/shard_map/all_to_all | solution.py:353

commit v13 on v12

--- a/solution.py
+++ b/solution.py
@@ -22,7 +22,7 @@
 
 def legendre_kernel(
     waves_hbm, se_hbm, so_hbm, le_hbm, lo_hbm, out_ref,
-    waves_ref, se_ref, so_ref, le_ref, lo_ref, columns_ref, sym_ref, sems, wave_sem,
+    waves_ref, se_ref, so_ref, le_ref, lo_ref, columns_ref, anti_ref, sems, wave_sem,
 ):
     pairs, lats, he = le_ref.shape
     ho = lo_ref.shape[2]
@@ -44,9 +44,9 @@
 
     wave_copy = pltpu.make_async_copy(waves_hbm, waves_ref, wave_sem)
     wave_copy.start()
-    ahead = 2
+    ahead = 3
     for g in range(min(ahead, groups)):
-        for copy in even_copies(g) + odd_copies(g):
+        for copy in odd_copies(g) + even_copies(g):
             copy.start()
     wave_copy.wait()
 
@@ -70,28 +70,25 @@
     @pl.loop(0, groups)
     def _(g):
         base = pl.multiple_of(g * ROWS, ROWS)
-        for copy in even_copies(g):
+        for copy in odd_copies(g) + even_copies(g):
             copy.wait()
 
         @pl.when(g + ahead < groups)
         def _():
-            for copy in even_copies(g + ahead) + odd_copies(g + ahead):
+            for copy in odd_copies(g + ahead) + even_copies(g + ahead):
                 copy.start()
 
+        for p in range(0, ROWS, 2):
+            odd = [split(lo_ref[base + q], ids_o, (M - waves_ref[base + q]) // 2) for q in (p, p + 1)]
+            anti_ref[p], anti_ref[p + 1] = both(odd, [so_ref[base + p], so_ref[base + p + 1]])
         columns_ref[...] = se_ref[g].astype(jnp.float32).reshape(columns_ref.shape)
         for p in range(0, ROWS, 2):
-            even = [split(le_ref[base + q], ids_e, (M - waves_ref[base + q] + 1) // 2) for q in (p, p + 1)]
+            lows = [waves_ref[base + q] for q in (p, p + 1)]
+            even = [split(le_ref[base + p + i], ids_e, (M - low + 1) // 2) for i, low in enumerate(lows)]
             xe = [columns_ref[pl.ds(q, he, stride=ROWS), :].astype(jnp.bfloat16) for q in (p, p + 1)]
-            sym_ref[p], sym_ref[p + 1] = both(even, xe)
-        for copy in odd_copies(g):
-            copy.wait()
-        for p in range(0, ROWS, 2):
-            lows = [waves_ref[base + q] for q in (p, p + 1)]
-            odd = [split(lo_ref[base + p + i], ids_o, (M - low) // 2) for i, low in enumerate(lows)]
-            antis = both(odd, [so_ref[base + p], so_ref[base + p + 1]])
-            for i, (low, anti) in enumerate(zip(lows, antis)):
+            for i, (low, sym) in enumerate(zip(lows, both(even, xe))):
                 parity = low % 2
-                sym = sym_ref[p + i]
+                anti = anti_ref[p + i]
                 for h, rows in enumerate((sym + anti, sym - anti)):
                     for w in range(2):
                         start = (parity ^ w) * (lats * pairs) + base + p + i
@@ -288,10 +285,10 @@
             left_ref[s, w, at, :total] = im if w else re
             left_ref[s, w, at, total:] = -re if w else im
         block(s, 0)
-    for i in range(1, chunks):
-        load(i).wait()
     for s in range(slots):
         for i in range(1, chunks):
+            if s == 0:
+                load(i).wait()
             block(s, i)
         base = slice(s * rows, (s + 1) * rows)
         copy = pltpu.make_async_copy(row_ref.at[base], out_hbm.at[base], out_sems.at[s])

time: 58.8 us -> 58.9 us (level)
  transfers between devices with their start and end apart: 2 -> 2, of which waited for: 1 -> 1; matrix products, arithmetic and copies ran while one was open for 1% -> 1% of each run, Pallas kernels for 26% -> 25%
where the time goes in v13:
time: 58.9 us; the launch traced here: 58.7 us
  waiting for transfers between devices  22.2 us (38%)
  Pallas kernels  21.5 us (37%)
  starting transfers between devices  12.6 us (21%)
  local copies, waits for them, and re-layouts  1.59 us (3%)
  other arithmetic  0.76 us (1%)
    all_to_all x1, waiting for transfers between devices, on_device(): lax.all_to_all(picked.reshape(devices, slots, 2, 2, pairs, width), 'wave'...  22.2 us
    pallas_call x1, Pallas kernels, wave_tables(): pl.pallas_call(table_kernel, out_shape=[jax.ShapeDtypeStruct((2, 2, total...  7.48 us
    pallas_call x1, Pallas kernels, legendre_stage(): pl.pallas_call(legendre_kernel, out_shape=pltpu.VMEM((2, 2 * lats * pairs...  7.43 us
    all_to_all x1, starting transfers between devices, on_device(): index = lax.all_to_all(own, 'wave', 0, 0, tiled=True)[:, 0]  6.55 us
    all_to_all x1, starting transfers between devices, on_device(): lax.all_to_all(picked.reshape(devices, slots, 2, 2, pairs, width), 'wave'...  6.04 us
    pallas_call x1, Pallas kernels, fourier_stage(): pl.pallas_call(fourier_kernel, out_shape=jax.ShapeDtypeStruct((rows, NLON...  4.88 us
    pallas_call x1, Pallas kernels, pick_latitudes(): pl.pallas_call(pick_kernel, out_shape=pltpu.HBM(shape, jnp.bfloat16), gri...  1.67 us
  transfers between devices with their start and end apart: 2, of which 1 were waited for; matrix products, arithmetic and copies ran while one was open for 1% of the time, Pallas kernels for 25%

profile of v13, /device:TPU:13, one launch (start us, length us, event | category | flops | bytes accessed | tf_op | source)
XLA Modules:
  0.0 58.7 jit_solution(2498368531781825858)
XLA Ops:
  0.0 0.7 %pad_add_fusion = s32[128]{0:T(128)S(1)} fusion(s32[86]{0:T(128)S(1)} %broadcast_in_dim.23, s32[2]{0:T(128)} %param.7, s32[40]{0:T(128)} %waves_hbm.1), kind=kLoop, calls=%fused_computation.13 | loop fusion | flops 256 | bytes 1024 | tf_op jit(solution)/shard_map/concatenate | solution.py:343
  0.7 0.6 %broadcast_in_dim.24 = s32[16,1,128]{2,1,0:T(1,128)} broadcast(s32[128]{0:T(128)S(1)} %pad_add_fusion), dimensions={2} | broadcast | bytes 8704 | tf_op jit(solution)/shard_map/broadcast_in_dim | solution.py:344
  1.4 6.6 %all-to-all-start = ((s32[16,1,128]{2,1,0:T(1,128)}), s32[16,1,128]{2,1,0:T(1,128)S(1)}, u32[]{:S(2)}, u32[]{:S(2)}) async-start(s32[16,1,128]{2,1,0:T(1,128)} %broadcast_in_dim.24), calls=%async_computation | async-start | bytes 16384 | tf_op jit(solution)/shard_map/all_to_all | solution.py:345
  7.9 7.4 %legendre.1.rows_ref = f32[2,2560,128]{2,1,0:T(8,128)S(1)} custom-call(s32[40]{0:T(128)} %waves_hbm.1, bf16[641,40,128]{2,1,0:T(8,128)(2,1)} %bitcast.5, bf16[40,640,128]{2,1,0:T(8,128)(2,1)} %so_hbm.1, bf16[40,32,641]{2,1,0:T(8,128)(2,1)} %le_hbm.1, bf16[40,32,640]{2,1,0:T(8,128)(2,1)} %lo_hbm.1), custom_call_target="tpu_custom_call" | custom-call | flops 1679032320 | bytes 16396800 | tf_op jit(solution)/shard_map/legendre/pallas_call | solution.py:112
  15.4 0.0 all-to-all-done
  15.4 0.1 slice.8
  15.4 0.1 reshape.13.bands_ref
  15.5 1.7 %pick.1 = bf16[32,2,2,40,128]{4,3,2,1,0:T(8,128)(2,1)} custom-call(s32[32]{0:T(128)S(1)} %reshape.13.bands_ref, f32[2,2560,128]{2,1,0:T(8,128)S(1)} %legendre.1.rows_ref), custom_call_target="tpu_custom_call" | custom-call | tf_op jit(solution)/shard_map/pick/pallas_call | solution.py:165
  17.2 6.0 %all-to-all-start.1 = ((bf16[16,2,2,2,40,128]{5,4,3,2,1,0:T(8,128)(2,1)}), bf16[16,2,2,2,40,128]{5,4,3,2,1,0:T(8,128)(2,1)S(1)}, u32[]{:S(2)}, u32[]{:S(2)}) async-start(bf16[16,2,2,2,40,128]{5,4,3,2,1,0:T(8,128)(2,1)} %bitcast.6), calls=%async_computation.1 | async-start | bytes 2621440 | tf_op jit(solution)/shard_map/all_to_all | solution.py:350
  23.2 0.1 reshape.15
  23.3 0.6 %broadcast_in_dim.27.sign_hbm = f32[8,640]{1,0:T(8,128)} broadcast(f32[640]{0:T(1024)S(1)} %fusion.4), dimensions={1} | broadcast | bytes 23040 | tf_op jit(solution)/shard_map/broadcast_in_dim | solution.py:353
  24.0 0.1 broadcast_in_dim.28.waves_ref
  24.1 7.5 %tables.1 = (bf16[2,2,640,256]{3,2,1,0:T(8,128)(2,1)S(1)}, bf16[2,2,2,640,256]{4,3,2,1,0:T(8,128)(2,1)}) custom-call(s32[640,128]{1,0:T(8,128)S(1)} %broadcast_in_dim.28.waves_ref), custom_call_target="tpu_custom_call" | custom-call | flops 6881280 | bytes 3440640 | tf_op jit(solution)/shard_map/tables/pallas_call | solution.py:213
  31.6 22.2 %all-to-all-done.1.arrived_ref = bf16[16,2,2,2,40,128]{5,4,3,2,1,0:T(8,128)(2,1)S(1)} async-done(((bf16[16,2,2,2,40,128]{5,4,3,2,1,0:T(8,128)(2,1)}), bf16[16,2,2,2,40,128]{5,4,3,2,1,0:T(8,128)(2,1)S(1)}, u32[]{:S(2)}, u32[]{:S(2)}) %all-to-all-start.1) | async-done | bytes 1310752 | tf_op jit(solution)/shard_map/all_to_all | solution.py:350
  53.8 4.9 %fourier.1 = bf16[256,2688]{1,0:T(8,128)(2,1)} custom-call(bf16[16,2,2,2,40,128]{5,4,3,2,1,0:T(8,128)(2,1)S(1)} %all-to-all-done.1.arrived_ref, bf16[2,2,640,256]{3,2,1,0:T(8,128)(2,1)S(1)} %get-tuple-element.14.first_ref, bf16[2,2,2,640,256]{4,3,2,1,0:T(8,128)(2,1)} %get-tuple-element.15.rest_hbm, f32[8,640]{1,0:T(8,128)} %broadcast_in_dim.27.sign_hbm), custom_call_target="tpu_custom_call" | custom-call | flops 1761607680 | bytes 3440640 | tf_op jit(solution)/shard_map/fourier/pallas_call | solution.py:306
  (2 shorter events, 0.0 us)
Async XLA Ops:
  1.4 14.0 %all-to-all-start = ((s32[16,1,128]{2,1,0:T(1,128)}), s32[16,1,128]{2,1,0:T(1,128)S(1)}, u32[]{:S(2)}, u32[]{:S(2)}) async-start(s32[16,1,128]{2,1,0:T(1,128)} %broadcast_in_dim.24), calls=%async_computation | async-start | bytes 16384 | tf_op jit(solution)/shard_map/all_to_all | solution.py:345
  17.2 36.6 %all-to-all-start.1 = ((bf16[16,2,2,2,40,128]{5,4,3,2,1,0:T(8,128)(2,1)}), bf16[16,2,2,2,40,128]{5,4,3,2,1,0:T(8,128)(2,1)S(1)}, u32[]{:S(2)}, u32[]{:S(2)}) async-start(bf16[16,2,2,2,40,128]{5,4,3,2,1,0:T(8,128)(2,1)} %bitcast.6), calls=%async_computation.1 | async-start | bytes 2621440 | tf_op jit(solution)/shard_map/all_to_all | solution.py:350

commit v14 on v13

--- a/solution.py
+++ b/solution.py
@@ -181,7 +181,13 @@
     return jnp.where(low % 2 == 0, low, M - 1 - low)
 
 
-def table_kernel(waves_ref, first_ref, rest_ref):
+def table_part(w, i, first_ref, second_ref, rest_ref):
+    if i == 0:
+        return first_ref.at[w]
+    return second_ref if (w, i) == (0, 1) else rest_ref.at[2 * i + w - 3]
+
+
+def table_kernel(waves_ref, first_ref, second_ref, rest_ref):
     even = even_wave(waves_ref[...])
     odd = M - 1 - even
     lane = lax.broadcasted_iota(jnp.int32, even.shape, 1).astype(jnp.float32)
@@ -200,27 +206,29 @@
         dc, ds = jnp.cos(step), jnp.sin(step)
         for b in range(0, QUARTER, LANES):
             at = slice(b % CHUNK, b % CHUNK + LANES)
-            out_ref = rest_ref.at[b // CHUNK - 1] if b >= CHUNK else first_ref
-            out_ref[w, 0, :, at] = c.astype(jnp.bfloat16)
-            out_ref[w, 1, :, at] = s.astype(jnp.bfloat16)
+            out_ref = table_part(w, b // CHUNK, first_ref, second_ref, rest_ref)
+            out_ref[0, :, at] = c.astype(jnp.bfloat16)
+            out_ref[1, :, at] = s.astype(jnp.bfloat16)
             c, s = c * dc + s * ds, s * dc - c * ds
 
 
 def wave_tables(waves):
     total = waves.shape[0]
     rows = 64
-    rest = pl.cdiv(QUARTER, CHUNK) - 1
+    rest = 2 * pl.cdiv(QUARTER, CHUNK) - 3
     return pl.pallas_call(
         table_kernel,
         out_shape=[
             jax.ShapeDtypeStruct((2, 2, total, CHUNK), jnp.bfloat16),
-            pltpu.HBM((rest, 2, 2, total, CHUNK), jnp.bfloat16),
+            jax.ShapeDtypeStruct((2, total, CHUNK), jnp.bfloat16),
+            pltpu.HBM((rest, 2, total, CHUNK), jnp.bfloat16),
         ],
         grid=(total // rows,),
         in_specs=[pl.BlockSpec((rows, LANES), lambda i: (i, 0))],
         out_specs=[
             pl.BlockSpec((2, 2, rows, CHUNK), lambda i: (0, 0, i, 0)),
-            pl.BlockSpec((rest, 2, 2, rows, CHUNK), lambda i: (0, 0, 0, i, 0)),
+            pl.BlockSpec((2, rows, CHUNK), lambda i: (0, i, 0)),
+            pl.BlockSpec((rest, 2, rows, CHUNK), lambda i: (0, 0, i, 0)),
         ],
         compiler_params=pltpu.CompilerParams(vmem_limit_bytes=16 * 1024 * 1024),
         cost_estimate=pl.CostEstimate(
@@ -231,25 +239,24 @@
 
 
 def fourier_kernel(
-    arrived_ref, first_ref, rest_hbm, sign_hbm, out_hbm,
+    arrived_ref, first_ref, second_ref, rest_hbm, sign_hbm, out_hbm,
     left_ref, rest_ref, sign_ref, row_ref, sems, sign_sem, out_sems,
 ):
     devices, slots, _, _, pairs, width = arrived_ref.shape
     fields = width // 2
     total = devices * pairs
-    chunks = 1 + rest_ref.shape[0]
+    chunks = (rest_ref.shape[0] + 3) // 2
     rows = 2 * fields
 
     def load(i):
-        return pltpu.make_async_copy(rest_hbm.at[i - 1], rest_ref.at[i - 1], sems.at[i - 1])
+        return pltpu.make_async_copy(rest_hbm.at[i], rest_ref.at[i], sems.at[i])
 
     def block(s, i):
-        table_ref = rest_ref.at[i - 1] if i else first_ref
         lo, hi = i * CHUNK, min((i + 1) * CHUNK, QUARTER)
         e, o = [
             jnp.dot(
                 left_ref[s, w],
-                table_ref[w].reshape(2 * total, CHUNK),
+                table_part(w, i, first_ref, second_ref, rest_ref)[...].reshape(2 * total, CHUNK),
                 preferred_element_type=jnp.float32,
             )[:, : hi - lo]
             for w in range(2)
@@ -261,7 +268,7 @@
 
     sign_copy = pltpu.make_async_copy(sign_hbm, sign_ref, sign_sem)
     sign_copy.start()
-    for i in range(1, chunks):
+    for i in range(rest_ref.shape[0]):
         load(i).start()
 
     stores = []
@@ -285,10 +292,10 @@
             left_ref[s, w, at, :total] = im if w else re
             left_ref[s, w, at, total:] = -re if w else im
         block(s, 0)
+    for i in range(rest_ref.shape[0]):
+        load(i).wait()
     for s in range(slots):
         for i in range(1, chunks):
-            if s == 0:
-                load(i).wait()
             block(s, i)
         base = slice(s * rows, (s + 1) * rows)
         copy = pltpu.make_async_copy(row_ref.at[base], out_hbm.at[base], out_sems.at[s])
@@ -298,7 +305,7 @@
         copy.wait()
 
 
-def fourier_stage(arrived, sign, first, rest):
+def fourier_stage(arrived, sign, first, second, rest):
     devices, slots, _, _, pairs, width = arrived.shape
     fields = width // 2
     total = devices * pairs
@@ -306,7 +313,7 @@
     out = pl.pallas_call(
         fourier_kernel,
         out_shape=jax.ShapeDtypeStruct((rows, NLON), jnp.bfloat16),
-        in_specs=[pl.BlockSpec(memory_space=pltpu.VMEM)] * 2 + [pl.BlockSpec(memory_space=pl.ANY)] * 2,
+        in_specs=[pl.BlockSpec(memory_space=pltpu.VMEM)] * 3 + [pl.BlockSpec(memory_space=pl.ANY)] * 2,
         out_specs=pl.BlockSpec(memory_space=pl.ANY),
         scratch_shapes=[
             pltpu.VMEM((slots, 2, 4 * fields, 2 * total), jnp.bfloat16),
@@ -322,7 +329,7 @@
             flops=16 * rows * total * QUARTER, bytes_accessed=8 * total * QUARTER, transcendentals=0
         ),
         name="fourier",
-    )(arrived, first, in_hbm(rest), in_hbm(sign))
+    )(arrived, first, second, in_hbm(rest), in_hbm(sign))
     return out.reshape(slots, 2, fields, NLON)
 
 

time: 58.9 us -> 58.6 us (level)
  no operation moved by 1% of the time
where the time goes in v14:
time: 58.6 us; the launch traced here: 58.4 us
  waiting for transfers between devices  22.4 us (38%)
  Pallas kernels  21 us (36%)
  starting transfers between devices  12.6 us (22%)
  local copies, waits for them, and re-layouts  1.59 us (3%)
  other arithmetic  0.76 us (1%)
    all_to_all x1, waiting for transfers between devices, on_device(): lax.all_to_all(picked.reshape(devices, slots, 2, 2, pairs, width), 'wave'...  22.3 us
    pallas_call x1, Pallas kernels, legendre_stage(): pl.pallas_call(legendre_kernel, out_shape=pltpu.VMEM((2, 2 * lats * pairs...  7.43 us
    pallas_call x1, Pallas kernels, wave_tables(): pl.pallas_call(table_kernel, out_shape=[jax.ShapeDtypeStruct((2, 2, total...  7.36 us
    all_to_all x1, starting transfers between devices, on_device(): index = lax.all_to_all(own, 'wave', 0, 0, tiled=True)[:, 0]  6.55 us
    all_to_all x1, starting transfers between devices, on_device(): lax.all_to_all(picked.reshape(devices, slots, 2, 2, pairs, width), 'wave'...  6.04 us
    pallas_call x1, Pallas kernels, fourier_stage(): pl.pallas_call(fourier_kernel, out_shape=jax.ShapeDtypeStruct((rows, NLON...  4.58 us
    pallas_call x1, Pallas kernels, pick_latitudes(): pl.pallas_call(pick_kernel, out_shape=pltpu.HBM(shape, jnp.bfloat16), gri...  1.67 us
  transfers between devices with their start and end apart: 2, of which 1 were waited for; matrix products, arithmetic and copies ran while one was open for 1% of the time, Pallas kernels for 25%

profile of v14, /device:TPU:13, one launch (start us, length us, event | category | flops | bytes accessed | tf_op | source)
XLA Modules:
  0.0 58.4 jit_solution(3732526199377061688)
XLA Ops:
  0.0 0.7 %pad_add_fusion = s32[128]{0:T(128)S(1)} fusion(s32[86]{0:T(128)S(1)} %broadcast_in_dim.23, s32[2]{0:T(128)} %param.7, s32[40]{0:T(128)} %waves_hbm.1), kind=kLoop, calls=%fused_computation.13 | loop fusion | flops 256 | bytes 1024 | tf_op jit(solution)/shard_map/concatenate | solution.py:350
  0.7 0.6 %broadcast_in_dim.24 = s32[16,1,128]{2,1,0:T(1,128)} broadcast(s32[128]{0:T(128)S(1)} %pad_add_fusion), dimensions={2} | broadcast | bytes 8704 | tf_op jit(solution)/shard_map/broadcast_in_dim | solution.py:351
  1.4 6.6 %all-to-all-start = ((s32[16,1,128]{2,1,0:T(1,128)}), s32[16,1,128]{2,1,0:T(1,128)S(1)}, u32[]{:S(2)}, u32[]{:S(2)}) async-start(s32[16,1,128]{2,1,0:T(1,128)} %broadcast_in_dim.24), calls=%async_computation | async-start | bytes 16384 | tf_op jit(solution)/shard_map/all_to_all | solution.py:352
  7.9 7.4 %legendre.1.rows_ref = f32[2,2560,128]{2,1,0:T(8,128)S(1)} custom-call(s32[40]{0:T(128)} %waves_hbm.1, bf16[641,40,128]{2,1,0:T(8,128)(2,1)} %bitcast.5, bf16[40,640,128]{2,1,0:T(8,128)(2,1)} %so_hbm.1, bf16[40,32,641]{2,1,0:T(8,128)(2,1)} %le_hbm.1, bf16[40,32,640]{2,1,0:T(8,128)(2,1)} %lo_hbm.1), custom_call_target="tpu_custom_call" | custom-call | flops 1679032320 | bytes 16396800 | tf_op jit(solution)/shard_map/legendre/pallas_call | solution.py:112
  15.4 0.0 all-to-all-done
  15.4 0.1 slice.8
  15.4 0.1 reshape.13.bands_ref
  15.5 1.7 %pick.1 = bf16[32,2,2,40,128]{4,3,2,1,0:T(8,128)(2,1)} custom-call(s32[32]{0:T(128)S(1)} %reshape.13.bands_ref, f32[2,2560,128]{2,1,0:T(8,128)S(1)} %legendre.1.rows_ref), custom_call_target="tpu_custom_call" | custom-call | tf_op jit(solution)/shard_map/pick/pallas_call | solution.py:165
  17.2 6.0 %all-to-all-start.1 = ((bf16[16,2,2,2,40,128]{5,4,3,2,1,0:T(8,128)(2,1)}), bf16[16,2,2,2,40,128]{5,4,3,2,1,0:T(8,128)(2,1)S(1)}, u32[]{:S(2)}, u32[]{:S(2)}) async-start(bf16[16,2,2,2,40,128]{5,4,3,2,1,0:T(8,128)(2,1)} %bitcast.6), calls=%async_computation.1 | async-start | bytes 2621440 | tf_op jit(solution)/shard_map/all_to_all | solution.py:357
  23.2 0.1 reshape.15
  23.3 0.6 %broadcast_in_dim.27.sign_hbm = f32[8,640]{1,0:T(8,128)} broadcast(f32[640]{0:T(1024)S(1)} %fusion.4), dimensions={1} | broadcast | bytes 23040 | tf_op jit(solution)/shard_map/broadcast_in_dim | solution.py:360
  24.0 0.1 broadcast_in_dim.28.waves_ref
  24.1 7.4 %tables.1 = (bf16[2,2,640,256]{3,2,1,0:T(8,128)(2,1)S(1)}, bf16[2,640,256]{2,1,0:T(8,128)(2,1)S(1)}, bf16[3,2,640,256]{3,2,1,0:T(8,128)(2,1)}) custom-call(s32[640,128]{1,0:T(8,128)S(1)} %broadcast_in_dim.28.waves_ref), custom_call_target="tpu_custom_call" | custom-call | flops 6881280 | bytes 3440640 | tf_op jit(solution)/shard_map/tables/pallas_call | solution.py:219
  31.5 22.3 %all-to-all-done.1.arrived_ref = bf16[16,2,2,2,40,128]{5,4,3,2,1,0:T(8,128)(2,1)S(1)} async-done(((bf16[16,2,2,2,40,128]{5,4,3,2,1,0:T(8,128)(2,1)}), bf16[16,2,2,2,40,128]{5,4,3,2,1,0:T(8,128)(2,1)S(1)}, u32[]{:S(2)}, u32[]{:S(2)}) %all-to-all-start.1) | async-done | bytes 1310752 | tf_op jit(solution)/shard_map/all_to_all | solution.py:357
  53.8 4.6 %fourier.1 = bf16[256,2688]{1,0:T(8,128)(2,1)} custom-call(bf16[16,2,2,2,40,128]{5,4,3,2,1,0:T(8,128)(2,1)S(1)} %all-to-all-done.1.arrived_ref, bf16[2,2,640,256]{3,2,1,0:T(8,128)(2,1)S(1)} %get-tuple-element.15.first_ref, bf16[2,640,256]{2,1,0:T(8,128)(2,1)S(1)} %get-tuple-element.16.second_ref, bf16[3,2,640,256]{3,2,1,0:T(8,128)(2,1)} %get-tuple-element.17.rest_hbm, ...), custom_call_target="tpu_custom_call" | custom-call | flops 1761607680 | bytes 3440640 | tf_op jit(solution)/shard_map/fourier/pallas_call | solution.py:313
  (2 shorter events, 0.0 us)
Async XLA Ops:
  1.4 14.0 %all-to-all-start = ((s32[16,1,128]{2,1,0:T(1,128)}), s32[16,1,128]{2,1,0:T(1,128)S(1)}, u32[]{:S(2)}, u32[]{:S(2)}) async-start(s32[16,1,128]{2,1,0:T(1,128)} %broadcast_in_dim.24), calls=%async_computation | async-start | bytes 16384 | tf_op jit(solution)/shard_map/all_to_all | solution.py:352
  17.2 36.6 %all-to-all-start.1 = ((bf16[16,2,2,2,40,128]{5,4,3,2,1,0:T(8,128)(2,1)}), bf16[16,2,2,2,40,128]{5,4,3,2,1,0:T(8,128)(2,1)S(1)}, u32[]{:S(2)}, u32[]{:S(2)}) async-start(bf16[16,2,2,2,40,128]{5,4,3,2,1,0:T(8,128)(2,1)} %bitcast.6), calls=%async_computation.1 | async-start | bytes 2621440 | tf_op jit(solution)/shard_map/all_to_all | solution.py:357

commit v15 on v14

--- a/solution.py
+++ b/solution.py
@@ -44,7 +44,7 @@
 
     wave_copy = pltpu.make_async_copy(waves_hbm, waves_ref, wave_sem)
     wave_copy.start()
-    ahead = 3
+    ahead = groups
     for g in range(min(ahead, groups)):
         for copy in odd_copies(g) + even_copies(g):
             copy.start()
@@ -291,11 +291,12 @@
             re, im = signed[:fields], signed[fields:]
             left_ref[s, w, at, :total] = im if w else re
             left_ref[s, w, at, total:] = -re if w else im
-        block(s, 0)
+        if s == 0:
+            block(s, 0)
     for i in range(rest_ref.shape[0]):
         load(i).wait()
     for s in range(slots):
-        for i in range(1, chunks):
+        for i in range(s == 0, chunks):
             block(s, i)
         base = slice(s * rows, (s + 1) * rows)
         copy = pltpu.make_async_copy(row_ref.at[base], out_hbm.at[base], out_sems.at[s])

time: 58.6 us -> 58.7 us (level)
  no operation moved by 1% of the time
where the time goes in v15:
time: 58.7 us; the launch traced here: 58.4 us
  waiting for transfers between devices  22.4 us (38%)
  Pallas kernels  21.1 us (36%)
  starting transfers between devices  12.6 us (21%)
  local copies, waits for them, and re-layouts  1.59 us (3%)
  other arithmetic  0.76 us (1%)
    all_to_all x1, waiting for transfers between devices, on_device(): lax.all_to_all(picked.reshape(devices, slots, 2, 2, pairs, width), 'wave'...  22.3 us
    pallas_call x1, Pallas kernels, legendre_stage(): pl.pallas_call(legendre_kernel, out_shape=pltpu.VMEM((2, 2 * lats * pairs...  7.46 us
    pallas_call x1, Pallas kernels, wave_tables(): pl.pallas_call(table_kernel, out_shape=[jax.ShapeDtypeStruct((2, 2, total...  7.36 us
    all_to_all x1, starting transfers between devices, on_device(): index = lax.all_to_all(own, 'wave', 0, 0, tiled=True)[:, 0]  6.55 us
    all_to_all x1, starting transfers between devices, on_device(): lax.all_to_all(picked.reshape(devices, slots, 2, 2, pairs, width), 'wave'...  6.03 us
    pallas_call x1, Pallas kernels, fourier_stage(): pl.pallas_call(fourier_kernel, out_shape=jax.ShapeDtypeStruct((rows, NLON...  4.59 us
    pallas_call x1, Pallas kernels, pick_latitudes(): pl.pallas_call(pick_kernel, out_shape=pltpu.HBM(shape, jnp.bfloat16), gri...  1.67 us
  transfers between devices with their start and end apart: 2, of which 1 were waited for; matrix products, arithmetic and copies ran while one was open for 1% of the time, Pallas kernels for 25%

profile of v15, /device:TPU:13, one launch (start us, length us, event | category | flops | bytes accessed | tf_op | source)
XLA Modules:
  0.0 58.4 jit_solution(12730288633384017309)
XLA Ops:
  0.0 0.7 %pad_add_fusion = s32[128]{0:T(128)S(1)} fusion(s32[86]{0:T(128)S(1)} %broadcast_in_dim.23, s32[2]{0:T(128)} %param.7, s32[40]{0:T(128)} %waves_hbm.1), kind=kLoop, calls=%fused_computation.13 | loop fusion | flops 256 | bytes 1024 | tf_op jit(solution)/shard_map/concatenate | solution.py:351
  0.7 0.6 %broadcast_in_dim.24 = s32[16,1,128]{2,1,0:T(1,128)} broadcast(s32[128]{0:T(128)S(1)} %pad_add_fusion), dimensions={2} | broadcast | bytes 8704 | tf_op jit(solution)/shard_map/broadcast_in_dim | solution.py:352
  1.4 6.6 %all-to-all-start = ((s32[16,1,128]{2,1,0:T(1,128)}), s32[16,1,128]{2,1,0:T(1,128)S(1)}, u32[]{:S(2)}, u32[]{:S(2)}) async-start(s32[16,1,128]{2,1,0:T(1,128)} %broadcast_in_dim.24), calls=%async_computation | async-start | bytes 16384 | tf_op jit(solution)/shard_map/all_to_all | solution.py:353
  7.9 7.5 %legendre.1.rows_ref = f32[2,2560,128]{2,1,0:T(8,128)S(1)} custom-call(s32[40]{0:T(128)} %waves_hbm.1, bf16[641,40,128]{2,1,0:T(8,128)(2,1)} %bitcast.5, bf16[40,640,128]{2,1,0:T(8,128)(2,1)} %so_hbm.1, bf16[40,32,641]{2,1,0:T(8,128)(2,1)} %le_hbm.1, bf16[40,32,640]{2,1,0:T(8,128)(2,1)} %lo_hbm.1), custom_call_target="tpu_custom_call" | custom-call | flops 1679032320 | bytes 16396800 | tf_op jit(solution)/shard_map/legendre/pallas_call | solution.py:112
  15.4 0.0 all-to-all-done
  15.4 0.1 slice.8
  15.5 0.1 reshape.13.bands_ref
  15.6 1.7 %pick.1 = bf16[32,2,2,40,128]{4,3,2,1,0:T(8,128)(2,1)} custom-call(s32[32]{0:T(128)S(1)} %reshape.13.bands_ref, f32[2,2560,128]{2,1,0:T(8,128)S(1)} %legendre.1.rows_ref), custom_call_target="tpu_custom_call" | custom-call | tf_op jit(solution)/shard_map/pick/pallas_call | solution.py:165
  17.2 6.0 %all-to-all-start.1 = ((bf16[16,2,2,2,40,128]{5,4,3,2,1,0:T(8,128)(2,1)}), bf16[16,2,2,2,40,128]{5,4,3,2,1,0:T(8,128)(2,1)S(1)}, u32[]{:S(2)}, u32[]{:S(2)}) async-start(bf16[16,2,2,2,40,128]{5,4,3,2,1,0:T(8,128)(2,1)} %bitcast.6), calls=%async_computation.1 | async-start | bytes 2621440 | tf_op jit(solution)/shard_map/all_to_all | solution.py:358
  23.3 0.1 reshape.15
  23.4 0.6 %broadcast_in_dim.27.sign_hbm = f32[8,640]{1,0:T(8,128)} broadcast(f32[640]{0:T(1024)S(1)} %fusion.4), dimensions={1} | broadcast | bytes 23040 | tf_op jit(solution)/shard_map/broadcast_in_dim | solution.py:361
  24.0 0.1 broadcast_in_dim.28.waves_ref
  24.1 7.4 %tables.1 = (bf16[2,2,640,256]{3,2,1,0:T(8,128)(2,1)S(1)}, bf16[2,640,256]{2,1,0:T(8,128)(2,1)S(1)}, bf16[3,2,640,256]{3,2,1,0:T(8,128)(2,1)}) custom-call(s32[640,128]{1,0:T(8,128)S(1)} %broadcast_in_dim.28.waves_ref), custom_call_target="tpu_custom_call" | custom-call | flops 6881280 | bytes 3440640 | tf_op jit(solution)/shard_map/tables/pallas_call | solution.py:219
  31.5 22.3 %all-to-all-done.1.arrived_ref = bf16[16,2,2,2,40,128]{5,4,3,2,1,0:T(8,128)(2,1)S(1)} async-done(((bf16[16,2,2,2,40,128]{5,4,3,2,1,0:T(8,128)(2,1)}), bf16[16,2,2,2,40,128]{5,4,3,2,1,0:T(8,128)(2,1)S(1)}, u32[]{:S(2)}, u32[]{:S(2)}) %all-to-all-start.1) | async-done | bytes 1310752 | tf_op jit(solution)/shard_map/all_to_all | solution.py:358
  53.8 4.6 %fourier.1 = bf16[256,2688]{1,0:T(8,128)(2,1)} custom-call(bf16[16,2,2,2,40,128]{5,4,3,2,1,0:T(8,128)(2,1)S(1)} %all-to-all-done.1.arrived_ref, bf16[2,2,640,256]{3,2,1,0:T(8,128)(2,1)S(1)} %get-tuple-element.15.first_ref, bf16[2,640,256]{2,1,0:T(8,128)(2,1)S(1)} %get-tuple-element.16.second_ref, bf16[3,2,640,256]{3,2,1,0:T(8,128)(2,1)} %get-tuple-element.17.rest_hbm, ...), custom_call_target="tpu_custom_call" | custom-call | flops 1761607680 | bytes 3440640 | tf_op jit(solution)/shard_map/fourier/pallas_call | solution.py:314
  (2 shorter events, 0.0 us)
Async XLA Ops:
  1.4 14.0 %all-to-all-start = ((s32[16,1,128]{2,1,0:T(1,128)}), s32[16,1,128]{2,1,0:T(1,128)S(1)}, u32[]{:S(2)}, u32[]{:S(2)}) async-start(s32[16,1,128]{2,1,0:T(1,128)} %broadcast_in_dim.24), calls=%async_computation | async-start | bytes 16384 | tf_op jit(solution)/shard_map/all_to_all | solution.py:353
  17.2 36.6 %all-to-all-start.1 = ((bf16[16,2,2,2,40,128]{5,4,3,2,1,0:T(8,128)(2,1)}), bf16[16,2,2,2,40,128]{5,4,3,2,1,0:T(8,128)(2,1)S(1)}, u32[]{:S(2)}, u32[]{:S(2)}) async-start(bf16[16,2,2,2,40,128]{5,4,3,2,1,0:T(8,128)(2,1)} %bitcast.6), calls=%async_computation.1 | async-start | bytes 2621440 | tf_op jit(solution)/shard_map/all_to_all | solution.py:358

commit v16 on v15

--- a/solution.py
+++ b/solution.py
@@ -44,7 +44,7 @@
 
     wave_copy = pltpu.make_async_copy(waves_hbm, waves_ref, wave_sem)
     wave_copy.start()
-    ahead = groups
+    ahead = 3
     for g in range(min(ahead, groups)):
         for copy in odd_copies(g) + even_copies(g):
             copy.start()
@@ -152,7 +152,7 @@
         return carry
 
     for i in range(sems.shape[0]):
-        lax.fori_loop(i * piece, (i + 1) * piece, emit, 0, unroll=4)
+        lax.fori_loop(i * piece, (i + 1) * piece, emit, 0, unroll=8)
         store(i).start()
     for i in range(sems.shape[0]):
         store(i).wait()

time: 58.7 us -> 58.7 us (level)
  no operation moved by 1% of the time
where the time goes in v16:
time: 58.7 us; the launch traced here: 58.4 us
  waiting for transfers between devices  22.4 us (38%)
  Pallas kernels  21 us (36%)
  starting transfers between devices  12.6 us (21%)
  local copies, waits for them, and re-layouts  1.59 us (3%)
  other arithmetic  0.76 us (1%)
    all_to_all x1, waiting for transfers between devices, on_device(): lax.all_to_all(picked.reshape(devices, slots, 2, 2, pairs, width), 'wave'...  22.3 us
    pallas_call x1, Pallas kernels, legendre_stage(): pl.pallas_call(legendre_kernel, out_shape=pltpu.VMEM((2, 2 * lats * pairs...  7.43 us
    pallas_call x1, Pallas kernels, wave_tables(): pl.pallas_call(table_kernel, out_shape=[jax.ShapeDtypeStruct((2, 2, total...  7.36 us
    all_to_all x1, starting transfers between devices, on_device(): index = lax.all_to_all(own, 'wave', 0, 0, tiled=True)[:, 0]  6.55 us
    all_to_all x1, starting transfers between devices, on_device(): lax.all_to_all(picked.reshape(devices, slots, 2, 2, pairs, width), 'wave'...  6.04 us
    pallas_call x1, Pallas kernels, fourier_stage(): pl.pallas_call(fourier_kernel, out_shape=jax.ShapeDtypeStruct((rows, NLON...  4.59 us
    pallas_call x1, Pallas kernels, pick_latitudes(): pl.pallas_call(pick_kernel, out_shape=pltpu.HBM(shape, jnp.bfloat16), gri...  1.66 us
  transfers between devices with their start and end apart: 2, of which 1 were waited for; matrix products, arithmetic and copies ran while one was open for 1% of the time, Pallas kernels for 25%

profile of v16, /device:TPU:13, one launch (start us, length us, event | category | flops | bytes accessed | tf_op | source)
XLA Modules:
  0.0 58.4 jit_solution(12517695382465064859)
XLA Ops:
  0.0 0.7 %pad_add_fusion = s32[128]{0:T(128)S(1)} fusion(s32[86]{0:T(128)S(1)} %broadcast_in_dim.23, s32[2]{0:T(128)} %param.7, s32[40]{0:T(128)} %waves_hbm.1), kind=kLoop, calls=%fused_computation.13 | loop fusion | flops 256 | bytes 1024 | tf_op jit(solution)/shard_map/concatenate | solution.py:351
  0.7 0.6 %broadcast_in_dim.24 = s32[16,1,128]{2,1,0:T(1,128)} broadcast(s32[128]{0:T(128)S(1)} %pad_add_fusion), dimensions={2} | broadcast | bytes 8704 | tf_op jit(solution)/shard_map/broadcast_in_dim | solution.py:352
  1.4 6.6 %all-to-all-start = ((s32[16,1,128]{2,1,0:T(1,128)}), s32[16,1,128]{2,1,0:T(1,128)S(1)}, u32[]{:S(2)}, u32[]{:S(2)}) async-start(s32[16,1,128]{2,1,0:T(1,128)} %broadcast_in_dim.24), calls=%async_computation | async-start | bytes 16384 | tf_op jit(solution)/shard_map/all_to_all | solution.py:353
  7.9 7.4 %legendre.1.rows_ref = f32[2,2560,128]{2,1,0:T(8,128)S(1)} custom-call(s32[40]{0:T(128)} %waves_hbm.1, bf16[641,40,128]{2,1,0:T(8,128)(2,1)} %bitcast.5, bf16[40,640,128]{2,1,0:T(8,128)(2,1)} %so_hbm.1, bf16[40,32,641]{2,1,0:T(8,128)(2,1)} %le_hbm.1, bf16[40,32,640]{2,1,0:T(8,128)(2,1)} %lo_hbm.1), custom_call_target="tpu_custom_call" | custom-call | flops 1679032320 | bytes 16396800 | tf_op jit(solution)/shard_map/legendre/pallas_call | solution.py:112
  15.4 0.0 all-to-all-done
  15.4 0.1 slice.8
  15.4 0.1 reshape.13.bands_ref
  15.5 1.7 %pick.1 = bf16[32,2,2,40,128]{4,3,2,1,0:T(8,128)(2,1)} custom-call(s32[32]{0:T(128)S(1)} %reshape.13.bands_ref, f32[2,2560,128]{2,1,0:T(8,128)S(1)} %legendre.1.rows_ref), custom_call_target="tpu_custom_call" | custom-call | tf_op jit(solution)/shard_map/pick/pallas_call | solution.py:165
  17.2 6.0 %all-to-all-start.1 = ((bf16[16,2,2,2,40,128]{5,4,3,2,1,0:T(8,128)(2,1)}), bf16[16,2,2,2,40,128]{5,4,3,2,1,0:T(8,128)(2,1)S(1)}, u32[]{:S(2)}, u32[]{:S(2)}) async-start(bf16[16,2,2,2,40,128]{5,4,3,2,1,0:T(8,128)(2,1)} %bitcast.6), calls=%async_computation.1 | async-start | bytes 2621440 | tf_op jit(solution)/shard_map/all_to_all | solution.py:358
  23.2 0.1 reshape.15
  23.3 0.6 %broadcast_in_dim.27.sign_hbm = f32[8,640]{1,0:T(8,128)} broadcast(f32[640]{0:T(1024)S(1)} %fusion.4), dimensions={1} | broadcast | bytes 23040 | tf_op jit(solution)/shard_map/broadcast_in_dim | solution.py:361
  23.9 0.1 broadcast_in_dim.28.waves_ref
  24.1 7.4 %tables.1 = (bf16[2,2,640,256]{3,2,1,0:T(8,128)(2,1)S(1)}, bf16[2,640,256]{2,1,0:T(8,128)(2,1)S(1)}, bf16[3,2,640,256]{3,2,1,0:T(8,128)(2,1)}) custom-call(s32[640,128]{1,0:T(8,128)S(1)} %broadcast_in_dim.28.waves_ref), custom_call_target="tpu_custom_call" | custom-call | flops 6881280 | bytes 3440640 | tf_op jit(solution)/shard_map/tables/pallas_call | solution.py:219
  31.5 22.3 %all-to-all-done.1.arrived_ref = bf16[16,2,2,2,40,128]{5,4,3,2,1,0:T(8,128)(2,1)S(1)} async-done(((bf16[16,2,2,2,40,128]{5,4,3,2,1,0:T(8,128)(2,1)}), bf16[16,2,2,2,40,128]{5,4,3,2,1,0:T(8,128)(2,1)S(1)}, u32[]{:S(2)}, u32[]{:S(2)}) %all-to-all-start.1) | async-done | bytes 1310752 | tf_op jit(solution)/shard_map/all_to_all | solution.py:358
  53.8 4.6 %fourier.1 = bf16[256,2688]{1,0:T(8,128)(2,1)} custom-call(bf16[16,2,2,2,40,128]{5,4,3,2,1,0:T(8,128)(2,1)S(1)} %all-to-all-done.1.arrived_ref, bf16[2,2,640,256]{3,2,1,0:T(8,128)(2,1)S(1)} %get-tuple-element.15.first_ref, bf16[2,640,256]{2,1,0:T(8,128)(2,1)S(1)} %get-tuple-element.16.second_ref, bf16[3,2,640,256]{3,2,1,0:T(8,128)(2,1)} %get-tuple-element.17.rest_hbm, ...), custom_call_target="tpu_custom_call" | custom-call | flops 1761607680 | bytes 3440640 | tf_op jit(solution)/shard_map/fourier/pallas_call | solution.py:314
  (2 shorter events, 0.0 us)
Async XLA Ops:
  1.4 14.0 %all-to-all-start = ((s32[16,1,128]{2,1,0:T(1,128)}), s32[16,1,128]{2,1,0:T(1,128)S(1)}, u32[]{:S(2)}, u32[]{:S(2)}) async-start(s32[16,1,128]{2,1,0:T(1,128)} %broadcast_in_dim.24), calls=%async_computation | async-start | bytes 16384 | tf_op jit(solution)/shard_map/all_to_all | solution.py:353
  17.2 36.6 %all-to-all-start.1 = ((bf16[16,2,2,2,40,128]{5,4,3,2,1,0:T(8,128)(2,1)}), bf16[16,2,2,2,40,128]{5,4,3,2,1,0:T(8,128)(2,1)S(1)}, u32[]{:S(2)}, u32[]{:S(2)}) async-start(bf16[16,2,2,2,40,128]{5,4,3,2,1,0:T(8,128)(2,1)} %bitcast.6), calls=%async_computation.1 | async-start | bytes 2621440 | tf_op jit(solution)/shard_map/all_to_all | solution.py:358

commit v17 on v16

--- a/solution.py
+++ b/solution.py
@@ -135,16 +135,17 @@
     )(*(in_hbm(x) for x in operands))
 
 
-def pick_kernel(bands_ref, rows_ref, out_hbm, out_ref, sems):
+def pick_kernel(column, index_ref, rows_ref, out_hbm, out_ref, sems):
     lats, _, _, pairs, _ = out_ref.shape
     piece = lats // sems.shape[0]
+    slots = lats // index_ref.shape[0]
 
     def store(i):
         at = pl.ds(i * piece, piece)
         return pltpu.make_async_copy(out_ref.at[at], out_hbm.at[at], sems.at[i])
 
     def emit(slot, carry):
-        band = bands_ref[slot]
+        band = index_ref[slot // slots, column + slot % slots]
         for h in range(2):
             for w in range(2):
                 start = pl.multiple_of((w * lats + band) * pairs, ROWS)
@@ -158,12 +159,11 @@
         store(i).wait()
 
 
-def pick_latitudes(bands, rows, pairs):
-    lats = bands.shape[0]
+def pick_latitudes(index, rows, lats, pairs):
     width = rows.shape[2]
     shape = (lats, 2, 2, pairs, width)
     return pl.pallas_call(
-        pick_kernel,
+        functools.partial(pick_kernel, pairs),
         out_shape=pltpu.HBM(shape, jnp.bfloat16),
         grid_spec=pltpu.PrefetchScalarGridSpec(
             num_scalar_prefetch=1,
@@ -174,7 +174,7 @@
         ),
         compiler_params=pltpu.CompilerParams(vmem_limit_bytes=16 * 1024 * 1024),
         name="pick",
-    )(bands, in_vmem(rows))
+    )(index, in_vmem(rows))
 
 
 def even_wave(low):
@@ -351,9 +351,8 @@
     own = jnp.concatenate([wave_pairs, band_owner, jnp.zeros(rest, jnp.int32)])
     own = jnp.broadcast_to(own, (devices, 1) + own.shape)
     index = lax.all_to_all(own, "wave", 0, 0, tiled=True)[:, 0]
-    all_bands = index[:, pairs : pairs + slots].reshape(-1)
     rows = legendre_stage(wave_pairs, spectra_even, spectra_odd, legendre_even, legendre_odd)
-    picked = pick_latitudes(all_bands, rows, pairs)
+    picked = pick_latitudes(index, rows, devices * slots, pairs)
     index, picked = lax.optimization_barrier((index, picked))
     arrived = lax.all_to_all(picked.reshape(devices, slots, 2, 2, pairs, width), "wave", 0, 0, tiled=True)
     all_pairs = index[:, :pairs].reshape(-1)

time: 58.7 us -> 58.6 us (level)
  no operation moved by 1% of the time
where the time goes in v17:
time: 58.6 us; the launch traced here: 58.4 us
  waiting for transfers between devices  22.4 us (38%)
  Pallas kernels  21.2 us (36%)
  starting transfers between devices  12.6 us (22%)
  local copies, waits for them, and re-layouts  1.43 us (2%)
  other arithmetic  0.76 us (1%)
    all_to_all x1, waiting for transfers between devices, on_device(): lax.all_to_all(picked.reshape(devices, slots, 2, 2, pairs, width), 'wave'...  22.3 us
    pallas_call x1, Pallas kernels, legendre_stage(): pl.pallas_call(legendre_kernel, out_shape=pltpu.VMEM((2, 2 * lats * pairs...  7.43 us
    pallas_call x1, Pallas kernels, wave_tables(): pl.pallas_call(table_kernel, out_shape=[jax.ShapeDtypeStruct((2, 2, total...  7.36 us
    all_to_all x1, starting transfers between devices, on_device(): index = lax.all_to_all(own, 'wave', 0, 0, tiled=True)[:, 0]  6.55 us
    all_to_all x1, starting transfers between devices, on_device(): lax.all_to_all(picked.reshape(devices, slots, 2, 2, pairs, width), 'wave'...  6.04 us
    pallas_call x1, Pallas kernels, fourier_stage(): pl.pallas_call(fourier_kernel, out_shape=jax.ShapeDtypeStruct((rows, NLON...  4.59 us
    pallas_call x1, Pallas kernels, pick_latitudes(): pl.pallas_call(functools.partial(pick_kernel, pairs), out_shape=pltpu.HBM...  1.79 us
  transfers between devices with their start and end apart: 2, of which 1 were waited for; matrix products, arithmetic and copies ran while one was open for 1% of the time, Pallas kernels for 25%

profile of v17, /device:TPU:13, one launch (start us, length us, event | category | flops | bytes accessed | tf_op | source)
XLA Modules:
  0.0 58.4 jit_solution(7914507269563653271)
XLA Ops:
  0.0 0.7 %pad_add_fusion = s32[128]{0:T(128)S(1)} fusion(s32[86]{0:T(128)S(1)} %broadcast_in_dim.23, s32[2]{0:T(128)} %param.7, s32[40]{0:T(128)} %waves_hbm.1), kind=kLoop, calls=%fused_computation.13 | loop fusion | flops 256 | bytes 1024 | tf_op jit(solution)/shard_map/concatenate | solution.py:351
  0.7 0.6 %broadcast_in_dim.24 = s32[16,1,128]{2,1,0:T(1,128)} broadcast(s32[128]{0:T(128)S(1)} %pad_add_fusion), dimensions={2} | broadcast | bytes 8704 | tf_op jit(solution)/shard_map/broadcast_in_dim | solution.py:352
  1.4 6.6 %all-to-all-start = ((s32[16,1,128]{2,1,0:T(1,128)}), s32[16,1,128]{2,1,0:T(1,128)S(1)}, u32[]{:S(2)}, u32[]{:S(2)}) async-start(s32[16,1,128]{2,1,0:T(1,128)} %broadcast_in_dim.24), calls=%async_computation | async-start | bytes 16384 | tf_op jit(solution)/shard_map/all_to_all | solution.py:353
  7.9 7.4 %legendre.1.rows_ref = f32[2,2560,128]{2,1,0:T(8,128)S(1)} custom-call(s32[40]{0:T(128)} %waves_hbm.1, bf16[641,40,128]{2,1,0:T(8,128)(2,1)} %bitcast.7, bf16[40,640,128]{2,1,0:T(8,128)(2,1)} %so_hbm.1, bf16[40,32,641]{2,1,0:T(8,128)(2,1)} %le_hbm.1, bf16[40,32,640]{2,1,0:T(8,128)(2,1)} %lo_hbm.1), custom_call_target="tpu_custom_call" | custom-call | flops 1679032320 | bytes 16396800 | tf_op jit(solution)/shard_map/legendre/pallas_call | solution.py:112
  15.4 0.0 all-to-all-done
  15.4 1.8 %pick.1 = bf16[32,2,2,40,128]{4,3,2,1,0:T(8,128)(2,1)} custom-call(s32[16,128]{1,0:T(8,128)S(1)} %bitcast.5, f32[2,2560,128]{2,1,0:T(8,128)S(1)} %legendre.1.rows_ref), custom_call_target="tpu_custom_call" | custom-call | tf_op jit(solution)/shard_map/pick/pallas_call | solution.py:165
  17.2 6.0 %all-to-all-start.1 = ((bf16[16,2,2,2,40,128]{5,4,3,2,1,0:T(8,128)(2,1)}), bf16[16,2,2,2,40,128]{5,4,3,2,1,0:T(8,128)(2,1)S(1)}, u32[]{:S(2)}, u32[]{:S(2)}) async-start(bf16[16,2,2,2,40,128]{5,4,3,2,1,0:T(8,128)(2,1)} %bitcast.8), calls=%async_computation.1 | async-start | bytes 2621440 | tf_op jit(solution)/shard_map/all_to_all | solution.py:357
  23.2 0.1 reshape.11
  23.3 0.6 %broadcast_in_dim.27.sign_hbm = f32[8,640]{1,0:T(8,128)} broadcast(f32[640]{0:T(1024)S(1)} %fusion.4), dimensions={1} | broadcast | bytes 23040 | tf_op jit(solution)/shard_map/broadcast_in_dim | solution.py:360
  23.9 0.1 broadcast_in_dim.28.waves_ref
  24.1 7.4 %tables.1 = (bf16[2,2,640,256]{3,2,1,0:T(8,128)(2,1)S(1)}, bf16[2,640,256]{2,1,0:T(8,128)(2,1)S(1)}, bf16[3,2,640,256]{3,2,1,0:T(8,128)(2,1)}) custom-call(s32[640,128]{1,0:T(8,128)S(1)} %broadcast_in_dim.28.waves_ref), custom_call_target="tpu_custom_call" | custom-call | flops 6881280 | bytes 3440640 | tf_op jit(solution)/shard_map/tables/pallas_call | solution.py:219
  31.4 22.3 %all-to-all-done.1.arrived_ref = bf16[16,2,2,2,40,128]{5,4,3,2,1,0:T(8,128)(2,1)S(1)} async-done(((bf16[16,2,2,2,40,128]{5,4,3,2,1,0:T(8,128)(2,1)}), bf16[16,2,2,2,40,128]{5,4,3,2,1,0:T(8,128)(2,1)S(1)}, u32[]{:S(2)}, u32[]{:S(2)}) %all-to-all-start.1) | async-done | bytes 1310752 | tf_op jit(solution)/shard_map/all_to_all | solution.py:357
  53.8 4.6 %fourier.1 = bf16[256,2688]{1,0:T(8,128)(2,1)} custom-call(bf16[16,2,2,2,40,128]{5,4,3,2,1,0:T(8,128)(2,1)S(1)} %all-to-all-done.1.arrived_ref, bf16[2,2,640,256]{3,2,1,0:T(8,128)(2,1)S(1)} %get-tuple-element.15.first_ref, bf16[2,640,256]{2,1,0:T(8,128)(2,1)S(1)} %get-tuple-element.16.second_ref, bf16[3,2,640,256]{3,2,1,0:T(8,128)(2,1)} %get-tuple-element.17.rest_hbm, ...), custom_call_target="tpu_custom_call" | custom-call | flops 1761607680 | bytes 3440640 | tf_op jit(solution)/shard_map/fourier/pallas_call | solution.py:314
  (2 shorter events, 0.0 us)
Async XLA Ops:
  1.4 14.0 %all-to-all-start = ((s32[16,1,128]{2,1,0:T(1,128)}), s32[16,1,128]{2,1,0:T(1,128)S(1)}, u32[]{:S(2)}, u32[]{:S(2)}) async-start(s32[16,1,128]{2,1,0:T(1,128)} %broadcast_in_dim.24), calls=%async_computation | async-start | bytes 16384 | tf_op jit(solution)/shard_map/all_to_all | solution.py:353
  17.2 36.6 %all-to-all-start.1 = ((bf16[16,2,2,2,40,128]{5,4,3,2,1,0:T(8,128)(2,1)}), bf16[16,2,2,2,40,128]{5,4,3,2,1,0:T(8,128)(2,1)S(1)}, u32[]{:S(2)}, u32[]{:S(2)}) async-start(bf16[16,2,2,2,40,128]{5,4,3,2,1,0:T(8,128)(2,1)} %bitcast.8), calls=%async_computation.1 | async-start | bytes 2621440 | tf_op jit(solution)/shard_map/all_to_all | solution.py:357
